TPU v7x, 32 devices: a whole 2x2x4 slice. The times are simulated.
32 devices in a mesh: gx: 4 (over x, core), gy: 8 (over z, y).
Axes of the slice: x: 2, y: 2, z: 4, core: 2. Of those that a mesh axis runs over, the one named last changes fastest.
Arguments:
- pixels: bfloat16 [8192, 1536], P(('gx', 'gy')), may hold values from -6 to 6
- frame_index: int32 [8192], P(('gx', 'gy')), may hold values from 0 to 2
- patch_cell: int32 [2, 8192], P(None, ('gx', 'gy')), may hold values from 0 to 55
- tile_id: int32 [8192], P(('gx', 'gy')), may hold values from 0 to 16, as said below
- halo_index: int32 [4096], P(('gx', 'gy')), may hold values from 0 to 255
- w_patch: bfloat16 [1536, 768], replicated, may hold values from -0.15625 to 0.15625
- first_gain: float32 [768], replicated, may hold values from 0.1 to 1.9
- first_bias: float32 [768], replicated, may hold values from -2 to 2
- w_project: bfloat16 [768, 2304], replicated, may hold values from -0.21875 to 0.21875
- project_bias: float32 [1536], replicated, may hold values from -3 to 3
- w_output: bfloat16 [768, 768], replicated, may hold values from -3 to 3
- merge_bias: float32 [768], replicated, may hold values from -3 to 3
- second_gain: float32 [768], replicated, may hold values from 0.1 to 1.9
- second_bias: float32 [768], replicated, may hold values from -2 to 2
- w_up: bfloat16 [768, 3072], replicated, may hold values from -0.21875 to 0.21875
- up_bias: float32 [3072], replicated, may hold values from -3 to 3
- w_down: bfloat16 [3072, 768], replicated, may hold values from -0.109375 to 0.109375
- down_bias: float32 [768], replicated, may hold values from -3 to 3
- w_head: bfloat16 [768, 1536], replicated, may hold values from -0.21875 to 0.21875
- cotangent: bfloat16 [8192, 1536], P(('gx', 'gy')), may hold values from -6 to 6
Outputs:
- predicted: bfloat16 [8192, 1536], P(('gx', 'gy'))
- pixel_grad: bfloat16 [8192, 1536], P(('gx', 'gy'))
- patch_grad: float32 [1536, 768], P('gy')
- first_gain_grad: float32 [768], P('gy')
- first_bias_grad: float32 [768], P('gy')
- project_grad: float32 [768, 2304], P('gy')
- project_bias_grad: float32 [1536], P('gy')
- output_grad: float32 [768, 768], P('gy')
- merge_bias_grad: float32 [768], P('gy')
- second_gain_grad: float32 [768], P('gy')
- second_bias_grad: float32 [768], P('gy')
- up_grad: float32 [768, 3072], P('gy')
- up_bias_grad: float32 [3072], P('gy')
- down_grad: float32 [3072, 768], P('gy')
- down_bias_grad: float32 [768], P('gy')
- head_grad: float32 [768, 1536], P('gy')
Inputs may be any that keep to these rules, and one draw needn't show every extreme that they name: `tile_id`: on each device's 256 rows, the first rows (at least 64, at most 192) belong to tile 0, shared by all devices of a gx column; the rest belong to tiles 1 + 2 b and 2 + 2 b, used by device gy index b alone; its last row is in tile 2 + 2 b.
All inputs are finite; a program needn't handle non-finite values.
Results may differ from a plain program's by a relative error of at most 0.019.
Values may be sent and summed in bfloat16 or wider, within the bound.
No kernel may reach another device: no remote copies, remote signals or barrier semaphores. Data moves between devices by JAX's collectives and lax.ppermute only.
A program may use at most 256 MiB of HBM per device.

v0:
```python
import jax
import jax.numpy as jnp
from jax import lax
from jax.sharding import PartitionSpec as P

HEADS = 12
HEAD_DIM = 64


EPS = 1e-06
NEG = -1e30


def shifted(x, axis, by):
    length = lax.axis_size(axis)
    pairs = [(i, i + by) for i in range(length) if 0 <= i + by < length]
    return lax.ppermute(x, axis, pairs)


def sincos_band(coordinate, band_width):
    half_width = band_width // 2
    omegas = 1.0 / 10000.0 ** (jnp.arange(half_width, dtype=jnp.float32) / half_width)
    angles = coordinate.astype(jnp.float32)[:, None] * omegas[None, :]
    return jnp.concatenate([jnp.sin(angles), jnp.cos(angles)], axis=1)


def positions(frame_index, patch_cell, model_width):
    unit_width = model_width // 16
    return jnp.concatenate(
        [
            sincos_band(frame_index, 4 * unit_width),
            sincos_band(patch_cell[0], 6 * unit_width),
            sincos_band(patch_cell[1], 6 * unit_width),
        ],
        axis=1,
    )


def layer_norm(inputs, scale_gain, shift_bias):
    centered = inputs - jnp.mean(inputs, axis=-1, keepdims=True)
    variance = jnp.mean(centered * centered, axis=-1, keepdims=True)
    return centered * lax.rsqrt(variance + EPS) * scale_gain + shift_bias


def exact_gelu(inputs):
    return jax.nn.gelu(inputs, approximate=False)


def sweep_rows(advance, running, arrays):
    total_rows = arrays[0].shape[0]
    for extent in (2048, 512):
        if total_rows > extent and total_rows % extent == 0:
            pieces = tuple(
                (
                    member.reshape((total_rows // extent, extent) + member.shape[1:])
                    for member in arrays
                )
            )
            running, _ = lax.scan(
                lambda carried, pieces_now: (advance(carried, pieces_now), None), running, pieces
            )
            return running
    return advance(running, arrays)


def shards(
    pixels,
    frame_index,
    patch_cell,
    tile_id,
    halo_index,
    w_patch,
    first_gain,
    first_bias,
    w_project,
    project_bias,
    w_output,
    merge_bias,
    second_gain,
    second_bias,
    w_up,
    up_bias,
    w_down,
    down_bias,
    w_head,
    cotangent,
):
    own_rows = pixels.shape[0]
    rim_count = halo_index.shape[0]
    model_width = w_output.shape[0]
    scaling = HEAD_DIM ** (-0.5)
    embedded = jnp.dot(pixels, w_patch, preferred_element_type=jnp.float32)
    stream = embedded + positions(frame_index, patch_cell, model_width)
    outgoing = jnp.take(stream, halo_index, axis=0).astype(jnp.bfloat16)
    arrived = shifted(outgoing, "gx", 1)
    joined = jnp.concatenate([stream, arrived.astype(jnp.float32)], axis=0)
    normed, first_back = jax.vjp(layer_norm, joined, first_gain, first_bias)
    first_low = normed.astype(jnp.bfloat16)
    queries = (
        jnp.dot(
            first_low[:own_rows], w_project[:, :model_width], preferred_element_type=jnp.float32
        )
        + project_bias[:model_width]
    ).astype(jnp.bfloat16)
    pair_full = jnp.dot(first_low, w_project[:, model_width:], preferred_element_type=jnp.float32)
    keys_low = pair_full[:, :model_width].astype(jnp.bfloat16)
    values_low = (pair_full[:, model_width:] + project_bias[model_width:]).astype(jnp.bfloat16)
    left_live = lax.axis_index("gx") > 0
    rim_ids = jnp.where(
        left_live, jnp.zeros((rim_count,), jnp.int32), -jnp.ones((rim_count,), jnp.int32)
    )
    key_ids = jnp.concatenate([tile_id, rim_ids]).astype(jnp.bfloat16)
    query_ids = tile_id.astype(jnp.float32)
    query_heads = queries.reshape(own_rows, HEADS, HEAD_DIM)

    def masked_scores(key_block, id_block):
        key_heads = key_block.reshape(key_block.shape[0], HEADS, HEAD_DIM)
        scores = (
            jnp.einsum("qhd,khd->hqk", query_heads, key_heads, preferred_element_type=jnp.float32)
            * scaling
        )
        allowed = query_ids[:, None] == id_block.astype(jnp.float32)[None, :]
        return (jnp.where(allowed[None], scores, NEG), allowed)

    def lse_step(running, block_items):
        key_block, id_block = (block_items[0], block_items[-1])
        scores, allowed = masked_scores(key_block, id_block)
        peak_score, total_weight = running
        new_peak = jnp.maximum(peak_score, jnp.max(scores, axis=2))
        weights = jnp.where(allowed[None], jnp.exp(scores - new_peak[:, :, None]), 0.0)
        return (new_peak, total_weight * jnp.exp(peak_score - new_peak) + jnp.sum(weights, axis=2))

    start_stats = (
        jnp.full((HEADS, own_rows), NEG, jnp.float32),
        jnp.zeros((HEADS, own_rows), jnp.float32),
    )
    zero_query = jnp.zeros((own_rows, HEADS, HEAD_DIM), jnp.float32)
    peak_score, total_weight = sweep_rows(
        lse_step,
        start_stats,
        (
            lax.all_gather(keys_low, "gy", axis=0, tiled=True),
            lax.all_gather(key_ids, "gy", axis=0, tiled=True),
        ),
    )
    log_sum = peak_score + jnp.log(total_weight)

    def value_step(running, block_items):
        key_block, value_block, id_block = block_items
        scores, allowed = masked_scores(key_block, id_block)
        weights = jnp.where(allowed[None], jnp.exp(scores - log_sum[:, :, None]), 0.0).astype(
            jnp.bfloat16
        )
        value_heads = value_block.reshape(value_block.shape[0], HEADS, HEAD_DIM)
        return running + jnp.einsum(
            "hqk,khd->qhd", weights, value_heads, preferred_element_type=jnp.float32
        )

    mixed_full = sweep_rows(
        value_step,
        zero_query,
        (
            lax.all_gather(keys_low, "gy", axis=0, tiled=True),
            lax.all_gather(values_low, "gy", axis=0, tiled=True),
            lax.all_gather(key_ids, "gy", axis=0, tiled=True),
        ),
    )
    mixed_low = mixed_full.reshape(own_rows, model_width).astype(jnp.bfloat16)
    after_attn = (
        stream + jnp.dot(mixed_low, w_output, preferred_element_type=jnp.float32) + merge_bias
    )
    normed_two, second_back = jax.vjp(layer_norm, after_attn, second_gain, second_bias)
    second_low = normed_two.astype(jnp.bfloat16)
    pre_act = jnp.dot(second_low, w_up, preferred_element_type=jnp.float32) + up_bias
    activated, gelu_back = jax.vjp(exact_gelu, pre_act)
    act_low = activated.astype(jnp.bfloat16)
    after_mlp = (
        after_attn + jnp.dot(act_low, w_down, preferred_element_type=jnp.float32) + down_bias
    )
    final_low = after_mlp.astype(jnp.bfloat16)
    predicted = jnp.dot(final_low, w_head, preferred_element_type=jnp.float32).astype(jnp.bfloat16)
    head_grad = jnp.dot(final_low.T, cotangent, preferred_element_type=jnp.float32)
    mlp_grad = jnp.dot(cotangent, w_head.T, preferred_element_type=jnp.float32)
    down_bias_grad = jnp.sum(mlp_grad, axis=0)
    mlp_low = mlp_grad.astype(jnp.bfloat16)
    down_grad = jnp.dot(act_low.T, mlp_low, preferred_element_type=jnp.float32)
    act_grad = jnp.dot(mlp_low, w_down.T, preferred_element_type=jnp.float32)
    pre_grad = gelu_back(act_grad)[0].astype(jnp.bfloat16)
    up_grad = jnp.dot(second_low.T, pre_grad, preferred_element_type=jnp.float32)
    up_bias_grad = jnp.sum(pre_grad.astype(jnp.float32), axis=0)
    normed_two_grad = jnp.dot(pre_grad, w_up.T, preferred_element_type=jnp.float32)
    resid_grad, second_gain_grad, second_bias_grad = second_back(normed_two_grad)
    attn_grad = mlp_grad + resid_grad
    merge_bias_grad = jnp.sum(attn_grad, axis=0)
    attn_low = attn_grad.astype(jnp.bfloat16)
    output_grad = jnp.dot(mixed_low.T, attn_low, preferred_element_type=jnp.float32)
    mixed_grad = jnp.dot(attn_low, w_output.T, preferred_element_type=jnp.float32).astype(
        jnp.bfloat16
    )
    grad_heads = mixed_grad.reshape(own_rows, HEADS, HEAD_DIM)
    delta_rows = jnp.sum(grad_heads.astype(jnp.float32) * mixed_full, axis=2).T

    def query_step(running, block_items):
        key_block, value_block, id_block = block_items
        scores, allowed = masked_scores(key_block, id_block)
        weights = jnp.where(allowed[None], jnp.exp(scores - log_sum[:, :, None]), 0.0)
        value_heads = value_block.reshape(value_block.shape[0], HEADS, HEAD_DIM)
        key_heads = key_block.reshape(key_block.shape[0], HEADS, HEAD_DIM)
        weight_grad = jnp.einsum(
            "qhd,khd->hqk", grad_heads, value_heads, preferred_element_type=jnp.float32
        )
        score_grad = (weights * (weight_grad - delta_rows[:, :, None])).astype(jnp.bfloat16)
        return running + jnp.einsum(
            "hqk,khd->qhd", score_grad, key_heads, preferred_element_type=jnp.float32
        )

    query_acc = sweep_rows(
        query_step,
        zero_query,
        (
            lax.all_gather(keys_low, "gy", axis=0, tiled=True),
            lax.all_gather(values_low, "gy", axis=0, tiled=True),
            lax.all_gather(key_ids, "gy", axis=0, tiled=True),
        ),
    )
    query_grad = (query_acc * scaling).reshape(own_rows, model_width).astype(jnp.bfloat16)
    key_count = keys_low.shape[0]
    own_key_heads = keys_low.reshape(key_count, HEADS, HEAD_DIM)
    own_value_heads = values_low.reshape(key_count, HEADS, HEAD_DIM)
    own_key_ids = key_ids.astype(jnp.float32)

    def key_step(running, block_items):
        query_block, grad_block, lse_block, delta_block, id_block = block_items
        block_count = query_block.shape[0]
        block_heads = query_block.reshape(block_count, HEADS, HEAD_DIM)
        block_grads = grad_block.reshape(block_count, HEADS, HEAD_DIM)
        scores = (
            jnp.einsum(
                "qhd,khd->hqk", block_heads, own_key_heads, preferred_element_type=jnp.float32
            )
            * scaling
        )
        allowed = id_block[:, None] == own_key_ids[None, :]
        scores = jnp.where(allowed[None], scores, NEG)
        weights = jnp.where(allowed[None], jnp.exp(scores - lse_block.T[:, :, None]), 0.0)
        key_acc, value_acc = running
        value_acc = value_acc + jnp.einsum(
            "hqk,qhd->khd",
            weights.astype(jnp.bfloat16),
            block_grads,
            preferred_element_type=jnp.float32,
        )
        weight_grad = jnp.einsum(
            "qhd,khd->hqk", block_grads, own_value_heads, preferred_element_type=jnp.float32
        )
        score_grad = (weights * (weight_grad - delta_block.T[:, :, None])).astype(jnp.bfloat16)
        key_acc = key_acc + jnp.einsum(
            "hqk,qhd->khd", score_grad, block_heads, preferred_element_type=jnp.float32
        )
        return (key_acc, value_acc)

    column_lse, column_delta, column_ids = (
        lax.all_gather(log_sum.T, "gy", axis=0, tiled=True),
        lax.all_gather(delta_rows.T, "gy", axis=0, tiled=True),
        lax.all_gather(query_ids, "gy", axis=0, tiled=True),
    )
    zero_keys = jnp.zeros((key_count, HEADS, HEAD_DIM), jnp.float32)
    key_acc, value_acc = sweep_rows(
        key_step,
        (zero_keys, zero_keys),
        (
            lax.all_gather(queries, "gy", axis=0, tiled=True),
            lax.all_gather(mixed_grad, "gy", axis=0, tiled=True),
            column_lse,
            column_delta,
            column_ids,
        ),
    )
    key_grad = (key_acc * scaling).reshape(key_count, model_width).astype(jnp.bfloat16)
    value_grad = value_acc.reshape(key_count, model_width).astype(jnp.bfloat16)
    pair_grad = jnp.concatenate([key_grad, value_grad], axis=1)
    project_bias_grad = jnp.concatenate(
        [
            jnp.sum(query_grad.astype(jnp.float32), axis=0),
            jnp.sum(value_grad.astype(jnp.float32), axis=0),
        ]
    )
    project_grad = jnp.concatenate(
        [
            jnp.dot(first_low[:own_rows].T, query_grad, preferred_element_type=jnp.float32),
            jnp.dot(first_low.T, pair_grad, preferred_element_type=jnp.float32),
        ],
        axis=1,
    )
    query_part = jnp.dot(
        query_grad, w_project[:, :model_width].T, preferred_element_type=jnp.float32
    )
    normed_grad = jnp.dot(
        pair_grad, w_project[:, model_width:].T, preferred_element_type=jnp.float32
    )
    normed_grad = normed_grad + jnp.pad(query_part, ((0, rim_count), (0, 0)))
    joined_grad, first_gain_grad, first_bias_grad = first_back(normed_grad)
    returned = shifted(joined_grad[own_rows:].astype(jnp.bfloat16), "gx", -1).astype(jnp.float32)
    stream_grad = (joined_grad[:own_rows] + attn_grad).at[halo_index].add(returned)
    embed_low = stream_grad.astype(jnp.bfloat16)
    patch_grad = jnp.dot(pixels.T, embed_low, preferred_element_type=jnp.float32)
    pixel_grad = jnp.dot(embed_low, w_patch.T, preferred_element_type=jnp.float32).astype(
        jnp.bfloat16
    )
    shares = (
        lax.psum_scatter(
            patch_grad.astype(jnp.bfloat16), "gy", scatter_dimension=0, tiled=True
        ).astype(jnp.float32),
        lax.psum_scatter(
            first_gain_grad.astype(jnp.bfloat16), "gy", scatter_dimension=0, tiled=True
        ).astype(jnp.float32),
        lax.psum_scatter(
            first_bias_grad.astype(jnp.bfloat16), "gy", scatter_dimension=0, tiled=True
        ).astype(jnp.float32),
        lax.psum_scatter(
            project_grad.astype(jnp.bfloat16), "gy", scatter_dimension=0, tiled=True
        ).astype(jnp.float32),
        lax.psum_scatter(
            project_bias_grad.astype(jnp.bfloat16), "gy", scatter_dimension=0, tiled=True
        ).astype(jnp.float32),
        lax.psum_scatter(
            output_grad.astype(jnp.bfloat16), "gy", scatter_dimension=0, tiled=True
        ).astype(jnp.float32),
        lax.psum_scatter(
            merge_bias_grad.astype(jnp.bfloat16), "gy", scatter_dimension=0, tiled=True
        ).astype(jnp.float32),
        lax.psum_scatter(
            second_gain_grad.astype(jnp.bfloat16), "gy", scatter_dimension=0, tiled=True
        ).astype(jnp.float32),
        lax.psum_scatter(
            second_bias_grad.astype(jnp.bfloat16), "gy", scatter_dimension=0, tiled=True
        ).astype(jnp.float32),
        lax.psum_scatter(
            up_grad.astype(jnp.bfloat16), "gy", scatter_dimension=0, tiled=True
        ).astype(jnp.float32),
        lax.psum_scatter(
            up_bias_grad.astype(jnp.bfloat16), "gy", scatter_dimension=0, tiled=True
        ).astype(jnp.float32),
        lax.psum_scatter(
            down_grad.astype(jnp.bfloat16), "gy", scatter_dimension=0, tiled=True
        ).astype(jnp.float32),
        lax.psum_scatter(
            down_bias_grad.astype(jnp.bfloat16), "gy", scatter_dimension=0, tiled=True
        ).astype(jnp.float32),
        lax.psum_scatter(
            head_grad.astype(jnp.bfloat16), "gy", scatter_dimension=0, tiled=True
        ).astype(jnp.float32),
    )
    summed = (
        lax.psum(shares[0].astype(jnp.bfloat16), "gx").astype(jnp.float32),
        lax.psum(shares[1].astype(jnp.bfloat16), "gx").astype(jnp.float32),
        lax.psum(shares[2].astype(jnp.bfloat16), "gx").astype(jnp.float32),
        lax.psum(shares[3].astype(jnp.bfloat16), "gx").astype(jnp.float32),
        lax.psum(shares[4].astype(jnp.bfloat16), "gx").astype(jnp.float32),
        lax.psum(shares[5].astype(jnp.bfloat16), "gx").astype(jnp.float32),
        lax.psum(shares[6].astype(jnp.bfloat16), "gx").astype(jnp.float32),
        lax.psum(shares[7].astype(jnp.bfloat16), "gx").astype(jnp.float32),
        lax.psum(shares[8].astype(jnp.bfloat16), "gx").astype(jnp.float32),
        lax.psum(shares[9].astype(jnp.bfloat16), "gx").astype(jnp.float32),
        lax.psum(shares[10].astype(jnp.bfloat16), "gx").astype(jnp.float32),
        lax.psum(shares[11].astype(jnp.bfloat16), "gx").astype(jnp.float32),
        lax.psum(shares[12].astype(jnp.bfloat16), "gx").astype(jnp.float32),
        lax.psum(shares[13].astype(jnp.bfloat16), "gx").astype(jnp.float32),
    )
    return (
        predicted,
        pixel_grad,
        summed[0],
        summed[1],
        summed[2],
        summed[3],
        summed[4],
        summed[5],
        summed[6],
        summed[7],
        summed[8],
        summed[9],
        summed[10],
        summed[11],
        summed[12],
        summed[13],
    )


def solution(mesh):
    in_specs = (
        P(("gx", "gy"), None),
        P(("gx", "gy")),
        P(None, ("gx", "gy")),
        P(("gx", "gy")),
        P(("gx", "gy")),
        P(),
        P(),
        P(),
        P(),
        P(),
        P(),
        P(),
        P(),
        P(),
        P(),
        P(),
        P(),
        P(),
        P(),
        P(("gx", "gy"), None),
    )
    out_specs = (
        P(("gx", "gy"), None),
        P(("gx", "gy"), None),
        P("gy", None),
        P("gy"),
        P("gy"),
        P("gy", None),
        P("gy"),
        P("gy", None),
        P("gy"),
        P("gy"),
        P("gy"),
        P("gy", None),
        P("gy"),
        P("gy", None),
        P("gy"),
        P("gy", None),
    )
    return jax.shard_map(shards, mesh=mesh, in_specs=in_specs, out_specs=out_specs, check_vma=False)
```

profile of v0, /device:TPU:0, one launch (start us, length us, event | category | flops | bytes accessed | tf_op | source)
XLA Modules:
  0.0 1222.6 jit_solution(1948480287461323862)
XLA Ops:
  30.6 27.4 %all-gather = bf16[8,1,384]{2,1,0:T(2,128)(2,1)S(1)} all-gather(bf16[1,1,384]{2,1,0:T(2,128)(2,1)S(1)} %reshape.369), channel_id=1, replica_groups=mesh['gx'=4,'gy'=8] {'gy'}, dimensions={0}, use_global_device_ids=true | all-gather | bytes 6912 | tf_op jit(solution)/shard_map/all_gather | solution.py:165
  58.6 19.3 %all-gather.1 = f32[8,1,256]{2,1,0:T(1,128)S(1)} all-gather(f32[1,1,256]{2,1,0:T(1,128)S(1)} %bitcast.253), channel_id=1, replica_groups=mesh['gx'=4,'gy'=8] {'gy'}, dimensions={0}, use_global_device_ids=true | all-gather | bytes 9216 | tf_op jit(solution)/shard_map/all_gather | solution.py:265
  90.0 24.1 %all-gather.7.cloned.1.call-done = bf16[3072,768]{1,0:T(8,128)(2,1)} async-done(((bf16[384,768]{1,0:T(8,128)(2,1)}), bf16[3072,768]{1,0:T(8,128)(2,1)}) %all-gather.7.cloned.1.call-update) | async-done | bytes 4718608 | tf_op jit(solution)/shard_map/all_gather | solution.py:164
  114.1 6.7 copy.88
  120.8 74.1 %all-gather.9.cloned.1.call-done = bf16[3072,768]{1,0:T(8,128)(2,1)} async-done(((bf16[384,768]{1,0:T(8,128)(2,1)}), bf16[3072,768]{1,0:T(8,128)(2,1)}) %all-gather.9.cloned.1.call-update) | async-done | bytes 4718608 | tf_op jit(solution)/shard_map/all_gather | solution.py:163
  194.9 6.7 copy.89
  201.6 77.2 %while.48 = (s32[]{:T(128)}, f32[12,256]{1,0:T(8,128)S(1)}, f32[12,256]{1,0:T(8,128)}, f32[256]{0:T(256)}, bf16[6,512]{1,0:T(8,128)(2,1)}, /*index=5*/bf16[6,512...) while((s32[]{:T(128)}, f32[12,256]{1,0:T(8,128)S(1)}, ...), condition=%wide.region_5.6_spmd.clone, body=%wide.region_2.0_spmd.clone.sunk | while | flops 214056448 | bytes 16517324 | solution.py:59
  204.4 4.4 fusion.186
  209.5 4.3 select_reduce_fusion.2
  217.2 4.4 fusion.186
  222.4 4.4 select_reduce_fusion.2
  230.2 4.4 fusion.186
  235.3 4.3 select_reduce_fusion.2
  243.1 4.4 fusion.186
  248.2 4.3 select_reduce_fusion.2
  255.9 4.4 fusion.186
  261.0 4.3 select_reduce_fusion.2
  268.7 4.4 fusion.186
  273.8 4.3 select_reduce_fusion.2
  280.1 52.8 %while.49 = (s32[]{:T(128)}, f32[256,12,64]{0,2,1:T(8,128)}, bf16[6,512,768]{1,2,0:T(8,128)(2,1)}, f32[256]{0:T(256)}, bf16[6,512]{1,0:T(8,128)(2,1)}, /*index=5...) while((s32[]{:T(128)}, f32[256,12,64]{0,2,1:T(8,128)}, ...), condition=%wide.region_7.8_spmd.clone, body=%wide.region_6.7_spmd.clone.sunk | while | flops 411042304 | bytes 6969499 | solution.py:59
  284.2 4.5 fusion.192
  292.8 4.7 fusion.192
  301.6 4.7 fusion.192
  310.5 4.7 fusion.192
  319.3 4.7 fusion.192
  328.1 4.7 fusion.192
  336.5 11.9 multiply_convert_fusion.6
  359.0 86.1 %while.51 = (s32[]{:T(128)}, f32[256,12,64]{0,2,1:T(8,128)}, bf16[6,512,768]{1,2,0:T(8,128)(2,1)}, f32[256]{0:T(256)S(1)}, bf16[6,512]{1,0:T(8,128)(2,1)}, /*ind...) while((s32[]{:T(128)}, f32[256,12,64]{0,2,1:T(8,128)}, ...), condition=%wide.region_16.17_spmd.clone, body=%wide.region_15.16_spmd.clone.sunk | while | flops 615514624 | bytes 20740240 | solution.py:59
  366.6 6.7 fusion.210
  380.8 6.9 fusion.210
  395.1 6.9 fusion.210
  404.4 3.7 fusion.209
  409.5 6.9 fusion.210
  423.9 6.9 fusion.210
  438.3 6.9 fusion.210
  445.2 30.9 %all_gather.34 = f32[2048,12]{0,1:T(8,128)S(1)} all-gather(f32[256,12]{0,1:T(8,128)} %bitcast.260), channel_id=1, replica_groups=mesh['gx'=4,'gy'=8] {'gy'}, dimensions={0}, use_global_device_ids=true | all-gather | bytes 110592 | tf_op jit(solution)/shard_map/all_gather | solution.py:263
  476.2 30.8 %all_gather.36 = f32[2048,12]{0,1:T(8,128)S(1)} all-gather(f32[256,12]{0,1:T(8,128)} %bitcast.259), channel_id=1, replica_groups=mesh['gx'=4,'gy'=8] {'gy'}, dimensions={0}, use_global_device_ids=true | all-gather | bytes 110592 | tf_op jit(solution)/shard_map/all_gather | solution.py:264
  512.4 122.8 %while.50 = (s32[]{:T(128)}, f32[384,12,64]{0,2,1:T(8,128)}, f32[384,12,64]{0,2,1:T(8,128)}, bf16[4,512,768]{2,1,0:T(8,128)(2,1)}, f32[4,512]{1,0:T(4,128)}, /*i...) while((s32[]{:T(128)}, f32[384,12,64]{0,2,1:T(8,128)}, ...), condition=%wide.region_14.15_spmd.clone, body=%wide.region_13.14_spmd.clone.sunk | while | flops 1237647360 | bytes 47660724 | solution.py:59
  517.3 6.4 fusion.200
  526.7 9.7 fusion.201
  536.5 6.3 fusion.202
  547.5 6.4 fusion.200
  556.9 10.0 fusion.201
  566.9 6.7 fusion.202
  578.3 6.4 fusion.200
  587.7 10.0 fusion.201
  597.7 6.7 fusion.202
  609.1 6.4 fusion.200
  618.5 10.0 fusion.201
  628.5 6.7 fusion.202
  639.1 3.8 fusion.102
  653.6 4.3 copy.103
  660.8 4.3 fusion.76
  668.1 5.1 convolution_convert_fusion.1
  674.4 5.0 convolution_convert_fusion
  688.7 39.1 %reduce-scatter.19.cloned.1.call-done = bf16[192,768]{1,0:T(8,128)(2,1)} async-done(((bf16[1536,768]{1,0:T(8,128)(2,1)}), bf16[192,768]{1,0:T(8,128)(2,1)}) %reduce-scatter.19.cloned.1.call-update) | async-done | bytes 294928
  729.7 65.0 %reduce-scatter.11.cloned.1.call-done = bf16[96,768]{1,0:T(8,128)(2,1)} async-done(((bf16[768,768]{1,0:T(8,128)(2,1)}), bf16[96,768]{1,0:T(8,128)(2,1)}) %reduce-scatter.11.cloned.1.call-update) | async-done | bytes 147472 | tf_op jit(solution)/shard_map/reduce_scatter | solution.py:326
  794.7 71.6 %reduce-scatter.17.cloned.1.call-done = bf16[96,1536]{1,0:T(8,128)(2,1)} async-done(((bf16[768,1536]{1,0:T(8,128)(2,1)}), bf16[96,1536]{1,0:T(8,128)(2,1)}) %reduce-scatter.17.cloned.1.call-update) | async-done | bytes 294928 | tf_op jit(solution)/shard_map/reduce_scatter | solution.py:350
  866.3 98.1 %reduce-scatter.13.cloned.1.call-done = bf16[96,3072]{1,0:T(8,128)(2,1)} async-done(((bf16[768,3072]{1,0:T(8,128)(2,1)}), bf16[96,3072]{1,0:T(8,128)(2,1)}) %reduce-scatter.13.cloned.1.call-update) | async-done | bytes 589840 | tf_op jit(solution)/shard_map/reduce_scatter | solution.py:338
  964.4 98.8 %reduce-scatter.15.cloned.1.call-done = bf16[384,768]{1,0:T(8,128)(2,1)} async-done(((bf16[3072,768]{1,0:T(8,128)(2,1)}), bf16[384,768]{1,0:T(8,128)(2,1)}) %reduce-scatter.15.cloned.1.call-update) | async-done | bytes 589840 | tf_op jit(solution)/shard_map/reduce_scatter | solution.py:344
  1063.2 82.2 %reduce-scatter.9.cloned.1.call-done = bf16[96,2304]{1,0:T(8,128)(2,1)} async-done(((bf16[768,2304]{1,0:T(8,128)(2,1)}), bf16[96,2304]{1,0:T(8,128)(2,1)}) %reduce-scatter.9.cloned.1.call-update) | async-done | bytes 442384 | tf_op jit(solution)/shard_map/reduce_scatter | solution.py:320
  1149.9 36.4 %all-reduce.10 = (bf16[768]{0:T(1024)(128)(2,1)S(1)}, bf16[768]{0:T(1024)(128)(2,1)S(1)}, bf16[1536]{0:T(1024)(128)(2,1)S(1)}, bf16[768]{0:T(1024)(128)(2,1)S(1)...) all-reduce(bf16[768]{0:T(1024)(128)(2,1)} %get-tuple-element.540, ...), channel_id=3, replica_groups=mesh['gx'=4,'gy'=8] {'gy'}, use_global_device_ids=true, to_apply=%region_23.24.clone | all-reduce | flops 9216 | bytes 36864
  1186.9 6.4 all-reduce.11
  1200.9 5.9 all-reduce.15.cloned.1.call-done
  (422 shorter events, 230.1 us)
Async XLA Ops:
  7.2 71.3 %copy-start = (bf16[768,1536]{1,0:T(8,128)(2,1)S(1)}, bf16[768,1536]{1,0:T(8,128)(2,1)}, u32[]{:S(2)}) copy-start(bf16[768,1536]{1,0:T(8,128)(2,1)} %param.46) | copy-start | bytes 7077892
  7.2 106.9 %all-gather.7.cloned.1.call-start = ((), (), s32[]{:S(2)}) async-start(), calls=%async_computation.6 | async-start | bytes 5308416 | tf_op jit(solution)/shard_map/all_gather | solution.py:164
  8.1 5.2 copy-start.59
  15.5 6.5 copy-start.54
  18.3 315.8 %copy-start.1 = (f32[256,768]{1,0:T(8,128)}, f32[256,768]{1,0:T(8,128)S(1)}, u32[]{:S(2)}) copy-start(f32[256,768]{1,0:T(8,128)S(1)} %convolution_add_fusion.3) | copy-start | bytes 2359300
  18.3 5.4 copy-start.45
  18.4 5.4 copy-start.56
  19.2 4.9 copy-start.35
  19.3 3.7 collective-permute-start
  25.2 4.7 copy-start.58
  27.6 167.3 %all-gather.9.cloned.1.call-start = ((), (), s32[]{:S(2)}) async-start(), calls=%async_computation.7 | async-start | bytes 5308416 | tf_op jit(solution)/shard_map/all_gather | solution.py:163
  29.8 482.6 %all-gather.11.cloned.1.call-start = ((), (), s32[]{:S(2)}) async-start(), calls=%async_computation.8 | async-start | bytes 3538944 | tf_op jit(solution)/shard_map/all_gather | solution.py:272
  30.0 55.6 %copy-start.36 = (f32[256]{0:T(256)}, f32[256]{0:T(256)S(1)}, u32[]{:S(2)}) copy-start(f32[256]{0:T(256)S(1)} %get-tuple-element.985) | copy-start | bytes 3076
  89.5 422.9 %all-gather.13.cloned.1.call-start = ((), (), s32[]{:S(2)}) async-start(), calls=%async_computation.9 | async-start | bytes 3538944 | tf_op jit(solution)/shard_map/all_gather | solution.py:273
  203.1 5.7 copy-start.3
  209.5 4.3 copy-start.31
  216.0 5.6 copy-start.3
  222.4 4.4 copy-start.31
  229.0 5.6 copy-start.3
  235.3 4.3 copy-start.31
  241.8 5.6 copy-start.3
  248.2 4.3 copy-start.31
  254.6 5.6 copy-start.3
  261.0 4.3 copy-start.31
  267.5 5.7 copy-start.3
  273.8 4.3 copy-start.31
  280.1 54.0 %copy-start.57 = (f32[768]{0:T(1024)S(1)}, f32[768]{0:T(1024)}, u32[]{:S(2)}) copy-start(f32[768]{0:T(1024)} %param.39) | copy-start | bytes 9220
  334.1 14.2 %slice-start.2 = ((s8[4718592]{0:T(1024)(128)(4,1)}), s8[4194304]{0:T(1024)(128)(4,1)S(1)}, s32[]{:S(2)}) async-start(s8[4718592]{0:T(1024)(128)(4,1)} %bitcast.265), calls=%async_computation.19 | async-start | bytes 8388608
  334.1 17.1 %slice-start = ((s8[4718592]{0:T(1024)(128)(4,1)}), s8[4194304]{0:T(1024)(128)(4,1)S(1)}, s32[]{:S(2)}) async-start(s8[4718592]{0:T(1024)(128)(4,1)} %bitcast.263), calls=%async_computation.17 | async-start | bytes 8388608
  336.2 17.3 %copy-start.5 = (f32[256,768]{1,0:T(8,128)}, f32[256,768]{1,0:T(8,128)S(1)}, u32[]{:S(2)}) copy-start(f32[256,768]{1,0:T(8,128)S(1)} %get-tuple-element.679) | copy-start | bytes 2359300
  336.4 17.1 %copy-start.52 = (f32[256]{0:T(256)}, f32[256]{0:T(256)S(1)}, u32[]{:S(2)}) copy-start(f32[256]{0:T(256)S(1)} %fusion.98) | copy-start | bytes 3076
  336.5 11.9 copy-start.19
  336.5 11.9 slice-start.3
  336.5 14.7 %slice-start.1 = ((s8[4718592]{0:T(1024)(128)(4,1)}), s8[524288]{0:T(1024)(128)(4,1)S(1)}, s32[]{:S(2)}) async-start(s8[4718592]{0:T(1024)(128)(4,1)} %bitcast.263), calls=%async_computation.18 | async-start | bytes 1048576
  353.9 5.1 copy-start.38
  359.0 368.8 %reduce-scatter.19.cloned.1.call-start = ((), (), s32[]{:S(2)}) async-start(), calls=%async_computation.15 | async-start | bytes 2654208
  445.2 67.3 %copy-start.41 = (f32[384]{0:T(512)S(1)}, f32[384]{0:T(512)}, u32[]{:S(2)}) copy-start(f32[384]{0:T(512)} %get-tuple-element.1023) | copy-start | bytes 4612
  526.7 9.8 copy-start.4
  556.9 10.0 copy-start.4
  587.7 10.0 copy-start.4
  618.5 10.0 copy-start.4
  635.2 3.8 copy-start.8
  635.2 3.9 copy-start.26
  635.2 3.9 copy-start.44
  635.2 3.9 copy-start.46
  637.4 5.5 copy-start.29
  639.0 3.9 copy-start.30
  644.5 3.3 collective-permute-start.1
  653.6 4.4 copy-start.16
  657.9 136.8 %reduce-scatter.11.cloned.1.call-start = ((), (), s32[]{:S(2)}) async-start(), calls=%async_computation.11 | async-start | bytes 1327104 | tf_op jit(solution)/shard_map/reduce_scatter | solution.py:326
  660.7 205.6 %reduce-scatter.17.cloned.1.call-start = ((), (), s32[]{:S(2)}) async-start(), calls=%async_computation.14 | async-start | bytes 2654208 | tf_op jit(solution)/shard_map/reduce_scatter | solution.py:350
  660.8 5.1 copy-start.25
  668.0 296.4 %reduce-scatter.13.cloned.1.call-start = ((), (), s32[]{:S(2)}) async-start(), calls=%async_computation.12 | async-start | bytes 5308416 | tf_op jit(solution)/shard_map/reduce_scatter | solution.py:338
  673.3 390.0 %reduce-scatter.15.cloned.1.call-start = ((), (), s32[]{:S(2)}) async-start(), calls=%async_computation.13 | async-start | bytes 5308416 | tf_op jit(solution)/shard_map/reduce_scatter | solution.py:344
  679.5 466.0 %reduce-scatter.9.cloned.1.call-start = ((), (), s32[]{:S(2)}) async-start(), calls=%async_computation.10 | async-start | bytes 3981312 | tf_op jit(solution)/shard_map/reduce_scatter | solution.py:320
  688.6 456.9 %copy-start.61 = (u32[32]{0:T(128)S(1)}, u32[32]{0:T(128)}, u32[]{:S(2)}) copy-start(u32[32]{0:T(128)} %constant.200) | copy-start | bytes 388
  688.6 459.5 %copy-start.34 = (bf16[256,768]{1,0:T(8,128)(2,1)S(1)}, bf16[256,768]{1,0:T(8,128)(2,1)}, u32[]{:S(2)}) copy-start(bf16[256,768]{1,0:T(8,128)(2,1)} %copy-done.33) | copy-start | bytes 1179652
  688.7 518.1 %all-reduce.15.cloned.1.call-start = ((), (), s32[]{:S(2)}) async-start(), calls=%async_computation.16 | async-start | bytes 4915200 | tf_op jit(solution)/shard_map/psum | solution.py:355
  729.7 420.1 %copy-start.51 = (bf16[12,64]{1,0:T(8,128)(2,1)S(1)}, bf16[12,64]{1,0:T(8,128)(2,1)}, u32[]{:S(2)}) copy-start(bf16[12,64]{1,0:T(8,128)(2,1)} %get-tuple-element.645) | copy-start | bytes 4612
  729.7 420.2 %copy-start.55 = (bf16[768]{0:T(1024)(128)(2,1)S(1)}, bf16[768]{0:T(1024)(128)(2,1)}, u32[]{:S(2)}) copy-start(bf16[768]{0:T(1024)(128)(2,1)} %get-tuple-element.641) | copy-start | bytes 4612
  1145.5 52.1 %copy-start.12 = (f32[256,768]{1,0:T(8,128)S(1)}, f32[256,768]{1,0:T(8,128)}, u32[]{:S(2)}) copy-start(f32[256,768]{1,0:T(8,128)} %copy-done.11) | copy-start | bytes 2359300
  1206.8 5.7 copy-start.28
  1206.8 6.9 copy-start.27
  1208.9 5.9 copy-start.39
  (38 other events, 80.9 us)
Sparse Core Ops, SparseCore 0:
  27.7 86.3 all-gather.6
  116.8 78.0 all-gather.8
  197.1 58.5 all-gather.10
  359.1 58.3 all-gather.12
  658.1 69.6 reduce-scatter.18
  731.6 63.0 reduce-scatter.10
  798.2 68.0 reduce-scatter.16
  869.9 94.4 reduce-scatter.12
  968.1 95.1 reduce-scatter.14
  1066.7 78.7 reduce-scatter.8
  1148.8 57.9 all-reduce.14
where the time goes:
time: 1230 us; the launch traced here: 1220 us
  waiting for transfers between devices  562 us (46%)
  matrix products  277 us (23%)
  blocking collectives  151 us (12%)
  local copies, waits for them, and re-layouts  116 us (9%)
  other arithmetic  94.2 us (8%)
  between operations  17.2 us (1%)
    reduce_scatter x1, waiting for transfers between devices, shards(): lax.psum_scatter(down_grad.astype(jnp.bfloat16), 'gy', scatter_dimension=...  98.8 us
    reduce_scatter x1, waiting for transfers between devices, shards(): lax.psum_scatter(up_grad.astype(jnp.bfloat16), 'gy', scatter_dimension=0,...  98.1 us
    reduce_scatter x1, waiting for transfers between devices, shards(): lax.psum_scatter(project_grad.astype(jnp.bfloat16), 'gy', scatter_dimensi...  82.2 us
    all_gather x1, waiting for transfers between devices, shards(): lax.all_gather(keys_low, 'gy', axis=0, tiled=True)  74.1 us
    reduce_scatter x1, waiting for transfers between devices, shards(): lax.psum_scatter(head_grad.astype(jnp.bfloat16), 'gy', scatter_dimension=...  71.6 us
    dynamic_slice x46, local copies, waits for them, and re-layouts, sweep_rows(): lax.scan(lambda carried, pieces_now: (advance(carried, pieces_now), None)...  67.4 us
    reduce_scatter x1, waiting for transfers between devices, shards(): lax.psum_scatter(output_grad.astype(jnp.bfloat16), 'gy', scatter_dimensio...  65 us
    dot_general x12, matrix products, masked_scores(): jnp.einsum('qhd,khd->hqk', query_heads, key_heads, preferred_element_type...  48.3 us
  transfers between devices with their start and end apart: 13, of which 11 were waited for; matrix products, arithmetic and copies ran while one was open for 25% of the time, Pallas kernels for 0%

commit v1 on v0

v1 whole, which is shorter than its diff:
```python
import functools

import jax
import jax.numpy as jnp
from jax import lax
from jax.experimental import pallas as pl
from jax.experimental.pallas import tpu as pltpu
from jax.sharding import PartitionSpec as P

HEADS = 12
HEAD_DIM = 64
PAIR = 2 * HEAD_DIM
LANES = 384
SHARED = 192
EPS = 1e-06
NEG = -1e30
F32 = jnp.float32
BF16 = jnp.bfloat16
VMEM_LIMIT = 56 * 2**20


def dot(a, b):
    return jnp.dot(a, b, preferred_element_type=F32)


def dot_nt(a, b):
    return lax.dot_general(a, b, (((1,), (1,)), ((), ())), preferred_element_type=F32)


def dot_tn(a, b):
    return lax.dot_general(a, b, (((0,), (0,)), ((), ())), preferred_element_type=F32)


def shifted(x, axis, by):
    length = lax.axis_size(axis)
    pairs = [(i, i + by) for i in range(length) if 0 <= i + by < length]
    return lax.ppermute(x, axis, pairs)


def swap(x, axis, bit):
    length = lax.axis_size(axis)
    return lax.ppermute(x, axis, [(i, i ^ bit) for i in range(length)])


def gather_column(unit):
    n = lax.axis_size("gy")
    if n != 8:
        whole = lax.all_gather(unit, "gy", axis=0, tiled=False)
        me = lax.axis_index("gy")
        return [jnp.roll(whole, -me, axis=0)]
    place = lax.axis_index("gy") // 2
    at_end = (place == 0) | (place == 3)

    def along(x, hops):
        pairs = [(2 * a + y, 2 * b + y) for a, b in hops for y in (0, 1)]
        return lax.ppermute(x, "gy", pairs)

    def across(x):
        return swap(x, "gy", 1)

    outer = [(0, 1), (1, 0), (2, 3), (3, 2)]
    middle = [(1, 2), (2, 1)]
    outward = [(1, 0), (2, 3)]
    near = along(unit, outer)
    mid = along(unit, middle)
    y0 = across(unit)
    y1 = across(near)
    far_end = along(mid, outward)
    far_mid = along(near, middle)
    far = jnp.where(at_end, far_end, far_mid)
    y2 = across(far)
    last_end = along(far_mid, outward)
    last = jnp.where(at_end, last_end, mid)
    y3 = across(last)
    return [part[None] for part in (unit, near, far, last, y0, y1, y2, y3)]


def sincos_band(coordinate, band_width):
    half_width = band_width // 2
    omegas = 1.0 / 10000.0 ** (jnp.arange(half_width, dtype=F32) / half_width)
    angles = coordinate.astype(F32)[:, None] * omegas[None, :]
    return jnp.concatenate([jnp.sin(angles), jnp.cos(angles)], axis=1)


def positions(frame_index, patch_cell, model_width):
    unit_width = model_width // 16
    return jnp.concatenate(
        [
            sincos_band(frame_index, 4 * unit_width),
            sincos_band(patch_cell[0], 6 * unit_width),
            sincos_band(patch_cell[1], 6 * unit_width),
        ],
        axis=1,
    )


def layer_norm(inputs, scale_gain, shift_bias):
    centered = inputs - jnp.mean(inputs, axis=-1, keepdims=True)
    variance = jnp.mean(centered * centered, axis=-1, keepdims=True)
    return centered * lax.rsqrt(variance + EPS) * scale_gain + shift_bias


def exact_gelu(inputs):
    return jax.nn.gelu(inputs, approximate=False)


def half_mask(rows):
    return lax.broadcasted_iota(jnp.int32, (rows, PAIR), 1) < HEAD_DIM


def only_half(x, head):
    low_half = half_mask(x.shape[0])
    zero = jnp.zeros_like(x)
    return jnp.where(low_half, x, zero) if head == 0 else jnp.where(low_half, zero, x)


def merge_halves(first, second):
    return jnp.where(half_mask(first.shape[0]), first, second)


def key_bias(block_refs, key_rows, groups):
    rows = []
    for group in groups:
        width = len(group) * key_rows
        lane = lax.broadcasted_iota(jnp.int32, (1, width), 1).astype(F32)
        bias = jnp.full((1, width), NEG, F32)
        for place, (ref, index) in enumerate(group):
            count = ref[index, key_rows : key_rows + 8, 0:128].astype(F32)[0:1, 0:1]
            live = ref[index, key_rows : key_rows + 8, 128:256].astype(F32)[0:1, 0:1]
            local = lane - float(place * key_rows)
            good = (local >= 0.0) & (local < count)
            rim = (local >= float(SHARED)) & (local < float(key_rows)) & (live > 0.5)
            bias = jnp.where(good | rim, 0.0, bias)
        rows.append(bias)
    return rows


def group_blocks(block_refs):
    flat = [(ref, i) for ref in block_refs for i in range(ref.shape[0])]
    return [flat[i : i + 8] for i in range(0, len(flat), 8)]


def attend_kernel(n_blocks, key_rows, *refs):
    block_refs = refs[:n_blocks]
    own_ref, wq_ref, wk_ref, wv_ref, bq_ref, bv_ref, idc_ref, idr_ref = refs[n_blocks : n_blocks + 8]
    kv_ref, kvown_ref, q_ref, mixed_ref, lse_ref, lrow_ref = refs[n_blocks + 8 :]
    own_rows = idc_ref.shape[0]
    wkv = jnp.concatenate([wk_ref[...], wv_ref[...]], axis=1)
    shift = jnp.concatenate([jnp.zeros_like(bv_ref[...]), bv_ref[...]], axis=1)
    groups = group_blocks(block_refs)
    base = 0
    for group in groups:
        for ref, index in group:
            kv_ref[0, base : base + key_rows, :] = (dot(ref[index, 0:key_rows, :], wkv) + shift).astype(BF16)
            base += key_rows
    kvown_ref[0] = (dot(own_ref[...], wkv) + shift).astype(BF16)
    q = (dot(own_ref[0:own_rows, :], wq_ref[...]) + bq_ref[...]).astype(BF16) * BF16(HEAD_DIM**-0.5)
    q_ref[0] = q
    biases = key_bias(block_refs, key_rows, groups)
    idc, idr = idc_ref[...], idr_ref[...]
    allowed = (idc == idr) & (idc != 0)
    shared_row = idc == 0
    outs, lses = [], []
    for head in range(2):
        qs = only_half(q[0:SHARED], head)
        peak = weight = total = None
        base = 0
        for group, bias in zip(groups, biases):
            width = len(group) * key_rows
            keys = kv_ref[0, base : base + width, 0:PAIR]
            values = kv_ref[0, base : base + width, PAIR:]
            base += width
            scores = dot_nt(qs, keys) + bias
            top = jnp.max(scores, axis=1, keepdims=True)
            if peak is None:
                probs = jnp.exp(scores - top)
                weight = jnp.sum(probs, axis=1, keepdims=True)
                total = dot(probs.astype(BF16), values)
                peak = top
            else:
                new = jnp.maximum(peak, top)
                probs = jnp.exp(scores - new)
                fade = jnp.exp(peak - new)
                weight = weight * fade + jnp.sum(probs, axis=1, keepdims=True)
                total = total * fade + dot(probs.astype(BF16), values)
                peak = new
        shared_out = total / weight
        shared_lse = peak + jnp.log(weight)
        ql = only_half(q, head)
        scores = jnp.where(allowed, dot_nt(ql, kvown_ref[0, 0:own_rows, 0:PAIR]), NEG)
        top = jnp.max(scores, axis=1, keepdims=True)
        probs = jnp.exp(scores - top)
        weight = jnp.sum(probs, axis=1, keepdims=True)
        local_out = dot(probs.astype(BF16), kvown_ref[0, 0:own_rows, PAIR:]) / weight
        local_lse = top + jnp.log(weight)
        outs.append(
            jnp.concatenate(
                [jnp.where(shared_row[0:SHARED], shared_out, local_out[0:SHARED]), local_out[SHARED:]], axis=0
            )
        )
        lses.append(
            jnp.concatenate(
                [jnp.where(shared_row[0:SHARED], shared_lse, local_lse[0:SHARED]), local_lse[SHARED:]], axis=0
            )
        )
    mixed_ref[...] = merge_halves(*outs)
    lse = merge_halves(
        jnp.broadcast_to(lses[0], (own_rows, PAIR)), jnp.broadcast_to(lses[1], (own_rows, PAIR))
    )
    lse_ref[...] = lse
    turned = lse.T
    lrow_ref[0, 0:8, :] = turned[0:8]
    lrow_ref[0, 8:16, :] = turned[HEAD_DIM : HEAD_DIM + 8]


def full(shape):
    zeros = (0,) * len(shape)
    return pl.BlockSpec(tuple(shape), lambda h: zeros, pipeline_mode=pl.Buffered(1))


def params():
    return pltpu.CompilerParams(vmem_limit_bytes=VMEM_LIMIT)


def attend(blocks, first_low, w_project, project_bias, idc, idr, key_rows):
    own_rows = idc.shape[0]
    joined_rows = first_low.shape[0]
    pairs = HEADS // 2
    count = sum(b.shape[0] for b in blocks)
    width = first_low.shape[1]
    keys = count * key_rows
    bias = project_bias.reshape(1, -1)
    col = lambda off: pl.BlockSpec((width, PAIR), lambda h: (0, off + h))
    vec = lambda off: pl.BlockSpec((1, PAIR), lambda h: (0, off + h))
    out_shape = (
        jax.ShapeDtypeStruct((pairs, keys, 2 * PAIR), BF16),
        jax.ShapeDtypeStruct((pairs, joined_rows, 2 * PAIR), BF16),
        jax.ShapeDtypeStruct((pairs, own_rows, PAIR), BF16),
        jax.ShapeDtypeStruct((own_rows, width), F32),
        jax.ShapeDtypeStruct((own_rows, width), F32),
        jax.ShapeDtypeStruct((pairs, 16, own_rows), F32),
    )
    out_specs = (
        pl.BlockSpec((1, keys, 2 * PAIR), lambda h: (h, 0, 0)),
        pl.BlockSpec((1, joined_rows, 2 * PAIR), lambda h: (h, 0, 0)),
        pl.BlockSpec((1, own_rows, PAIR), lambda h: (h, 0, 0)),
        pl.BlockSpec((own_rows, PAIR), lambda h: (0, h)),
        pl.BlockSpec((own_rows, PAIR), lambda h: (0, h)),
        pl.BlockSpec((1, 16, own_rows), lambda h: (h, 0, 0)),
    )
    return pl.pallas_call(
        functools.partial(attend_kernel, len(blocks), key_rows),
        grid=(pairs,),
        in_specs=[full(b.shape) for b in blocks]
        + [full(first_low.shape), col(0), col(pairs), col(2 * pairs), vec(0), vec(pairs), full(idc.shape), full(idr.shape)],
        out_specs=out_specs,
        out_shape=out_shape,
        compiler_params=params(),
        cost_estimate=pl.CostEstimate(
            flops=2 * keys * width * (2 * width + 2 * SHARED), bytes_accessed=20 * 2**20, transcendentals=HEADS * keys * SHARED
        ),
        name="attend",
    )(*blocks, first_low, w_project, w_project, w_project, bias, bias, idc, idr)


def query_kernel(n_blocks, key_rows, *refs):
    block_refs = refs[:n_blocks]
    kv_ref, kvown_ref, q_ref, grad_ref, mixed_ref, lse_ref, wq_ref, bq_ref, idc_ref, idr_ref = refs[
        n_blocks : n_blocks + 10
    ]
    dq_ref, qall_ref = refs[n_blocks + 10 :]
    own_rows = idc_ref.shape[0]
    groups = group_blocks(block_refs)
    base = 0
    for group in groups:
        for ref, index in group:
            qall_ref[0, base : base + SHARED, :] = (dot(ref[index, 0:SHARED, :], wq_ref[...]) + bq_ref[...]).astype(
                BF16
            ) * BF16(HEAD_DIM**-0.5)
            base += SHARED
    biases = key_bias(block_refs, key_rows, groups)
    idc, idr = idc_ref[...], idr_ref[...]
    allowed = (idc == idr) & (idc != 0)
    shared_row = idc == 0
    q = q_ref[0]
    grad = grad_ref[...]
    product = grad.astype(F32) * mixed_ref[...]
    outs = []
    for head in range(2):
        delta = jnp.sum(only_half(product, head), axis=1, keepdims=True)
        lse = lse_ref[:, head * HEAD_DIM : head * HEAD_DIM + 1]
        qm = only_half(q, head)
        gm = only_half(grad, head)
        total = None
        base = 0
        for group, bias in zip(groups, biases):
            width = len(group) * key_rows
            keys = kv_ref[0, base : base + width, 0:PAIR]
            values = kv_ref[0, base : base + width, PAIR:]
            base += width
            probs = jnp.exp(dot_nt(qm[0:SHARED], keys) + bias - lse[0:SHARED])
            dp = dot_nt(gm[0:SHARED], values)
            ds = (probs * (dp - delta[0:SHARED])).astype(BF16)
            part = dot(ds, keys)
            total = part if total is None else total + part
        keys, values = kvown_ref[0, 0:own_rows, 0:PAIR], kvown_ref[0, 0:own_rows, PAIR:]
        probs = jnp.exp(jnp.where(allowed, dot_nt(qm, keys) - lse, NEG))
        ds = (probs * (dot_nt(gm, values) - delta)).astype(BF16)
        local = dot(ds, keys)
        outs.append(
            jnp.concatenate([jnp.where(shared_row[0:SHARED], total, local[0:SHARED]), local[SHARED:]], axis=0)
        )
    dq_ref[...] = (merge_halves(*outs) * HEAD_DIM**-0.5).astype(BF16)


def query_back(blocks, kv, kvown, q, mixed_grad, mixed, lse, w_project, project_bias, idc, idr, key_rows):
    own_rows = idc.shape[0]
    pairs = HEADS // 2
    count = sum(b.shape[0] for b in blocks)
    width = mixed_grad.shape[1]
    keys = count * key_rows
    bias = project_bias.reshape(1, -1)
    lane = lambda: pl.BlockSpec((own_rows, PAIR), lambda h: (0, h))
    lead = lambda x: pl.BlockSpec((1,) + x.shape[1:], lambda h: (h, 0, 0))
    return pl.pallas_call(
        functools.partial(query_kernel, len(blocks), key_rows),
        grid=(pairs,),
        in_specs=[full(b.shape) for b in blocks]
        + [
            lead(kv),
            lead(kvown),
            lead(q),
            lane(),
            lane(),
            lane(),
            pl.BlockSpec((width, PAIR), lambda h: (0, h)),
            pl.BlockSpec((1, PAIR), lambda h: (0, h)),
            full(idc.shape),
            full(idr.shape),
        ],
        out_specs=(
            pl.BlockSpec((own_rows, PAIR), lambda h: (0, h)),
            pl.BlockSpec((1, count * SHARED, PAIR), lambda h: (h, 0, 0)),
        ),
        out_shape=(
            jax.ShapeDtypeStruct((own_rows, width), BF16),
            jax.ShapeDtypeStruct((pairs, count * SHARED, PAIR), BF16),
        ),
        compiler_params=params(),
        cost_estimate=pl.CostEstimate(
            flops=2 * keys * width * 6 * SHARED, bytes_accessed=20 * 2**20, transcendentals=HEADS * keys * SHARED
        ),
        name="query_back",
    )(*blocks, kv, kvown, q, mixed_grad, mixed, lse, w_project, bias, idc, idr)


def key_kernel(n_blocks, *refs):
    grad_refs = refs[:n_blocks]
    kvown_ref, qall_ref, stat_ref, q_ref, grad_ref, lrow_ref, drow_ref, idc_ref, idr_ref, live_ref = refs[
        n_blocks : n_blocks + 10
    ]
    dk_ref, dv_ref, grads_ref = refs[n_blocks + 10 :]
    own_rows = idc_ref.shape[0]
    rim = kvown_ref.shape[1] - own_rows
    base = 0
    for ref in grad_refs:
        for i in range(ref.shape[0]):
            grads_ref[base : base + SHARED, :] = ref[i]
            base += SHARED
    idc, idr = idc_ref[...], idr_ref[...]
    allowed = (idc == idr) & (idc != 0)
    shared_row = idc == 0
    live = live_ref[0:1, 0:1] > 0.5
    kv = kvown_ref[0]
    k_all, v_all = kv[:, 0:PAIR], kv[:, PAIR:]
    k_sh = jnp.concatenate([k_all[0:SHARED], k_all[own_rows:]], axis=0)
    v_sh = jnp.concatenate([v_all[0:SHARED], v_all[own_rows:]], axis=0)
    q, grad = q_ref[0], grad_ref[...]
    dks, dvs = [], []
    chunk = min(base, 1536)
    for head in range(2):
        km, vm = only_half(k_sh, head), only_half(v_sh, head)
        dk = dv = None
        for start in range(0, base, chunk):
            q_all = qall_ref[0, start : start + chunk, :]
            g_all = grads_ref[start : start + chunk, :]
            lse = stat_ref[0, head : head + 1, start : start + chunk]
            delta = stat_ref[0, 2 + head : 3 + head, start : start + chunk]
            probs = jnp.exp(dot_nt(km, q_all) - lse)
            part_v = dot(probs.astype(BF16), g_all)
            ds = (probs * (dot_nt(vm, g_all) - delta)).astype(BF16)
            part_k = dot(ds, q_all)
            dk = part_k if dk is None else dk + part_k
            dv = part_v if dv is None else dv + part_v
        lse = lrow_ref[0, 8 * head : 8 * head + 1, :]
        delta = drow_ref[0, head : head + 1, :]
        probs = jnp.exp(jnp.where(allowed, dot_nt(only_half(k_all[0:own_rows], head), q) - lse, NEG))
        local_v = dot(probs.astype(BF16), grad)
        ds = (probs * (dot_nt(only_half(v_all[0:own_rows], head), grad) - delta)).astype(BF16)
        local_k = dot(ds, q)

        def rows(shared, local):
            return jnp.concatenate(
                [
                    jnp.where(shared_row[0:SHARED], shared[0:SHARED], local[0:SHARED]),
                    local[SHARED:],
                    jnp.where(live, shared[SHARED : SHARED + rim], 0.0),
                ],
                axis=0,
            )

        dks.append(rows(dk, local_k))
        dvs.append(rows(dv, local_v))
    dk_ref[...] = merge_halves(*dks).astype(BF16)
    dv_ref[...] = merge_halves(*dvs).astype(BF16)


def key_back(grads, kvown, qall, stats, q, mixed_grad, lrow, drow, idc, idr, live):
    own_rows = idc.shape[0]
    joined_rows = kvown.shape[1]
    pairs = HEADS // 2
    width = mixed_grad.shape[1]
    lead = lambda x: pl.BlockSpec((1,) + x.shape[1:], lambda h: (h, 0, 0))
    out = lambda: pl.BlockSpec((joined_rows, PAIR), lambda h: (0, h))
    return pl.pallas_call(
        functools.partial(key_kernel, len(grads)),
        grid=(pairs,),
        in_specs=[pl.BlockSpec((g.shape[0], SHARED, PAIR), lambda h: (0, 0, h)) for g in grads]
        + [
            lead(kvown),
            lead(qall),
            lead(stats),
            lead(q),
            pl.BlockSpec((own_rows, PAIR), lambda h: (0, h)),
            lead(lrow),
            lead(drow),
            full(idc.shape),
            full(idr.shape),
            full(live.shape),
        ],
        out_specs=(out(), out()),
        out_shape=(jax.ShapeDtypeStruct((joined_rows, width), BF16),) * 2,
        scratch_shapes=[pltpu.VMEM((qall.shape[1], PAIR), BF16)],
        compiler_params=params(),
        cost_estimate=pl.CostEstimate(
            flops=2 * qall.shape[1] * width * 4 * (SHARED + 128),
            bytes_accessed=10 * 2**20,
            transcendentals=HEADS * qall.shape[1] * (SHARED + 128),
        ),
        name="key_back",
    )(*grads, kvown, qall, stats, q, mixed_grad, lrow, drow, idc, idr, live)


def bit_of(axis, bit):
    return (lax.axis_index(axis) // bit) % 2


def halve(x, axis, bit, dim):
    mine = bit_of(axis, bit)
    send = lax.dynamic_index_in_dim(x, 1 - mine, dim, keepdims=False)
    keep = lax.dynamic_index_in_dim(x, mine, dim, keepdims=False)
    return keep + swap(send, axis, bit)


def core_stage(left, right):
    half = right.shape[1] // 2
    core = bit_of("gx", 1)
    other = lax.dynamic_slice_in_dim(right, (1 - core) * half, half, axis=1)
    mine = lax.dynamic_slice_in_dim(right, core * half, half, axis=1)
    arrived = swap(dot_tn(left, other).astype(BF16), "gx", 1)
    return (dot_tn(left, mine) + arrived.astype(F32)).astype(BF16)


def to_rows(x, n):
    r, blocks = x.shape[0] // n, x.shape[1] // LANES
    return x.reshape(n, r, blocks, LANES).transpose(0, 2, 1, 3).reshape(n, r * blocks, LANES)


def from_rows(x, r):
    blocks = x.shape[0] // r
    return x.reshape(blocks, r, LANES).transpose(1, 0, 2).reshape(r, blocks * LANES)


def scatter_sum(x, x_first):
    n, rows, lanes = x.shape
    x = x.reshape(2, 2, 2, 2, rows // 2, lanes)
    if x_first:
        x = halve(x, "gx", 2, 3)
        x = halve(x, "gy", 1, 2)
    else:
        x = halve(x, "gy", 1, 2)
        x = halve(x, "gx", 2, 2)
    x = halve(x, "gy", 2, 1)
    return halve(x, "gy", 4, 0)


def both_halves(x, axis, bit, dim):
    other = swap(x, axis, bit)
    mine = bit_of(axis, bit)
    first = jnp.where(mine == 0, x, other)
    second = jnp.where(mine == 0, other, x)
    return jnp.concatenate([first, second], axis=dim)


def shards(
    pixels,
    frame_index,
    patch_cell,
    tile_id,
    halo_index,
    w_patch,
    first_gain,
    first_bias,
    w_project,
    project_bias,
    w_output,
    merge_bias,
    second_gain,
    second_bias,
    w_up,
    up_bias,
    w_down,
    down_bias,
    w_head,
    cotangent,
):
    n_gx, n_gy = lax.axis_size("gx"), lax.axis_size("gy")
    own_rows = pixels.shape[0]
    rim_count = halo_index.shape[0]
    width = w_output.shape[0]
    key_rows = SHARED + rim_count
    idc, idr = tile_id.reshape(own_rows, 1), tile_id.reshape(1, own_rows)
    live = jnp.where(lax.axis_index("gx") > 0, 1.0, 0.0).astype(F32)
    count = jnp.sum((tile_id == 0).astype(F32))

    stream = dot(pixels, w_patch) + positions(frame_index, patch_cell, width)
    outgoing = jnp.take(stream, halo_index, axis=0).astype(BF16)
    arrived = shifted(outgoing, "gx", 1).astype(F32)
    normed_own, own_back = jax.vjp(layer_norm, stream, first_gain, first_bias)
    normed_rim, rim_back = jax.vjp(layer_norm, arrived, first_gain, first_bias)
    own_low, rim_low = normed_own.astype(BF16), normed_rim.astype(BF16)
    first_low = jnp.concatenate([own_low, rim_low], axis=0)
    lane = jnp.arange(width)[None, :]
    marks = jnp.where(lane < 128, count, live).astype(BF16)
    unit = jnp.concatenate([own_low[:SHARED], rim_low, jnp.broadcast_to(marks, (16, width))], axis=0)
    blocks = gather_column(unit)
    kv, kvown, q, mixed, lse, lrow = attend(blocks, first_low, w_project, project_bias, idc, idr, key_rows)

    mixed_low = mixed.astype(BF16)
    after_attn = stream + dot(mixed_low, w_output) + merge_bias
    normed_two, second_back = jax.vjp(layer_norm, after_attn, second_gain, second_bias)
    second_low = normed_two.astype(BF16)
    pre_act = dot(second_low, w_up) + up_bias
    activated, gelu_back = jax.vjp(exact_gelu, pre_act)
    act_low = activated.astype(BF16)
    after_mlp = after_attn + dot(act_low, w_down) + down_bias
    final_low = after_mlp.astype(BF16)
    predicted = dot(final_low, w_head).astype(BF16)
    mlp_grad = dot_nt(cotangent, w_head)
    down_bias_grad = jnp.sum(mlp_grad, axis=0)
    mlp_low = mlp_grad.astype(BF16)
    act_grad = dot_nt(mlp_low, w_down)
    pre_grad = gelu_back(act_grad)[0].astype(BF16)
    up_bias_grad = jnp.sum(pre_grad.astype(F32), axis=0)
    normed_two_grad = dot_nt(pre_grad, w_up)
    resid_grad, second_gain_grad, second_bias_grad = second_back(normed_two_grad)
    attn_grad = mlp_grad + resid_grad
    merge_bias_grad = jnp.sum(attn_grad, axis=0)
    attn_low = attn_grad.astype(BF16)
    mixed_grad = dot_nt(attn_low, w_output).astype(BF16)
    delta = jnp.sum((mixed_grad.astype(F32) * mixed).reshape(own_rows, HEADS, HEAD_DIM), axis=2).T

    in_shared = tile_id[:SHARED] == 0
    lse_row = lrow[:, ::8, :].reshape(HEADS, own_rows)
    lse_sent = jnp.where(in_shared[None], lse_row[:, :SHARED], 1e30)
    delta_sent = jnp.where(in_shared[None], delta[:, :SHARED], 0.0)

    def two(x):
        high = x.astype(BF16)
        return high, (x - high.astype(F32)).astype(BF16)

    stats = jnp.concatenate(two(lse_sent) + two(delta_sent), axis=1)
    stats = jnp.pad(stats, ((0, 16 - HEADS), (0, width - 4 * SHARED)))
    grad_sent = jnp.where(in_shared[:, None], mixed_grad[:SHARED], jnp.zeros((), BF16))
    grads = gather_column(jnp.concatenate([grad_sent, stats], axis=0))
    dq, qall = query_back(blocks, kv, kvown, q, mixed_grad, mixed, lse, w_project, project_bias, idc, idr, key_rows)
    packed = jnp.concatenate([g[:, SHARED : SHARED + HEADS, : 4 * SHARED] for g in grads], axis=0).astype(F32)
    packed = packed.reshape(n_gy, HEADS, 4, SHARED)
    packed = jnp.stack([packed[:, :, 0] + packed[:, :, 1], packed[:, :, 2] + packed[:, :, 3]], axis=0)
    packed = packed.reshape(2, n_gy, HEADS // 2, 2, SHARED).transpose(2, 0, 3, 1, 4)
    packed = packed.reshape(HEADS // 2, 4, n_gy * SHARED)
    live_tile = jnp.broadcast_to(live, (8, 128))
    dk, dv = key_back(
        grads, kvown, qall, packed, q, mixed_grad, lrow, delta.reshape(HEADS // 2, 2, own_rows), idc, idr, live_tile
    )

    dq_full = jnp.pad(dq, ((0, rim_count), (0, 0)))
    joint_grad = jnp.concatenate([dq_full, dk, dv], axis=1)
    project_bias_grad = jnp.concatenate([jnp.sum(dq.astype(F32), axis=0), jnp.sum(dv.astype(F32), axis=0)])
    normed_grad = dot_nt(joint_grad, w_project)
    rim_grad, rim_gain, rim_bias = rim_back(normed_grad[own_rows:])
    returned = shifted(rim_grad.astype(BF16), "gx", -1)
    own_grad, own_gain, own_bias = own_back(normed_grad[:own_rows])
    first_gain_grad, first_bias_grad = own_gain + rim_gain, own_bias + rim_bias
    spread = (jnp.arange(own_rows)[:, None] == halo_index[None, :]).astype(BF16)
    stream_grad = own_grad + attn_grad + dot(spread, returned)
    embed_low = stream_grad.astype(BF16)
    pixel_grad = dot_nt(embed_low, w_patch).astype(BF16)

    vectors = [
        first_gain_grad,
        first_bias_grad,
        project_bias_grad,
        merge_bias_grad,
        second_gain_grad,
        second_bias_grad,
        up_bias_grad,
        down_bias_grad,
    ]
    sizes = [v.shape[0] // n_gy for v in vectors]
    joined = [
        (final_low, cotangent),
        (act_low, mlp_low),
        (second_low, pre_grad),
        (mixed_low, attn_low),
        (first_low, joint_grad),
        (pixels, embed_low),
    ]
    if n_gx == 4 and n_gy == 8:
        core = bit_of("gx", 1)
        piles = [to_rows(core_stage(a, b), n_gy) for a, b in joined]
        flat = jnp.concatenate([v.reshape(n_gy, -1) for v in vectors], axis=1).astype(BF16)
        half = sum(sizes) // 2
        flat = flat.reshape(n_gy, 2, half)
        small = halve(flat, "gx", 1, 1)
        small = jnp.pad(small, ((0, 0), (0, 32 * LANES - half))).reshape(n_gy, 32, LANES)
        head_pile, down_pile, up_pile, output_pile, project_pile, patch_pile = piles
        parts = [
            scatter_sum(jnp.concatenate([head_pile, down_pile], axis=1), True),
            scatter_sum(jnp.concatenate([up_pile, output_pile], axis=1), False),
            scatter_sum(project_pile, True),
            scatter_sum(jnp.concatenate([patch_pile, small], axis=1), False),
        ]
        early = [both_halves(p, "gx", 2, 0) for p in parts]
        done = [swap(e, "gx", 1) for e in early]
        lows = [jnp.where(core == 0, e, d).astype(F32) for e, d in zip(early, done)]
        highs = [jnp.where(core == 0, d, e).astype(F32) for e, d in zip(early, done)]

        def cut(group, start, stop, r):
            return jnp.concatenate(
                [from_rows(lows[group][start:stop], r), from_rows(highs[group][start:stop], r)], axis=1
            )

        counts = [p.shape[1] for p in piles]
        rows = [a.shape[1] // n_gy for a, _ in joined]
        head_grad = cut(0, 0, counts[0], rows[0])
        down_grad = cut(0, counts[0], counts[0] + counts[1], rows[1])
        up_grad = cut(1, 0, counts[2], rows[2])
        output_grad = cut(1, counts[2], counts[2] + counts[3], rows[3])
        project_grad = cut(2, 0, counts[4], rows[4])
        patch_grad = cut(3, 0, counts[5], rows[5])
        tail = [part[3][counts[5] :].reshape(-1)[:half] for part in (lows, highs)]
        tail = jnp.concatenate(tail)
    else:

        def total(x):
            part = lax.psum_scatter(x.astype(BF16), "gy", scatter_dimension=0, tiled=True)
            return lax.psum(part, "gx").astype(F32)

        head_grad, down_grad, up_grad, output_grad, project_grad, patch_grad = [
            total(dot_tn(a, b)) for a, b in joined
        ]
        flat = jnp.concatenate([v.reshape(n_gy, -1) for v in vectors], axis=1)
        tail = total(flat).reshape(-1)
    starts = [sum(sizes[:i]) for i in range(len(sizes))]
    small_outs = [tail[s : s + z] for s, z in zip(starts, sizes)]
    return (
        predicted,
        pixel_grad,
        patch_grad,
        small_outs[0],
        small_outs[1],
        project_grad,
        small_outs[2],
        output_grad,
        small_outs[3],
        small_outs[4],
        small_outs[5],
        up_grad,
        small_outs[6],
        down_grad,
        small_outs[7],
        head_grad,
    )


def solution(mesh):
    tokens = P(("gx", "gy"))
    rows = P(("gx", "gy"), None)
    in_specs = (rows, tokens, P(None, ("gx", "gy")), tokens, tokens) + (P(),) * 14 + (rows,)
    matrix, vector = P("gy", None), P("gy")
    out_specs = (
        rows,
        rows,
        matrix,
        vector,
        vector,
        matrix,
        vector,
        matrix,
        vector,
        vector,
        vector,
        matrix,
        vector,
        matrix,
        vector,
        matrix,
    )
    return jax.shard_map(shards, mesh=mesh, in_specs=in_specs, out_specs=out_specs, check_vma=False)
```

time: 1230 us -> 513 us (0.42)
  waiting for transfers between devices: 562 us -> 159 us
  matrix products: 277 us -> 65.7 us
  blocking collectives: 151 us -> 0 us
  Pallas kernels: 0 us -> 75.1 us
  starting transfers between devices: 4.84 us -> 69.8 us
  other arithmetic: 94.2 us -> 51.2 us
  local copies, waits for them, and re-layouts: 116 us -> 81.8 us
  between operations: 17.2 us -> 2.84 us
    reduce_scatter x5 -> x0, waiting for transfers between devices: 416 us -> none  [the longest x1 98.8 us: shards(): lax.psum_scatter(down_grad.astype(jnp.bfloat16), 'gy', scatter_dimension=...]
    dot_general x57 -> x24, matrix products: 277 us -> 65.7 us  [the longest x12 29 us: dot_tn(): lax.dot_general(a, b, (((0,), (0,)), ((), ())), preferred_element_type=F32)]
    ppermute x0 -> x49, waiting for transfers between devices: none -> 159 us  [the longest x39 116 us: swap(): return lax.ppermute(x, axis, [(i, i ^ bit) for i in range(length)])]
    all_gather x4 -> x0, blocking collectives: 108 us -> none  [the longest x1 30.9 us: shards(): lax.all_gather(log_sum.T, 'gy', axis=0, tiled=True)]
    all_gather x4 -> x0, waiting for transfers between devices: 98.2 us -> none  [the longest x1 74.1 us: shards(): lax.all_gather(keys_low, 'gy', axis=0, tiled=True)]
    pallas_call x0 -> x3, Pallas kernels: none -> 75.1 us  [the longest x1 31.9 us: attend(): pl.pallas_call(functools.partial(attend_kernel, len(blocks), key_rows), g...]
    dynamic_slice x46 -> x3, local copies, waits for them, and re-layouts: 67.4 us -> 1.31 us  [the longest x1 1 us: halve(): send = lax.dynamic_index_in_dim(x, 1 - mine, dim, keepdims=False)]
    ppermute x0 -> x49, starting transfers between devices: none -> 66 us  [the longest x39 35.9 us: swap(): return lax.ppermute(x, axis, [(i, i ^ bit) for i in range(length)])]
  transfers between devices with their start and end apart: 13 -> 51, of which waited for: 11 -> 20; matrix products, arithmetic and copies ran while one was open for 25% -> 29% of each run, Pallas kernels for 0% -> 9%
where the time goes in v1:
time: 513 us; the launch traced here: 505 us
  waiting for transfers between devices  159 us (31%)
  local copies, waits for them, and re-layouts  81.8 us (16%)
  Pallas kernels  75.1 us (15%)
  starting transfers between devices  69.8 us (14%)
  matrix products  65.7 us (13%)
  other arithmetic  51.2 us (10%)
    ppermute x39, waiting for transfers between devices, swap(): return lax.ppermute(x, axis, [(i, i ^ bit) for i in range(length)])  116 us
    ppermute x10, waiting for transfers between devices, along(): return lax.ppermute(x, 'gy', pairs)  42.7 us
    ppermute x39, starting transfers between devices, swap(): return lax.ppermute(x, axis, [(i, i ^ bit) for i in range(length)])  35.9 us
    pallas_call x1, Pallas kernels, attend(): pl.pallas_call(functools.partial(attend_kernel, len(blocks), key_rows), g...  31.9 us
    ppermute x10, starting transfers between devices, along(): return lax.ppermute(x, 'gy', pairs)  30.1 us
    dot_general x12, matrix products, dot_tn(): lax.dot_general(a, b, (((0,), (0,)), ((), ())), preferred_element_type=F32)  29 us
    pallas_call x1, Pallas kernels, query_back(): pl.pallas_call(functools.partial(query_kernel, len(blocks), key_rows), gr...  24.9 us
    dot_general x6, matrix products, dot_nt(): lax.dot_general(a, b, (((1,), (1,)), ((), ())), preferred_element_type=F32)  21.3 us
  transfers between devices with their start and end apart: 51, of which 20 were waited for; matrix products, arithmetic and copies ran while one was open for 29% of the time, Pallas kernels for 9%

profile of v1, /device:TPU:0, one launch (start us, length us, event | category | flops | bytes accessed | tf_op | source)
XLA Modules:
  0.0 505.3 jit_solution(10594710249921014030)
XLA Ops:
  5.3 1.9 multiply_cosine_fusion
  7.2 2.2 concatenate.94
  9.4 3.0 fusion.95
  13.9 2.4 collective-permute-start
  22.6 1.9 pad_maximum_fusion.8
  24.5 2.4 collective-permute-start.1
  28.3 9.9 %collective-permute-done.1 = bf16[336,768]{1,0:T(8,128)(2,1)S(1)} collective-permute-done((bf16[336,768]{1,0:T(8,128)(2,1)S(1)}, bf16[336,768]{1,0:T(8,128)(2,1)S(1)}, u32[]{:S(2)}, u32[]{:S(2)}) %collective-permute-start.1) | collective-permute-done | bytes 516128 | tf_op jit(solution)/shard_map/ppermute | solution.py:56
  42.5 2.5 collective-permute-start.6
  45.1 13.3 %collective-permute-done.3 = bf16[336,768]{1,0:T(8,128)(2,1)} collective-permute-done((bf16[336,768]{1,0:T(8,128)(2,1)}, bf16[336,768]{1,0:T(8,128)(2,1)}, u32[]{:S(2)}, u32[]{:S(2)}) %collective-permute-start.3) | collective-permute-done | bytes 516128 | tf_op jit(solution)/shard_map/ppermute | solution.py:56
  58.4 1.9 broadcast_select_fusion.1
  61.8 9.1 %collective-permute-done.5 = bf16[336,768]{1,0:T(8,128)(2,1)} collective-permute-done((bf16[336,768]{1,0:T(8,128)(2,1)}, bf16[336,768]{1,0:T(8,128)(2,1)}, u32[]{:S(2)}, u32[]{:S(2)}) %collective-permute-start.5) | collective-permute-done | bytes 516128 | tf_op jit(solution)/shard_map/ppermute | solution.py:56
  70.9 1.9 broadcast_select_fusion
  76.3 2.9 fusion.96
  80.1 10.9 %collective-permute-done.9 = bf16[336,768]{1,0:T(8,128)(2,1)} collective-permute-done((bf16[336,768]{1,0:T(8,128)(2,1)}, bf16[336,768]{1,0:T(8,128)(2,1)}, u32[]{:S(2)}, u32[]{:S(2)}) %collective-permute-start.9) | collective-permute-done | bytes 516128 | tf_op jit(solution)/shard_map/ppermute | solution.py:42
  91.0 31.9 %attend.1 = (bf16[6,2560,256]{2,1,0:T(8,128)(2,1)}, bf16[6,384,256]{2,1,0:T(8,128)(2,1)}, bf16[6,256,128]{2,1,0:T(8,128)(2,1)}, f32[256,768]{1,0:T(8,128)}, f32[256,768]{1,0:T(8,128)}, /*index=5*/f32[6,16,256]{2,1,0:T(8,128)}) custom-call(bf16[1,336,768]{2,1,0:T(8,128)(2,1)} %get-tuple-element.68.refs_0_, bf16[1,336,768]{2,1,0:T(8,128)(2,1)} %bitcast.211, ...), custom_call_target="tpu_custom_call" | custom-call | flops 7549747200 | bytes 20971520 | tf_op jit(solution)/shard_map/attend/pallas_call | solution.py:251
  123.0 1.7 fusion.97
  125.0 4.2 convolution_add_fusion
  129.3 10.5 %fusion.85 = (bf16[3072]{0:T(1024)(128)(2,1)}, bf16[256,3072]{1,0:T(8,128)(2,1)S(1)}, f32[256,3072]{1,0:T(8,128)}) fusion(f32[256,3072]{1,0:T(8,128)S(1)} %convolution_add_fusion, bf16[256,768]{1,0:T(8,128)(2,1)S(1)} %get-tuple-element.107, bf16[3072,768]{1,0:T(8,128)(2,1)S(1)} %bitcast.231), kind=kOutput, calls=%fused_computation.252 | convolution fusion | flops 1265366016 | bytes 12982272 | tf_op jit(solution)/shard_map/dot_general | solution.py:27
  139.8 2.1 multiply_reduce_fusion
  144.7 2.3 copy.86
  153.8 15.9 %collective-permute-start.10 = (bf16[208,768]{1,0:T(8,128)(2,1)}, bf16[208,768]{1,0:T(8,128)(2,1)}, u32[]{:S(2)}, u32[]{:S(2)}) collective-permute-start(bf16[208,768]{1,0:T(8,128)(2,1)} %get-tuple-element.79), channel_id=1, source_target_pairs={{0,2},{1,3},{2,0},{3,1},{4,6},{5,7},{6,4},{7,5},{8,10},{9,11},{10,... | collective-permute-start | bytes 958472 | tf_op jit(solution)/shard_map/ppermute | solution.py:56
  169.7 1.6 collective-permute-start.11
  173.0 3.5 multiply_convert_fusion
  177.8 2.5 convolution_convert_fusion
  180.4 3.7 fusion.13
  184.7 1.7 convolution_convert_fusion.5
  186.3 24.9 %query_back.1 = (bf16[256,768]{1,0:T(8,128)(2,1)}, bf16[6,1536,128]{2,1,0:T(8,128)(2,1)}) custom-call(bf16[1,336,768]{2,1,0:T(8,128)(2,1)} %get-tuple-element.68.refs_0_, bf16[1,336,768]{2,1,0:T(8,128)(2,1)} %bitcast.212, bf16[1,336,768]{2,1,0:T(8,128)(2,1)} %bitcast.4.refs_2_, bf16[1,336,768]{2,1,0:T(8,128)(2,1)} %bitcast.5.refs_3_, ...), custom_call_target="tpu_custom_call" | custom-call | flops 4529848320 | bytes 20971520 | tf_op jit(solution)/shard_map/query_back/pallas_call | solution.py:325
  211.4 2.4 convolution_convert_fusion.2
  224.5 2.5 convolution_convert_fusion.6
  237.2 2.3 fusion.10
  239.5 3.9 collective-permute-done.12
  243.4 1.7 collective-permute-start.14
  248.9 6.5 %collective-permute-done.14 = bf16[208,768]{1,0:T(8,128)(2,1)S(1)} collective-permute-done((bf16[208,768]{1,0:T(8,128)(2,1)}, bf16[208,768]{1,0:T(8,128)(2,1)S(1)}, u32[]{:S(2)}, u32[]{:S(2)}) %collective-permute-start.14) | collective-permute-done | bytes 319520 | tf_op jit(solution)/shard_map/ppermute | solution.py:56
  261.0 1.8 add_convert_fusion.4
  269.9 18.3 %key_back.1 = (bf16[384,768]{1,0:T(8,128)(2,1)}, bf16[384,768]{1,0:T(8,128)(2,1)}) custom-call(bf16[1,208,768]{2,1,0:T(8,128)(2,1)} %copy-done.57, bf16[1,208,768]{2,1,0:T(8,128)(2,1)} %bitcast.15.refs_1_, bf16[1,208,768]{2,1,0:T(8,128)(2,1)} %bitcast.216, bf16[1,208,768]{2,1,0:T(8,128)(2,1)} %bitcast.17.refs_3_, bf16[1,208,768]{2,1,0:T(8,128)(2,1)} %bitcast.18.refs_4_, ...), custom_call_target="tpu_custom_call" | custom-call | flops 3019898880 | bytes 10485760 | tf_op jit(solution)/shard_map/key_back/pallas_call | solution.py:425
  288.2 2.7 fusion.9
  290.9 2.6 fusion.83
  293.7 3.6 convolution_convert_fusion.1
  306.1 2.5 collective-permute-start.20
  308.6 1.7 convolution_convert_fusion.4
  310.4 2.6 add_convert_fusion.1
  313.0 2.1 reshape.378
  315.2 2.1 copy.95
  319.7 1.8 add_convert_fusion.5
  325.8 2.7 add_convert_fusion
  330.3 37.8 %collective-permute-done.22 = bf16[2,2,2,112,384]{4,3,2,1,0:T(8,128)(2,1)S(1)} collective-permute-done((bf16[2,2,2,112,384]{4,3,2,1,0:T(8,128)(2,1)S(1)}, bf16[2,2,2,112,384]{4,3,2,1,0:T(8,128)(2,1)S(1)}, u32[]{:S(2)}, u32[]{:S(2)}) %collective-permute-start.22) | collective-permute-done | bytes 688160 | tf_op jit(solution)/shard_map/ppermute | solution.py:42
  370.1 4.0 add_convert_fusion.2
  374.0 3.8 copy.91
  377.9 5.1 %reshape.373 = bf16[8,96,3,384]{1,0,3,2:T(8,128)(2,1)} reshape(bf16[768,1152]{0,1:T(8,128)(2,1)} %copy.91) | data formatting | bytes 3538944 | tf_op jit(solution)/shard_map/reshape | solution.py:476
  382.9 4.4 copy.92
  388.8 1.9 collective-permute-start.29
  397.3 2.5 collective-permute-start.25
  399.9 11.5 %collective-permute-done.29 = bf16[2,2,2,144,384]{4,3,2,1,0:T(8,128)(2,1)S(1)} collective-permute-done((bf16[2,2,2,144,384]{4,3,2,1,0:T(8,128)(2,1)S(1)}, bf16[2,2,2,144,384]{4,3,2,1,0:T(8,128)(2,1)S(1)}, u32[]{:S(2)}, u32[]{:S(2)}) %collective-permute-start.29) | collective-permute-done | bytes 884768 | tf_op jit(solution)/shard_map/ppermute | solution.py:42
  411.6 1.9 collective-permute-start.26
  414.8 12.8 %collective-permute-done.26 = bf16[112,384]{1,0:T(8,128)(2,1)S(1)} collective-permute-done((bf16[112,384]{1,0:T(8,128)(2,1)S(1)}, bf16[112,384]{1,0:T(8,128)(2,1)S(1)}, u32[]{:S(2)}, u32[]{:S(2)}) %collective-permute-start.26) | collective-permute-done | bytes 86048 | tf_op jit(solution)/shard_map/ppermute | solution.py:42
  427.8 1.7 bitcast_add_fusion
  442.8 4.9 collective-permute-done.31
  447.7 2.5 collective-permute-start.32
  450.9 4.5 collective-permute-done.32
  464.0 1.6 collective-permute-start.47
  465.6 7.0 %collective-permute-done.40 = bf16[240,384]{1,0:T(8,128)(2,1)S(1)} collective-permute-done((bf16[240,384]{1,0:T(8,128)(2,1)S(1)}, bf16[240,384]{1,0:T(8,128)(2,1)S(1)}, u32[]{:S(2)}, u32[]{:S(2)}) %collective-permute-start.40) | collective-permute-done | bytes 184352 | tf_op jit(solution)/shard_map/ppermute | solution.py:42
  474.1 5.0 collective-permute-done.41
  481.0 11.8 %collective-permute-done.48 = bf16[288,384]{1,0:T(8,128)(2,1)S(1)} collective-permute-done((bf16[288,384]{1,0:T(8,128)(2,1)S(1)}, bf16[288,384]{1,0:T(8,128)(2,1)S(1)}, u32[]{:S(2)}, u32[]{:S(2)}) %collective-permute-start.48) | collective-permute-done | bytes 221216 | tf_op jit(solution)/shard_map/ppermute | solution.py:42
  495.3 5.0 collective-permute-done.49
  (470 shorter events, 136.2 us)
Async XLA Ops:
  0.6 75.7 %copy-start = (bf16[768,1536]{1,0:T(8,128)(2,1)S(1)}, bf16[768,1536]{1,0:T(8,128)(2,1)}, u32[]{:S(2)}) copy-start(bf16[768,1536]{1,0:T(8,128)(2,1)} %param.38) | copy-start | bytes 7077892
  13.9 7.3 %collective-permute-start = (bf16[128,768]{1,0:T(8,128)(2,1)S(1)}, bf16[128,768]{1,0:T(8,128)(2,1)S(1)}, u32[]{:S(2)}, u32[]{:S(2)}) collective-permute-start(bf16[128,768]{1,0:T(8,128)(2,1)S(1)} %select_convert_fusion.2), channel_id=1, source_target_pairs={{0,8},{8,16},{16,24},{1,9},{9,17},{17,25},{2,10},{10,18},{18,26},{... | collective-permute-start | bytes 589832 | tf_op jit(solution)/shard_map/ppermute | solution.py:37
  19.2 56.5 %copy-start.79 = (f32[1536]{0:T(1024)S(1)}, f32[1536]{0:T(1024)}, u32[]{:S(2)}) copy-start(f32[1536]{0:T(1024)} %param.29) | copy-start | bytes 18436
  22.6 271.1 %copy-start.39 = (bf16[128,768]{1,0:T(8,128)(2,1)}, bf16[128,768]{1,0:T(8,128)(2,1)S(1)}, u32[]{:S(2)}) copy-start(bf16[128,768]{1,0:T(8,128)(2,1)S(1)} %fusion.32) | copy-start | bytes 589828
  22.6 51.8 %copy-start.90 = (s32[256]{0:T(256)S(1)}, s32[256]{0:T(256)}, u32[]{:S(2)}) copy-start(s32[256]{0:T(256)} %param.23) | copy-start | bytes 3076
  24.5 13.8 %collective-permute-start.1 = (bf16[336,768]{1,0:T(8,128)(2,1)S(1)}, bf16[336,768]{1,0:T(8,128)(2,1)S(1)}, u32[]{:S(2)}, u32[]{:S(2)}) collective-permute-start(bf16[336,768]{1,0:T(8,128)(2,1)S(1)} %get-tuple-element.67), channel_id=1, source_target_pairs={{0,2},{1,3},{2,0},{3,1},{4,6},{5,7},{6,4},{7,5},{8,10},{9,11},{10,... | collective-permute-start | bytes 1548296 | tf_op jit(solution)/shard_map/ppermute | solution.py:56
  26.9 12.8 %collective-permute-start.2 = (bf16[336,768]{1,0:T(8,128)(2,1)S(1)}, bf16[336,768]{1,0:T(8,128)(2,1)}, u32[]{:S(2)}, u32[]{:S(2)}) collective-permute-start(bf16[336,768]{1,0:T(8,128)(2,1)S(1)} %get-tuple-element.67), channel_id=1, source_target_pairs={{2,4},{3,5},{4,2},{5,3},{10,12},{11,13},{12,10},{13,11},{18,20},{1... | collective-permute-start | bytes 1548296 | tf_op jit(solution)/shard_map/ppermute | solution.py:56
  38.3 2.7 collective-permute-start.4
  39.7 18.7 %collective-permute-start.3 = (bf16[336,768]{1,0:T(8,128)(2,1)}, bf16[336,768]{1,0:T(8,128)(2,1)}, u32[]{:S(2)}, u32[]{:S(2)}) collective-permute-start(bf16[336,768]{1,0:T(8,128)(2,1)} %collective-permute-done.2), channel_id=1, source_target_pairs={{2,0},{3,1},{4,6},{5,7},{10,8},{11,9},{12,14},{13,15},{18,16},{19,... | collective-permute-start | bytes 1548296 | tf_op jit(solution)/shard_map/ppermute | solution.py:56
  41.0 29.9 %collective-permute-start.5 = (bf16[336,768]{1,0:T(8,128)(2,1)}, bf16[336,768]{1,0:T(8,128)(2,1)}, u32[]{:S(2)}, u32[]{:S(2)}) collective-permute-start(bf16[336,768]{1,0:T(8,128)(2,1)} %collective-permute-done.4), channel_id=1, source_target_pairs={{2,0},{3,1},{4,6},{5,7},{10,8},{11,9},{12,14},{13,15},{18,16},{19,... | collective-permute-start | bytes 1548296 | tf_op jit(solution)/shard_map/ppermute | solution.py:56
  42.5 37.6 %collective-permute-start.6 = (bf16[336,768]{1,0:T(8,128)(2,1)}, bf16[336,768]{1,0:T(8,128)(2,1)}, u32[]{:S(2)}, u32[]{:S(2)}) collective-permute-start(bf16[336,768]{1,0:T(8,128)(2,1)} %copy-done.54), channel_id=1, source_target_pairs={{0,1},{1,0},{2,3},{3,2},{4,5},{5,4},{6,7},{7,6},{8,9},{9,8},{10,11... | collective-permute-start | bytes 1548296 | tf_op jit(solution)/shard_map/ppermute | solution.py:42
  45.0 35.1 %collective-permute-start.7 = (bf16[336,768]{1,0:T(8,128)(2,1)}, bf16[336,768]{1,0:T(8,128)(2,1)}, u32[]{:S(2)}, u32[]{:S(2)}) collective-permute-start(bf16[336,768]{1,0:T(8,128)(2,1)} %copy-done.55), channel_id=1, source_target_pairs={{0,1},{1,0},{2,3},{3,2},{4,5},{5,4},{6,7},{7,6},{8,9},{9,8},{10,11... | collective-permute-start | bytes 1548296 | tf_op jit(solution)/shard_map/ppermute | solution.py:42
  60.3 19.8 %collective-permute-start.8 = (bf16[336,768]{1,0:T(8,128)(2,1)}, bf16[336,768]{1,0:T(8,128)(2,1)}, u32[]{:S(2)}, u32[]{:S(2)}) collective-permute-start(bf16[336,768]{1,0:T(8,128)(2,1)} %broadcast_select_fusion.1), channel_id=1, source_target_pairs={{0,1},{1,0},{2,3},{3,2},{4,5},{5,4},{6,7},{7,6},{8,9},{9,8},{10,11... | collective-permute-start | bytes 1548296 | tf_op jit(solution)/shard_map/ppermute | solution.py:42
  72.9 18.2 %collective-permute-start.9 = (bf16[336,768]{1,0:T(8,128)(2,1)}, bf16[336,768]{1,0:T(8,128)(2,1)}, u32[]{:S(2)}, u32[]{:S(2)}) collective-permute-start(bf16[336,768]{1,0:T(8,128)(2,1)} %broadcast_select_fusion), channel_id=1, source_target_pairs={{0,1},{1,0},{2,3},{3,2},{4,5},{5,4},{6,7},{7,6},{8,9},{9,8},{10,11... | collective-permute-start | bytes 1548296 | tf_op jit(solution)/shard_map/ppermute | solution.py:42
  79.2 50.1 %copy-start.42 = (bf16[256,768]{1,0:T(8,128)(2,1)}, bf16[256,768]{1,0:T(8,128)(2,1)S(1)}, u32[]{:S(2)}) copy-start(bf16[256,768]{1,0:T(8,128)(2,1)S(1)} %get-tuple-element.107) | copy-start | bytes 1179652
  91.0 31.9 %copy-start.19 = (bf16[768,768]{1,0:T(8,128)(2,1)S(1)}, bf16[768,768]{1,0:T(8,128)(2,1)}, u32[]{:S(2)}) copy-start(bf16[768,768]{1,0:T(8,128)(2,1)} %param.30) | copy-start | bytes 3538948
  91.0 31.9 %copy-start.89 = (f32[768]{0:T(1024)S(1)}, f32[768]{0:T(1024)}, u32[]{:S(2)}) copy-start(f32[768]{0:T(1024)} %param.31) | copy-start | bytes 9220
  153.8 59.9 %copy-start.57 = (bf16[1,208,768]{2,1,0:T(8,128)(2,1)}, bf16[1,208,768]{2,1,0:T(8,128)(2,1)S(1)}, u32[]{:S(2)}) copy-start(bf16[1,208,768]{2,1,0:T(8,128)(2,1)S(1)} %get-tuple-element.80.refs_0_) | copy-start | bytes 958468
  153.8 73.3 %collective-permute-start.10 = (bf16[208,768]{1,0:T(8,128)(2,1)}, bf16[208,768]{1,0:T(8,128)(2,1)}, u32[]{:S(2)}, u32[]{:S(2)}) collective-permute-start(bf16[208,768]{1,0:T(8,128)(2,1)} %get-tuple-element.79), channel_id=1, source_target_pairs={{0,2},{1,3},{2,0},{3,1},{4,6},{5,7},{6,4},{7,5},{8,10},{9,11},{10,... | collective-permute-start | bytes 958472 | tf_op jit(solution)/shard_map/ppermute | solution.py:56
  169.7 61.6 %collective-permute-start.11 = (bf16[208,768]{1,0:T(8,128)(2,1)}, bf16[208,768]{1,0:T(8,128)(2,1)}, u32[]{:S(2)}, u32[]{:S(2)}) collective-permute-start(bf16[208,768]{1,0:T(8,128)(2,1)} %get-tuple-element.79), channel_id=1, source_target_pairs={{2,4},{3,5},{4,2},{5,3},{10,12},{11,13},{12,10},{13,11},{18,20},{1... | collective-permute-start | bytes 958472 | tf_op jit(solution)/shard_map/ppermute | solution.py:56
  171.4 62.6 %collective-permute-start.15 = (bf16[208,768]{1,0:T(8,128)(2,1)}, bf16[208,768]{1,0:T(8,128)(2,1)}, u32[]{:S(2)}, u32[]{:S(2)}) collective-permute-start(bf16[208,768]{1,0:T(8,128)(2,1)} %get-tuple-element.79), channel_id=1, source_target_pairs={{0,1},{1,0},{2,3},{3,2},{4,5},{5,4},{6,7},{7,6},{8,9},{9,8},{10,11... | collective-permute-start | bytes 958472 | tf_op jit(solution)/shard_map/ppermute | solution.py:42
  180.3 145.4 %collective-permute-start.44 = (bf16[3072,384]{1,0:T(8,128)(2,1)}, bf16[3072,384]{1,0:T(8,128)(2,1)}, u32[]{:S(2)}, u32[]{:S(2)}) collective-permute-start(bf16[3072,384]{1,0:T(8,128)(2,1)} %convolution_convert_fusion), channel_id=1, source_target_pairs={{0,8},{8,0},{16,24},{24,16},{1,9},{9,1},{17,25},{25,17},{2,10},{10... | collective-permute-start | bytes 7077896 | tf_op jit(solution)/shard_map/ppermute | solution.py:42
  184.1 52.6 %collective-permute-start.36 = (bf16[768,384]{1,0:T(8,128)(2,1)}, bf16[768,384]{1,0:T(8,128)(2,1)}, u32[]{:S(2)}, u32[]{:S(2)}) collective-permute-start(bf16[768,384]{1,0:T(8,128)(2,1)} %convolution_convert_fusion.7), channel_id=1, source_target_pairs={{0,8},{8,0},{16,24},{24,16},{1,9},{9,1},{17,25},{25,17},{2,10},{10... | collective-permute-start | bytes 1769480 | tf_op jit(solution)/shard_map/ppermute | solution.py:42
  211.3 25.9 %copy-start.6 = (f32[256,768]{1,0:T(8,128)S(1)}, f32[256,768]{1,0:T(8,128)}, u32[]{:S(2)}) copy-start(f32[256,768]{1,0:T(8,128)} %get-tuple-element.26.refs_12_) | copy-start | bytes 2359300
  227.1 33.9 %copy-start.51 = (bf16[256,768]{1,0:T(8,128)(2,1)S(1)}, bf16[256,768]{1,0:T(8,128)(2,1)}, u32[]{:S(2)}) copy-start(bf16[256,768]{1,0:T(8,128)(2,1)} %copy-done.50) | copy-start | bytes 1179652
  229.9 13.5 %collective-permute-start.13 = (bf16[208,768]{1,0:T(8,128)(2,1)}, bf16[208,768]{1,0:T(8,128)(2,1)}, u32[]{:S(2)}, u32[]{:S(2)}) collective-permute-start(bf16[208,768]{1,0:T(8,128)(2,1)} %collective-permute-done.10), channel_id=1, source_target_pairs={{2,4},{3,5},{4,2},{5,3},{10,12},{11,13},{12,10},{13,11},{18,20},{1... | collective-permute-start | bytes 958472 | tf_op jit(solution)/shard_map/ppermute | solution.py:56
  231.3 12.1 %collective-permute-start.12 = (bf16[208,768]{1,0:T(8,128)(2,1)}, bf16[208,768]{1,0:T(8,128)(2,1)}, u32[]{:S(2)}, u32[]{:S(2)}) collective-permute-start(bf16[208,768]{1,0:T(8,128)(2,1)} %collective-permute-done.11), channel_id=1, source_target_pairs={{2,0},{3,1},{4,6},{5,7},{10,8},{11,9},{12,14},{13,15},{18,16},{19,... | collective-permute-start | bytes 958472 | tf_op jit(solution)/shard_map/ppermute | solution.py:56
  233.9 27.0 %collective-permute-start.43 = (bf16[768,768]{1,0:T(8,128)(2,1)}, bf16[768,768]{1,0:T(8,128)(2,1)}, u32[]{:S(2)}, u32[]{:S(2)}) collective-permute-start(bf16[768,768]{1,0:T(8,128)(2,1)} %convolution_convert_fusion.6), channel_id=1, source_target_pairs={{0,8},{8,0},{16,24},{24,16},{1,9},{9,1},{17,25},{25,17},{2,10},{10... | collective-permute-start | bytes 3538952 | tf_op jit(solution)/shard_map/ppermute | solution.py:42
  236.7 10.3 %collective-permute-start.16 = (bf16[208,768]{1,0:T(8,128)(2,1)}, bf16[208,768]{1,0:T(8,128)(2,1)}, u32[]{:S(2)}, u32[]{:S(2)}) collective-permute-start(bf16[208,768]{1,0:T(8,128)(2,1)} %collective-permute-done.10), channel_id=1, source_target_pairs={{0,1},{1,0},{2,3},{3,2},{4,5},{5,4},{6,7},{7,6},{8,9},{9,8},{10,11... | collective-permute-start | bytes 958472 | tf_op jit(solution)/shard_map/ppermute | solution.py:42
  243.4 66.9 %collective-permute-start.35 = (bf16[768,1536]{1,0:T(8,128)(2,1)}, bf16[768,1536]{1,0:T(8,128)(2,1)}, u32[]{:S(2)}, u32[]{:S(2)}) collective-permute-start(bf16[768,1536]{1,0:T(8,128)(2,1)} %convolution_convert_fusion.2), channel_id=1, source_target_pairs={{0,8},{8,0},{16,24},{24,16},{1,9},{9,1},{17,25},{25,17},{2,10},{10... | collective-permute-start | bytes 7077896 | tf_op jit(solution)/shard_map/ppermute | solution.py:42
  243.4 12.0 %collective-permute-start.14 = (bf16[208,768]{1,0:T(8,128)(2,1)}, bf16[208,768]{1,0:T(8,128)(2,1)S(1)}, u32[]{:S(2)}, u32[]{:S(2)}) collective-permute-start(bf16[208,768]{1,0:T(8,128)(2,1)} %collective-permute-done.13), channel_id=1, source_target_pairs={{2,0},{3,1},{4,6},{5,7},{10,8},{11,9},{12,14},{13,15},{18,16},{19,... | collective-permute-start | bytes 958472 | tf_op jit(solution)/shard_map/ppermute | solution.py:56
  247.0 10.6 %collective-permute-start.17 = (bf16[208,768]{1,0:T(8,128)(2,1)S(1)}, bf16[208,768]{1,0:T(8,128)(2,1)S(1)}, u32[]{:S(2)}, u32[]{:S(2)}) collective-permute-start(bf16[208,768]{1,0:T(8,128)(2,1)S(1)} %broadcast_select_fusion.3), channel_id=1, source_target_pairs={{0,1},{1,0},{2,3},{3,2},{4,5},{5,4},{6,7},{7,6},{8,9},{9,8},{10,11... | collective-permute-start | bytes 958472 | tf_op jit(solution)/shard_map/ppermute | solution.py:42
  256.2 9.5 %collective-permute-start.18 = (bf16[208,768]{1,0:T(8,128)(2,1)}, bf16[208,768]{1,0:T(8,128)(2,1)}, u32[]{:S(2)}, u32[]{:S(2)}) collective-permute-start(bf16[208,768]{1,0:T(8,128)(2,1)} %broadcast_select_fusion.2), channel_id=1, source_target_pairs={{0,1},{1,0},{2,3},{3,2},{4,5},{5,4},{6,7},{7,6},{8,9},{9,8},{10,11... | collective-permute-start | bytes 958472 | tf_op jit(solution)/shard_map/ppermute | solution.py:42
  297.4 72.6 %collective-permute-start.28 = (bf16[768,1152]{1,0:T(8,128)(2,1)}, bf16[768,1152]{1,0:T(8,128)(2,1)}, u32[]{:S(2)}, u32[]{:S(2)}) collective-permute-start(bf16[768,1152]{1,0:T(8,128)(2,1)} %convolution_convert_fusion.1), channel_id=1, source_target_pairs={{0,8},{8,0},{16,24},{24,16},{1,9},{9,1},{17,25},{25,17},{2,10},{10... | collective-permute-start | bytes 5308424 | tf_op jit(solution)/shard_map/ppermute | solution.py:42
  298.6 4.8 collective-permute-start.19
  300.6 7.9 %collective-permute-start.21 = (bf16[8,576]{1,0:T(8,128)(2,1)S(1)}, bf16[8,576]{1,0:T(8,128)(2,1)S(1)}, u32[]{:S(2)}, u32[]{:S(2)}) collective-permute-start(bf16[8,576]{1,0:T(8,128)(2,1)S(1)} %bitcast.219), channel_id=1, source_target_pairs={{0,8},{8,0},{16,24},{24,16},{1,9},{9,1},{17,25},{25,17},{2,10},{10... | collective-permute-start | bytes 27656 | tf_op jit(solution)/shard_map/ppermute | solution.py:42
  306.1 13.4 %collective-permute-start.20 = (bf16[1536,384]{0,1:T(8,128)(2,1)}, bf16[1536,384]{0,1:T(8,128)(2,1)}, u32[]{:S(2)}, u32[]{:S(2)}) collective-permute-start(bf16[1536,384]{0,1:T(8,128)(2,1)} %fusion.7), channel_id=1, source_target_pairs={{0,8},{8,0},{16,24},{24,16},{1,9},{9,1},{17,25},{25,17},{2,10},{10... | collective-permute-start | bytes 3538952 | tf_op jit(solution)/shard_map/ppermute | solution.py:42
  318.9 74.3 %collective-permute-start.37 = (bf16[2,2,2,240,384]{4,3,2,1,0:T(8,128)(2,1)}, bf16[2,2,2,240,384]{4,3,2,1,0:T(8,128)(2,1)}, u32[]{:S(2)}, u32[]{:S(2)}) collective-permute-start(bf16[2,2,2,240,384]{4,3,2,1,0:T(8,128)(2,1)} %dynamic-slice_bitcast_fusion.1), channel_id=1, source_target_pairs={{0,1},{1,0},{2,3},{3,2},{4,5},{5,4},{6,7},{7,6},{8,9},{9,8},{10,11... | collective-permute-start | bytes 4423688 | tf_op jit(solution)/shard_map/ppermute | solution.py:42
  324.4 43.7 %collective-permute-start.22 = (bf16[2,2,2,112,384]{4,3,2,1,0:T(8,128)(2,1)S(1)}, bf16[2,2,2,112,384]{4,3,2,1,0:T(8,128)(2,1)S(1)}, u32[]{:S(2)}, u32[]{:S(2)}) collective-permute-start(bf16[2,2,2,112,384]{4,3,2,1,0:T(8,128)(2,1)S(1)} %dynamic-slice_bitcast_fusion.4), channel_id=1, source_target_pairs={{0,1},{1,0},{2,3},{3,2},{4,5},{5,4},{6,7},{7,6},{8,9},{9,8},{10,11... | collective-permute-start | bytes 2064392 | tf_op jit(solution)/shard_map/ppermute | solution.py:42
  328.8 41.2 %copy-start.34 = (bf16[256,768]{1,0:T(8,128)(2,1)S(1)}, bf16[256,768]{1,0:T(8,128)(2,1)}, u32[]{:S(2)}) copy-start(bf16[256,768]{1,0:T(8,128)(2,1)} %copy-done.31) | copy-start | bytes 1179652
  328.9 41.2 %copy-start.40 = (bf16[128,768]{1,0:T(8,128)(2,1)S(1)}, bf16[128,768]{1,0:T(8,128)(2,1)}, u32[]{:S(2)}) copy-start(bf16[128,768]{1,0:T(8,128)(2,1)} %copy-done.39) | copy-start | bytes 589828
  328.9 41.2 %copy-start.41 = (bf16[384,2304]{1,0:T(8,128)(2,1)S(1)}, bf16[384,2304]{1,0:T(8,128)(2,1)}, u32[]{:S(2)}) copy-start(bf16[384,2304]{1,0:T(8,128)(2,1)} %fusion.9) | copy-start | bytes 5308420
  330.3 97.4 %collective-permute-start.45 = (bf16[2,2,2,288,384]{4,3,2,1,0:T(8,128)(2,1)}, bf16[2,2,2,288,384]{4,3,2,1,0:T(8,128)(2,1)}, u32[]{:S(2)}, u32[]{:S(2)}) collective-permute-start(bf16[2,2,2,288,384]{4,3,2,1,0:T(8,128)(2,1)} %dynamic-slice_bitcast_fusion), channel_id=1, source_target_pairs={{0,16},{8,24},{16,0},{24,8},{1,17},{9,25},{17,1},{25,9},{2,18},{10... | collective-permute-start | bytes 5308424 | tf_op jit(solution)/shard_map/ppermute | solution.py:42
  369.8 20.8 %collective-permute-start.23 = (bf16[2,2,112,384]{3,2,1,0:T(8,128)(2,1)}, bf16[2,2,112,384]{3,2,1,0:T(8,128)(2,1)}, u32[]{:S(2)}, u32[]{:S(2)}) collective-permute-start(bf16[2,2,112,384]{3,2,1,0:T(8,128)(2,1)} %dynamic-slice_bitcast_fusion.8), channel_id=1, source_target_pairs={{0,16},{8,24},{16,0},{24,8},{1,17},{9,25},{17,1},{25,9},{2,18},{10... | collective-permute-start | bytes 1032200 | tf_op jit(solution)/shard_map/ppermute | solution.py:42
  388.8 22.6 %collective-permute-start.29 = (bf16[2,2,2,144,384]{4,3,2,1,0:T(8,128)(2,1)S(1)}, bf16[2,2,2,144,384]{4,3,2,1,0:T(8,128)(2,1)S(1)}, u32[]{:S(2)}, u32[]{:S(2)}) collective-permute-start(bf16[2,2,2,144,384]{4,3,2,1,0:T(8,128)(2,1)S(1)} %dynamic-slice_bitcast_fusion.2), channel_id=1, source_target_pairs={{0,16},{8,24},{16,0},{24,8},{1,17},{9,25},{17,1},{25,9},{2,18},{10... | collective-permute-start | bytes 2654216 | tf_op jit(solution)/shard_map/ppermute | solution.py:42
  391.8 5.5 %collective-permute-start.24 = (bf16[2,112,384]{2,1,0:T(8,128)(2,1)S(1)}, bf16[2,112,384]{2,1,0:T(8,128)(2,1)S(1)}, u32[]{:S(2)}, u32[]{:S(2)}) collective-permute-start(bf16[2,112,384]{2,1,0:T(8,128)(2,1)S(1)} %dynamic-slice_bitcast_fusion.12), channel_id=1, source_target_pairs={{0,2},{1,3},{2,0},{3,1},{4,6},{5,7},{6,4},{7,5},{8,10},{9,11},{10,... | collective-permute-start | bytes 516104 | tf_op jit(solution)/shard_map/ppermute | solution.py:42
  395.9 45.6 %collective-permute-start.38 = (bf16[2,2,240,384]{3,2,1,0:T(8,128)(2,1)}, bf16[2,2,240,384]{3,2,1,0:T(8,128)(2,1)}, u32[]{:S(2)}, u32[]{:S(2)}) collective-permute-start(bf16[2,2,240,384]{3,2,1,0:T(8,128)(2,1)} %dynamic-slice_bitcast_fusion.3), channel_id=1, source_target_pairs={{0,16},{8,24},{16,0},{24,8},{1,17},{9,25},{17,1},{25,9},{2,18},{10... | collective-permute-start | bytes 2211848 | tf_op jit(solution)/shard_map/ppermute | solution.py:42
  397.3 14.2 %collective-permute-start.25 = (bf16[112,384]{1,0:T(8,128)(2,1)S(1)}, bf16[112,384]{1,0:T(8,128)(2,1)S(1)}, u32[]{:S(2)}, u32[]{:S(2)}) collective-permute-start(bf16[112,384]{1,0:T(8,128)(2,1)S(1)} %dynamic-slice_bitcast_fusion.14), channel_id=1, source_target_pairs={{0,4},{1,5},{2,6},{3,7},{4,0},{5,1},{6,2},{7,3},{8,12},{9,13},{10,... | collective-permute-start | bytes 258056 | tf_op jit(solution)/shard_map/ppermute | solution.py:42
  411.6 16.0 %collective-permute-start.26 = (bf16[112,384]{1,0:T(8,128)(2,1)S(1)}, bf16[112,384]{1,0:T(8,128)(2,1)S(1)}, u32[]{:S(2)}, u32[]{:S(2)}) collective-permute-start(bf16[112,384]{1,0:T(8,128)(2,1)S(1)} %bitcast_add_fusion.15), channel_id=1, source_target_pairs={{0,16},{8,24},{16,0},{24,8},{1,17},{9,25},{17,1},{25,9},{2,18},{10... | collective-permute-start | bytes 258056 | tf_op jit(solution)/shard_map/ppermute | solution.py:42
  414.3 24.6 %collective-permute-start.30 = (bf16[2,2,144,384]{3,2,1,0:T(8,128)(2,1)}, bf16[2,2,144,384]{3,2,1,0:T(8,128)(2,1)}, u32[]{:S(2)}, u32[]{:S(2)}) collective-permute-start(bf16[2,2,144,384]{3,2,1,0:T(8,128)(2,1)} %dynamic-slice_bitcast_fusion.6), channel_id=1, source_target_pairs={{0,1},{1,0},{2,3},{3,2},{4,5},{5,4},{6,7},{7,6},{8,9},{9,8},{10,11... | collective-permute-start | bytes 1327112 | tf_op jit(solution)/shard_map/ppermute | solution.py:42
  427.7 3.6 collective-permute-start.27
  430.7 31.9 %collective-permute-start.46 = (bf16[2,2,288,384]{3,2,0,1:T(8,128)(2,1)}, bf16[2,2,288,384]{3,2,0,1:T(8,128)(2,1)}, u32[]{:S(2)}, u32[]{:S(2)}) collective-permute-start(bf16[2,2,288,384]{3,2,0,1:T(8,128)(2,1)} %bitcast.175), channel_id=1, source_target_pairs={{0,1},{1,0},{2,3},{3,2},{4,5},{5,4},{6,7},{7,6},{8,9},{9,8},{10,11... | collective-permute-start | bytes 2654216 | tf_op jit(solution)/shard_map/ppermute | solution.py:42
  440.1 7.6 %collective-permute-start.31 = (bf16[2,144,384]{2,1,0:T(8,128)(2,1)S(1)}, bf16[2,144,384]{2,1,0:T(8,128)(2,1)S(1)}, u32[]{:S(2)}, u32[]{:S(2)}) collective-permute-start(bf16[2,144,384]{2,1,0:T(8,128)(2,1)S(1)} %dynamic-slice_bitcast_fusion.10), channel_id=1, source_target_pairs={{0,2},{1,3},{2,0},{3,1},{4,6},{5,7},{6,4},{7,5},{8,10},{9,11},{10,... | collective-permute-start | bytes 663560 | tf_op jit(solution)/shard_map/ppermute | solution.py:42
  447.7 7.7 %collective-permute-start.32 = (bf16[144,384]{1,0:T(8,128)(2,1)S(1)}, bf16[144,384]{1,0:T(8,128)(2,1)S(1)}, u32[]{:S(2)}, u32[]{:S(2)}) collective-permute-start(bf16[144,384]{1,0:T(8,128)(2,1)S(1)} %dynamic-slice_bitcast_fusion.13), channel_id=1, source_target_pairs={{0,4},{1,5},{2,6},{3,7},{4,0},{5,1},{6,2},{7,3},{8,12},{9,13},{10,... | collective-permute-start | bytes 331784 | tf_op jit(solution)/shard_map/ppermute | solution.py:42
  450.3 11.2 %collective-permute-start.39 = (bf16[2,240,384]{2,1,0:T(8,128)(2,1)S(1)}, bf16[2,240,384]{2,1,0:T(8,128)(2,1)S(1)}, u32[]{:S(2)}, u32[]{:S(2)}) collective-permute-start(bf16[2,240,384]{2,1,0:T(8,128)(2,1)S(1)} %dynamic-slice_bitcast_fusion.7), channel_id=1, source_target_pairs={{0,2},{1,3},{2,0},{3,1},{4,6},{5,7},{6,4},{7,5},{8,10},{9,11},{10,... | collective-permute-start | bytes 1105928 | tf_op jit(solution)/shard_map/ppermute | solution.py:42
  455.5 4.9 collective-permute-start.33
  460.4 13.6 %collective-permute-start.34 = (bf16[288,384]{1,0:T(8,128)(2,1)S(1)}, bf16[288,384]{1,0:T(8,128)(2,1)S(1)}, u32[]{:S(2)}, u32[]{:S(2)}) collective-permute-start(bf16[288,384]{1,0:T(8,128)(2,1)S(1)} %pad_maximum_fusion.13), channel_id=1, source_target_pairs={{0,8},{8,0},{16,24},{24,16},{1,9},{9,1},{17,25},{25,17},{2,10},{10... | collective-permute-start | bytes 663560 | tf_op jit(solution)/shard_map/ppermute | solution.py:42
  461.5 11.1 %collective-permute-start.40 = (bf16[240,384]{1,0:T(8,128)(2,1)S(1)}, bf16[240,384]{1,0:T(8,128)(2,1)S(1)}, u32[]{:S(2)}, u32[]{:S(2)}) collective-permute-start(bf16[240,384]{1,0:T(8,128)(2,1)S(1)} %dynamic-slice_bitcast_fusion.11), channel_id=1, source_target_pairs={{0,4},{1,5},{2,6},{3,7},{4,0},{5,1},{6,2},{7,3},{8,12},{9,13},{10,... | collective-permute-start | bytes 552968 | tf_op jit(solution)/shard_map/ppermute | solution.py:42
  464.0 15.8 %collective-permute-start.47 = (bf16[2,288,384]{2,1,0:T(8,128)(2,1)S(1)}, bf16[2,288,384]{2,1,0:T(8,128)(2,1)S(1)}, u32[]{:S(2)}, u32[]{:S(2)}) collective-permute-start(bf16[2,288,384]{2,1,0:T(8,128)(2,1)S(1)} %dynamic-slice_bitcast_fusion.5), channel_id=1, source_target_pairs={{0,2},{1,3},{2,0},{3,1},{4,6},{5,7},{6,4},{7,5},{8,10},{9,11},{10,... | collective-permute-start | bytes 1327112 | tf_op jit(solution)/shard_map/ppermute | solution.py:42
  472.7 6.5 %collective-permute-start.41 = (bf16[240,384]{1,0:T(8,128)(2,1)S(1)}, bf16[240,384]{1,0:T(8,128)(2,1)S(1)}, u32[]{:S(2)}, u32[]{:S(2)}) collective-permute-start(bf16[240,384]{1,0:T(8,128)(2,1)S(1)} %bitcast_add_fusion.12), channel_id=1, source_target_pairs={{0,16},{8,24},{16,0},{24,8},{1,17},{9,25},{17,1},{25,9},{2,18},{10... | collective-permute-start | bytes 552968 | tf_op jit(solution)/shard_map/ppermute | solution.py:42
  479.3 14.9 %collective-permute-start.42 = (bf16[480,384]{1,0:T(8,128)(2,1)S(1)}, bf16[480,384]{1,0:T(8,128)(2,1)S(1)}, u32[]{:S(2)}, u32[]{:S(2)}) collective-permute-start(bf16[480,384]{1,0:T(8,128)(2,1)S(1)} %pad_maximum_fusion.10), channel_id=1, source_target_pairs={{0,8},{8,0},{16,24},{24,16},{1,9},{9,1},{17,25},{25,17},{2,10},{10... | collective-permute-start | bytes 1105928 | tf_op jit(solution)/shard_map/ppermute | solution.py:42
  479.9 12.9 %collective-permute-start.48 = (bf16[288,384]{1,0:T(8,128)(2,1)S(1)}, bf16[288,384]{1,0:T(8,128)(2,1)S(1)}, u32[]{:S(2)}, u32[]{:S(2)}) collective-permute-start(bf16[288,384]{1,0:T(8,128)(2,1)S(1)} %dynamic-slice_bitcast_fusion.9), channel_id=1, source_target_pairs={{0,4},{1,5},{2,6},{3,7},{4,0},{5,1},{6,2},{7,3},{8,12},{9,13},{10,... | collective-permute-start | bytes 663560 | tf_op jit(solution)/shard_map/ppermute | solution.py:42
  492.8 7.4 %collective-permute-start.49 = (bf16[288,384]{1,0:T(8,128)(2,1)S(1)}, bf16[288,384]{1,0:T(8,128)(2,1)S(1)}, u32[]{:S(2)}, u32[]{:S(2)}) collective-permute-start(bf16[288,384]{1,0:T(8,128)(2,1)S(1)} %bitcast_add_fusion.10), channel_id=1, source_target_pairs={{0,16},{8,24},{16,0},{24,8},{1,17},{9,25},{17,1},{25,9},{2,18},{10... | collective-permute-start | bytes 663560 | tf_op jit(solution)/shard_map/ppermute | solution.py:42
  500.4 1.9 collective-permute-start.50
  (87 other events, 620.0 us)

commit v2 on v1

v2 whole, which is shorter than its diff:
```python
import functools

import jax
import jax.numpy as jnp
import numpy as np
from jax import lax
from jax.experimental import pallas as pl
from jax.experimental.pallas import tpu as pltpu
from jax.sharding import PartitionSpec as P

HEADS = 12
HEAD_DIM = 64
PAIR = 2 * HEAD_DIM
PAIRS = HEADS // 2
SCALE = HEAD_DIM**-0.5
LANES = 384
SHARED = 192
MARKS = 16
GRID_SIDE = 56
EPS = 1e-06
NEG = -1e30
F32 = jnp.float32
BF16 = jnp.bfloat16
VMEM_LIMIT = 56 * 2**20


def dot(a, b):
    return jnp.dot(a, b, preferred_element_type=F32)


def dot_nt(a, b, precision=None):
    return lax.dot_general(a, b, (((1,), (1,)), ((), ())), preferred_element_type=F32, precision=precision)


def dot_tn(a, b):
    return lax.dot_general(a, b, (((0,), (0,)), ((), ())), preferred_element_type=F32)


def sds(shape, dtype):
    return jax.ShapeDtypeStruct(tuple(shape), dtype)


def shifted(x, axis, by):
    length = lax.axis_size(axis)
    pairs = [(i, i + by) for i in range(length) if 0 <= i + by < length]
    return lax.ppermute(x, axis, pairs)


def swap(x, axis, bit):
    length = lax.axis_size(axis)
    return lax.ppermute(x, axis, [(i, i ^ bit) for i in range(length)])


def gather_column(unit):
    n = lax.axis_size("gy")
    if n != 8:
        whole = lax.all_gather(unit, "gy", axis=0, tiled=False)
        return [[whole]]
    place = lax.axis_index("gy") // 2
    at_end = (place == 0) | (place == 3)

    def along(x, hops):
        pairs = [(2 * a + y, 2 * b + y) for a, b in hops for y in (0, 1)]
        return lax.ppermute(x, "gy", pairs)

    def across(x):
        return swap(x, "gy", 1)

    outer = [(0, 1), (1, 0), (2, 3), (3, 2)]
    middle = [(1, 2), (2, 1)]
    outward = [(1, 0), (2, 3)]
    y0 = across(unit)
    near = along(unit, outer)
    mid = along(unit, middle)
    y1 = across(near)
    far_end = along(mid, outward)
    far_mid = along(near, middle)
    far = jnp.where(at_end, far_end, far_mid)
    y2 = across(far)
    last_end = along(far_mid, outward)
    last = jnp.where(at_end, last_end, mid)
    y3 = across(last)
    groups = [[unit, near, y0], [y1, far, last], [y2, y3]]
    return [[part[None] for part in group] for group in groups]


def bit_of(axis, bit):
    return (lax.axis_index(axis) // bit) % 2


def call(kernel, ins, outs, name, grid=None, scratch=(), cost=4.0, after=()):
    specs = [spec for _, spec in ins] + [pl.BlockSpec(memory_space=pl.ANY)] * len(after)
    count = len(ins)

    def body(*refs):
        kernel(*refs[:count], *refs[count + len(after) :])

    return pl.pallas_call(
        body,
        grid=grid or (),
        in_specs=specs,
        out_specs=tuple(spec for _, spec in outs),
        out_shape=tuple(shape for shape, _ in outs),
        scratch_shapes=list(scratch),
        compiler_params=pltpu.CompilerParams(vmem_limit_bytes=VMEM_LIMIT),
        cost_estimate=pl.CostEstimate(flops=int(cost * 1e8), bytes_accessed=int(cost * 3e5), transcendentals=0),
        name=name,
    )(*[array for array, _ in ins], *after)


VMEM = pl.BlockSpec(memory_space=pltpu.VMEM)


def plain(*arrays):
    return [(a, VMEM) for a in arrays]


def fixed(array):
    zeros = (0,) * len(array.shape)
    return (array, pl.BlockSpec(tuple(array.shape), lambda h: zeros, pipeline_mode=pl.Buffered(1)))


def lead(array, first=0):
    zeros = (0,) * (len(array.shape) - 1)
    return (array, pl.BlockSpec((1,) + tuple(array.shape[1:]), lambda h: (first + h,) + zeros))


def lanes(array, first=0, width=PAIR):
    return (array, pl.BlockSpec((array.shape[0], width), lambda h: (0, first + h)))


def half_mask(rows):
    return lax.broadcasted_iota(jnp.int32, (rows, PAIR), 1) < HEAD_DIM


def only_half(x, head):
    low_half = half_mask(x.shape[0])
    zero = jnp.zeros_like(x)
    return jnp.where(low_half, x, zero) if head == 0 else jnp.where(low_half, zero, x)


def merge_halves(first, second):
    rows = first.shape[0]
    return jnp.where(half_mask(rows), jnp.broadcast_to(first, (rows, PAIR)), jnp.broadcast_to(second, (rows, PAIR)))


def normalise(x):
    centered = x - jnp.mean(x, axis=1, keepdims=True)
    scale = lax.rsqrt(jnp.mean(centered * centered, axis=1, keepdims=True) + EPS)
    return centered * scale, scale


def norm_back(grad, unit_rows, scale, gain):
    g = grad * gain
    inner = jnp.mean(g * unit_rows, axis=1, keepdims=True)
    rows = scale * (g - jnp.mean(g, axis=1, keepdims=True) - unit_rows * inner)
    return rows, jnp.sum(grad * unit_rows, axis=0, keepdims=True), jnp.sum(grad, axis=0, keepdims=True)


def group_blocks(block_refs):
    flat = [(ref, i) for ref in block_refs for i in range(ref.shape[0])]
    return [flat[i : i + 8] for i in range(0, len(flat), 8)]


def key_bias(groups, key_rows):
    rows = []
    for group in groups:
        width = len(group) * key_rows
        lane = lax.broadcasted_iota(jnp.int32, (1, width), 1).astype(F32)
        bias = jnp.full((1, width), NEG, F32)
        for place, (ref, index) in enumerate(group):
            marks = ref[index, key_rows : key_rows + MARKS, 0:256].astype(F32)
            count, live = marks[0:1, 0:1], marks[0:1, 128:129]
            local = lane - float(place * key_rows)
            good = (local >= 0.0) & (local < count)
            rim = (local >= float(SHARED)) & (local < float(key_rows)) & (live > 0.5)
            bias = jnp.where(good | rim, 0.0, bias)
        rows.append(bias)
    return rows


def position_table(width):
    unit_width = width // 16
    table = np.zeros((128, width), np.float32)
    bands = [(0, 8, 0, 4 * unit_width), (8, GRID_SIDE, 4 * unit_width, 6 * unit_width)]
    bands.append((64, GRID_SIDE, 10 * unit_width, 6 * unit_width))
    for row, count, lane, band in bands:
        half = band // 2
        power = np.arange(half, dtype=np.float32) / np.float32(half)
        omegas = np.float32(1.0) / np.power(np.float32(10000.0), power)
        angles = (np.arange(count, dtype=np.float32)[:, None] * omegas[None]).astype(np.float64)
        table[row : row + count, lane : lane + half] = np.sin(angles)
        table[row : row + count, lane + half : lane + band] = np.cos(angles)
    high = table.astype(jnp.bfloat16)
    low = (table - high.astype(np.float32)).astype(jnp.bfloat16)
    return jnp.asarray(high), jnp.asarray(low)


def embed_kernel(pix, weight, frame, cell, halo, high, low, gain, bias, stream_ref, rim_ref, low_ref):
    rows = pix.shape[0]
    code = lax.broadcasted_iota(jnp.int32, (128, rows), 0)
    first, second = cell[0:1, :], cell[1:2, :]
    hot = (code == frame[...]) | (code == first + 8) | (code == second + 64)
    hot = jnp.where(hot, 1.0, 0.0).astype(BF16)
    stream = dot(pix[...], weight[...]) + (dot_tn(hot, high[...]) + dot_tn(hot, low[...]))
    stream_ref[...] = stream
    place = lax.broadcasted_iota(jnp.int32, (rows, halo.shape[1]), 0)
    pick = jnp.where(place == halo[...], 1.0, 0.0).astype(BF16)
    rim_ref[...] = dot_tn(pick, stream.astype(BF16)).astype(BF16)
    unit_rows, _ = normalise(stream)
    low_ref[...] = (unit_rows * gain[...] + bias[...]).astype(BF16)


def unit_kernel(own, arrived, gain, bias, ids, live, unit_ref, joined_ref):
    rows, width = own.shape
    rim = arrived.shape[0]
    unit_rows, _ = normalise(arrived[...].astype(F32))
    rim_low = (unit_rows * gain[...] + bias[...]).astype(BF16)
    joined_ref[0:rows, :] = own[...]
    joined_ref[rows : rows + rim, :] = rim_low
    unit_ref[0:SHARED, :] = own[0:SHARED, :]
    unit_ref[SHARED : SHARED + rim, :] = rim_low
    count = jnp.sum(jnp.where(ids[...] == 0, 1.0, 0.0), axis=1, keepdims=True)
    lane = lax.broadcasted_iota(jnp.int32, (MARKS, width), 1)
    unit_ref[SHARED + rim :, :] = jnp.where(lane < 128, count, live[0:1, 0:1]).astype(BF16)


def attend_kernel(n_blocks, key_rows, first, last, *refs):
    refs = list(refs)

    def take(n):
        out = refs[:n]
        del refs[:n]
        return out

    block_refs = take(n_blocks)
    wk_ref, wv_ref, bv_ref = take(3)
    if first:
        own_ref, wq_ref, bq_ref, idr_ref = take(4)
    else:
        q_ref, acc_in, peak_in, weight_in = take(4)
        if last:
            out_in, lse_in = take(2)
    idc_ref = take(1)[0]
    kv_ref = take(1)[0]
    if first:
        q_ref, kvown_ref = take(2)
        if not last:
            out_ref, lse_ref = take(2)
    if last:
        mixed_ref, full_lse_ref = take(2)
    else:
        acc_ref, peak_ref, weight_ref = take(3)
    own_rows = idc_ref.shape[0]
    wkv = jnp.concatenate([wk_ref[...], wv_ref[...]], axis=1)
    shift = jnp.concatenate([jnp.zeros_like(bv_ref[...]), bv_ref[...]], axis=1)
    groups = group_blocks(block_refs)
    base = 0
    for group in groups:
        for ref, index in group:
            kv_ref[0, base : base + key_rows, :] = (dot(ref[index, 0:key_rows, :], wkv) + shift).astype(BF16)
            base += key_rows
    if first:
        kvown_ref[0] = (dot(own_ref[...], wkv) + shift).astype(BF16)
        q = (dot(own_ref[0:own_rows, :], wq_ref[...]) + bq_ref[...]).astype(BF16) * BF16(SCALE)
        q_ref[0] = q
    else:
        q = q_ref[0]
    biases = key_bias(groups, key_rows)
    results = []
    for head in range(2):
        qs = only_half(q[0:SHARED], head)
        column = slice(head * HEAD_DIM, head * HEAD_DIM + 1)
        if first:
            peak = weight = total = None
        else:
            peak, weight, total = peak_in[:, column], weight_in[:, column], acc_in[...]
        base = 0
        for group, bias in zip(groups, biases):
            width = len(group) * key_rows
            keys = kv_ref[0, base : base + width, 0:PAIR]
            values = kv_ref[0, base : base + width, PAIR:]
            base += width
            scores = dot_nt(qs, keys) + bias
            top = jnp.max(scores, axis=1, keepdims=True)
            if peak is None:
                probs = jnp.exp(scores - top)
                weight = jnp.sum(probs, axis=1, keepdims=True)
                total = dot(probs.astype(BF16), values)
                peak = top
            else:
                new = jnp.maximum(peak, top)
                probs = jnp.exp(scores - new)
                fade = jnp.exp(peak - new)
                weight = weight * fade + jnp.sum(probs, axis=1, keepdims=True)
                total = total * fade + dot(probs.astype(BF16), values)
                peak = new
        results.append((total, peak, weight))
    (total_a, peak_a, weight_a), (total_b, peak_b, weight_b) = results
    if first:
        idc = idc_ref[...]
        allowed = (idc == idr_ref[...]) & (idc != 0)
        local = []
        for head in range(2):
            scores = jnp.where(allowed, dot_nt(only_half(q, head), kvown_ref[0, 0:own_rows, 0:PAIR]), NEG)
            top = jnp.max(scores, axis=1, keepdims=True)
            probs = jnp.exp(scores - top)
            weight = jnp.sum(probs, axis=1, keepdims=True)
            out = dot(probs.astype(BF16), kvown_ref[0, 0:own_rows, PAIR:]) / weight
            local.append((out, top + jnp.log(weight)))
        local_out = merge_halves(local[0][0], local[1][0])
        local_lse = merge_halves(local[0][1], local[1][1])
        if not last:
            out_ref[...] = local_out
            lse_ref[...] = local_lse
    elif last:
        local_out, local_lse = out_in[...], lse_in[...]
    if last:
        shared_row = idc_ref[0:SHARED, :] == 0
        shared_out = merge_halves(total_a / weight_a, total_b / weight_b)
        shared_lse = merge_halves(peak_a + jnp.log(weight_a), peak_b + jnp.log(weight_b))
        mixed_ref[0:SHARED, :] = jnp.where(shared_row, shared_out, local_out[0:SHARED])
        mixed_ref[SHARED:, :] = local_out[SHARED:]
        full_lse_ref[0:SHARED, :] = jnp.where(shared_row, shared_lse, local_lse[0:SHARED])
        full_lse_ref[SHARED:, :] = local_lse[SHARED:]
    else:
        acc_ref[...] = merge_halves(total_a, total_b)
        peak_ref[...] = merge_halves(peak_a, peak_b)
        weight_ref[...] = merge_halves(weight_a, weight_b)


def attend(groups, first_low, w_project, project_bias, idc, idr, key_rows):
    own_rows, width = idc.shape[0], first_low.shape[1]
    wide = lambda rows: (sds((rows, width), F32), pl.BlockSpec((rows, PAIR), lambda h: (0, h)))
    deep = lambda rows, lane: (sds((PAIRS, rows, lane), BF16), pl.BlockSpec((1, rows, lane), lambda h: (h, 0, 0)))
    kvs, state = [], None
    for place, blocks in enumerate(groups):
        first, last = place == 0, place == len(groups) - 1
        keys = sum(b.shape[0] for b in blocks) * key_rows
        ins = [fixed(b) for b in blocks]
        ins += [lanes(w_project, PAIRS), lanes(w_project, 2 * PAIRS), lanes(project_bias, PAIRS)]
        if first:
            ins += [fixed(first_low), lanes(w_project), lanes(project_bias), fixed(idr)]
        else:
            ins += [lead(q)] + [lanes(s) for s in state]
            if last:
                ins += [lanes(local_out), lanes(local_lse)]
        ins += [fixed(idc)]
        outs = [deep(keys, 2 * PAIR)]
        if first:
            outs += [deep(own_rows, PAIR), deep(first_low.shape[0], 2 * PAIR)]
            if not last:
                outs += [wide(own_rows)] * 2
        outs += [wide(own_rows)] * 2 if last else [wide(SHARED)] * 3
        got = list(
            call(
                functools.partial(attend_kernel, len(blocks), key_rows, first, last),
                ins,
                outs,
                "attend",
                grid=(PAIRS,),
                cost=keys / 320.0 * 2,
            )
        )
        kvs.append(got.pop(0))
        if first:
            q, kvown = got.pop(0), got.pop(0)
            if not last:
                local_out, local_lse = got.pop(0), got.pop(0)
        state = got
    mixed, lse = state
    return kvs, kvown, q, mixed, lse


def erf(x):
    x = jnp.clip(x, -3.832506856900711, 3.832506856900711)
    s = x * x
    top = -2.72614225801306e-10
    for c in (2.77068142495902e-08, -2.10102402082508e-06, -5.69250639462346e-05, -7.34990630326855e-04, -2.95459980854025e-03, -1.60960333262415e-02):
        top = top * s + c
    low = -1.45660718464996e-05
    for c in (-2.13374055278905e-04, -1.68282697438203e-03, -7.37332916720468e-03, -1.42647390514189e-02):
        low = low * s + c
    return x * top / low


def middle_kernel(
    mixed, lse, stream, mlp_grad, act_grad, idc,
    w_output, merge_bias, gain, bias, w_up, up_bias, w_down, down_bias, w_head,
    predicted, act_ref, pre_ref, second_ref, mixed_low_ref, attn_low_ref, final_ref, attn_ref, grad_ref, unit_ref,
    stat_ref, up_sum, gain_sum, bias_sum, merge_sum,
):
    rows, width = mixed.shape
    hidden = w_up.shape[1]
    mixed_low = mixed[...].astype(BF16)
    mixed_low_ref[...] = mixed_low
    after = stream[...] + dot(mixed_low, w_output[...]) + merge_bias[...]
    unit_rows, scale = normalise(after)
    second = (unit_rows * gain[...] + bias[...]).astype(BF16)
    second_ref[...] = second
    out = after + down_bias[...]
    back = jnp.zeros((rows, width), F32)
    step = 768
    for start in range(0, hidden, step):
        part = slice(start, start + step)
        pre = dot(second, w_up[:, part]) + up_bias[:, part]
        cdf = 0.5 + 0.5 * erf(pre * 0.7071067811865476)
        act = (pre * cdf).astype(BF16)
        act_ref[:, part] = act
        slope = cdf + pre * (0.3989422804014327 * jnp.exp(-0.5 * pre * pre))
        grad = (act_grad[:, part] * slope).astype(BF16)
        pre_ref[:, part] = grad
        up_sum[:, part] = jnp.sum(grad.astype(F32), axis=0, keepdims=True)
        out += dot(act, w_down[part, :])
        back += dot_nt(grad, w_up[:, part])
    resid, gain_part, bias_part = norm_back(back, unit_rows, scale, gain[...])
    gain_sum[...] = gain_part
    bias_sum[...] = bias_part
    attn = mlp_grad[...] + resid
    attn_ref[...] = attn
    merge_sum[...] = jnp.sum(attn, axis=0, keepdims=True)
    attn_low = attn.astype(BF16)
    attn_low_ref[...] = attn_low
    grad = dot_nt(attn_low, w_output[...]).astype(BF16)
    grad_ref[...] = grad
    shared_row = idc[0:SHARED, :] == 0
    unit_ref[0:SHARED, :] = jnp.where(shared_row, grad[0:SHARED], jnp.zeros((SHARED, width), BF16))
    lane = lax.broadcasted_iota(jnp.int32, (MARKS, width), 1)
    head = lax.broadcasted_iota(jnp.int32, (MARKS, width), 0)
    ones = jnp.where(lane // HEAD_DIM == head, 1.0, 0.0)
    pick = jnp.where(lane == head * HEAD_DIM, 1.0, 0.0)
    delta = dot_nt(ones, grad.astype(F32) * mixed[...], lax.Precision.HIGHEST)
    turned = dot_nt(pick, lse[...], lax.Precision.HIGHEST)
    stat_ref[0] = turned
    stat_ref[1] = delta
    zeros = jnp.zeros((rows, 128), F32)
    ids = jnp.where(idc[...] == 0, 1.0, 0.0) + zeros
    row_ids = dot_nt(jnp.full((MARKS, 128), 1.0 / 128, F32), ids)
    shared_lane = row_ids[:, 0:SHARED] > 0.5
    sent = []
    for value, other in ((turned, -NEG), (delta, 0.0)):
        value = jnp.where(shared_lane, value[:, 0:SHARED], other)
        high = value.astype(BF16)
        sent += [high, (value - high.astype(F32)).astype(BF16)]
    unit_ref[SHARED:, :] = jnp.concatenate(sent, axis=1)
    final = out.astype(BF16)
    final_ref[...] = final
    predicted[...] = dot(final, w_head[...]).astype(BF16)


def query_kernel(n_blocks, n_kvs, key_rows, *refs):
    block_refs, kv_refs = refs[:n_blocks], refs[n_blocks : n_blocks + n_kvs]
    kvown_ref, q_ref, grad_ref, mixed_ref, lse_ref, wq_ref, bq_ref, idc_ref, idr_ref = refs[
        n_blocks + n_kvs : n_blocks + n_kvs + 9
    ]
    dq_ref, qall_ref = refs[-2:]
    own_rows = idc_ref.shape[0]
    flat = [(ref, i) for ref in block_refs for i in range(ref.shape[0])]
    base = 0
    for ref, index in flat:
        rows = (dot(ref[index, 0:SHARED, :], wq_ref[...]) + bq_ref[...]).astype(BF16)
        qall_ref[0, base : base + SHARED, :] = rows * BF16(SCALE)
        base += SHARED
    idc, idr = idc_ref[...], idr_ref[...]
    allowed = (idc == idr) & (idc != 0)
    shared_row = idc == 0
    q = q_ref[0]
    grad = grad_ref[...]
    product = grad.astype(F32) * mixed_ref[...]
    parts = []
    for kv_ref in kv_refs:
        count = kv_ref.shape[1] // key_rows
        parts += [(kv_ref, i, min(8, count - i)) for i in range(0, count, 8)]
    biases, used = [], 0
    for _, _, size in parts:
        biases += key_bias([flat[used : used + size]], key_rows)
        used += size
    outs = []
    for head in range(2):
        delta = jnp.sum(only_half(product, head), axis=1, keepdims=True)
        lse = lse_ref[:, head * HEAD_DIM : head * HEAD_DIM + 1]
        qm = only_half(q, head)
        gm = only_half(grad, head)
        total = None
        for (kv_ref, start, size), bias in zip(parts, biases):
            span = slice(start * key_rows, (start + size) * key_rows)
            keys = kv_ref[0, span, 0:PAIR]
            values = kv_ref[0, span, PAIR:]
            probs = jnp.exp(dot_nt(qm[0:SHARED], keys) + bias - lse[0:SHARED])
            dp = dot_nt(gm[0:SHARED], values)
            ds = (probs * (dp - delta[0:SHARED])).astype(BF16)
            part = dot(ds, keys)
            total = part if total is None else total + part
        keys, values = kvown_ref[0, 0:own_rows, 0:PAIR], kvown_ref[0, 0:own_rows, PAIR:]
        probs = jnp.exp(jnp.where(allowed, dot_nt(qm, keys) - lse, NEG))
        ds = (probs * (dot_nt(gm, values) - delta)).astype(BF16)
        local = dot(ds, keys)
        outs.append(
            jnp.concatenate([jnp.where(shared_row[0:SHARED], total, local[0:SHARED]), local[SHARED:]], axis=0)
        )
    dq_ref[...] = (merge_halves(*outs) * SCALE).astype(BF16)


def query_back(groups, kvs, kvown, q, mixed_grad, mixed, lse, w_project, project_bias, idc, idr, key_rows, first, pairs, after):
    own_rows = idc.shape[0]
    blocks = [b for group in groups for b in group]
    count = sum(b.shape[0] for b in blocks)
    ins = [fixed(b) for b in blocks] + [lead(kv, first) for kv in kvs] + [lead(kvown, first), lead(q, first)]
    ins += [lanes(x, first) for x in (mixed_grad, mixed, lse, w_project, project_bias)]
    ins += [fixed(idc), fixed(idr)]
    outs = [
        (sds((own_rows, pairs * PAIR), BF16), pl.BlockSpec((own_rows, PAIR), lambda h: (0, h))),
        (sds((pairs, count * SHARED, PAIR), BF16), pl.BlockSpec((1, count * SHARED, PAIR), lambda h: (h, 0, 0))),
    ]
    kernel = functools.partial(query_kernel, len(blocks), len(kvs), key_rows)
    return call(kernel, ins, outs, "query_back", grid=(pairs,), cost=4.0 * pairs, after=after)


def key_kernel(n_blocks, first, *refs):
    grad_refs, stat_refs = refs[:n_blocks], refs[n_blocks : 2 * n_blocks]
    kvown_ref, qall_ref, q_ref, grad_ref, own_stat_ref, idc_ref, idr_ref, live_ref = refs[2 * n_blocks : 2 * n_blocks + 8]
    dk_ref, dv_ref, grads_ref, stats_ref = refs[2 * n_blocks + 8 :]
    own_rows = idc_ref.shape[0]
    rim = kvown_ref.shape[1] - own_rows

    @pl.when(pl.program_id(0) == 0)
    def _():
        base = 0
        rows = [(ref, i) for ref in stat_refs for i in range(ref.shape[0])]
        for begin in range(0, len(rows), 2):
            sums = []
            for ref, i in rows[begin : begin + 2]:
                stat = ref[i].astype(F32)
                sums.append(
                    (
                        stat[:, 0:SHARED] + stat[:, SHARED : 2 * SHARED],
                        stat[:, 2 * SHARED : 3 * SHARED] + stat[:, 3 * SHARED :],
                    )
                )
            for kind in range(2):
                stats_ref[kind, :, base : base + 2 * SHARED] = jnp.concatenate([s[kind] for s in sums], axis=1)
            base += 2 * SHARED

    base = 0
    for ref in grad_refs:
        for i in range(ref.shape[0]):
            grads_ref[base : base + SHARED, :] = ref[i]
            base += SHARED
    idc, idr = idc_ref[...], idr_ref[...]
    allowed = (idc == idr) & (idc != 0)
    shared_row = idc == 0
    live = live_ref[0:1, 0:1] > 0.5
    kv = kvown_ref[0]
    k_all, v_all = kv[:, 0:PAIR], kv[:, PAIR:]
    k_sh = jnp.concatenate([k_all[0:SHARED], k_all[own_rows:]], axis=0)
    v_sh = jnp.concatenate([v_all[0:SHARED], v_all[own_rows:]], axis=0)
    q, grad = q_ref[0], grad_ref[...]
    dks, dvs = [], []
    chunk = min(base, 1536)
    for head in range(2):
        row = pl.ds(2 * (first + pl.program_id(0)) + head, 1)
        km, vm = only_half(k_sh, head), only_half(v_sh, head)
        dk = dv = None
        for start in range(0, base, chunk):
            q_all = qall_ref[0, start : start + chunk, :]
            g_all = grads_ref[start : start + chunk, :]
            lse = stats_ref[0, row, start : start + chunk]
            delta = stats_ref[1, row, start : start + chunk]
            probs = jnp.exp(dot_nt(km, q_all) - lse)
            part_v = dot(probs.astype(BF16), g_all)
            ds = (probs * (dot_nt(vm, g_all) - delta)).astype(BF16)
            part_k = dot(ds, q_all)
            dk = part_k if dk is None else dk + part_k
            dv = part_v if dv is None else dv + part_v
        lse = own_stat_ref[0, row, :]
        delta = own_stat_ref[1, row, :]
        probs = jnp.exp(jnp.where(allowed, dot_nt(only_half(k_all[0:own_rows], head), q) - lse, NEG))
        local_v = dot(probs.astype(BF16), grad)
        ds = (probs * (dot_nt(only_half(v_all[0:own_rows], head), grad) - delta)).astype(BF16)
        local_k = dot(ds, q)

        def rows(shared, local):
            return jnp.concatenate(
                [
                    jnp.where(shared_row[0:SHARED], shared[0:SHARED], local[0:SHARED]),
                    local[SHARED:],
                    jnp.where(live, shared[SHARED : SHARED + rim], 0.0),
                ],
                axis=0,
            )

        dks.append(rows(dk, local_k))
        dvs.append(rows(dv, local_v))
    dk_ref[...] = merge_halves(*dks).astype(BF16)
    dv_ref[...] = merge_halves(*dvs).astype(BF16)


def key_back(groups, kvown, qall, q, mixed_grad, own_stats, idc, idr, live, first, pairs, after):
    joined_rows, width = kvown.shape[1], mixed_grad.shape[1]
    grads = [g for group in groups for g in group]
    ins = [(g, pl.BlockSpec((g.shape[0], SHARED, PAIR), lambda h: (0, 0, first + h))) for g in grads]
    ins += [(g, pl.BlockSpec((g.shape[0], MARKS, width), lambda h: (0, SHARED // MARKS, 0))) for g in grads]
    ins += [lead(kvown, first), lead(qall), lead(q, first), lanes(mixed_grad, first)]
    ins += [fixed(own_stats), fixed(idc), fixed(idr), fixed(live)]
    out = (sds((joined_rows, pairs * PAIR), BF16), pl.BlockSpec((joined_rows, PAIR), lambda h: (0, h)))
    scratch = [pltpu.VMEM((qall.shape[1], PAIR), BF16), pltpu.VMEM((2, MARKS, qall.shape[1]), F32)]
    kernel = functools.partial(key_kernel, len(grads), first)
    return call(kernel, ins, [out, out], "key_back", grid=(pairs,), scratch=scratch, cost=3.0 * pairs, after=after)


def input_kernel(dq, dk, dv, weight, stream, arrived, gain, attn_grad, rim_ref, rows_ref, joint_ref, vec_ref):
    own, width = dq.shape
    dq, dk, dv = dq[...], dk[...], dv[...]
    wq, wk, wv = weight[:, 0:width], weight[:, width : 2 * width], weight[:, 2 * width :]
    rim_grad = dot_nt(dk[own:], wk) + dot_nt(dv[own:], wv)
    rim_rows, rim_scale = normalise(arrived[...].astype(F32))
    rim_back, rim_gain, rim_bias = norm_back(rim_grad, rim_rows, rim_scale, gain[...])
    rim_ref[...] = rim_back.astype(BF16)
    own_grad = dot_nt(dq, wq) + dot_nt(dk[:own], wk) + dot_nt(dv[:own], wv)
    own_rows, own_scale = normalise(stream[...])
    own_back, own_gain, own_bias = norm_back(own_grad, own_rows, own_scale, gain[...])
    rows_ref[...] = own_back + attn_grad[...]
    joint_ref[0:own, 0:width] = dq
    joint_ref[own:, 0:width] = jnp.zeros((dk.shape[0] - own, width), BF16)
    joint_ref[:, width : 2 * width] = dk
    joint_ref[:, 2 * width :] = dv
    vec_ref[0:1, :] = own_gain + rim_gain
    vec_ref[1:2, :] = own_bias + rim_bias
    vec_ref[2:3, :] = jnp.sum(dq.astype(F32), axis=0, keepdims=True)
    vec_ref[3:4, :] = jnp.sum(dv.astype(F32), axis=0, keepdims=True)


def pixel_kernel(rows, returned, halo, weight, low_ref, grad_ref):
    place = lax.broadcasted_iota(jnp.int32, (rows.shape[0], halo.shape[1]), 0)
    spread = jnp.where(place == halo[...], 1.0, 0.0).astype(BF16)
    low = (rows[...] + dot(spread, returned[...])).astype(BF16)
    low_ref[...] = low
    grad_ref[...] = dot_nt(low, weight[...]).astype(BF16)


def product_blocks(left, right, core_half, n):
    half = right.shape[1] // 2
    x = left[...]
    for j in range(half // LANES):
        columns = pl.ds(pl.multiple_of(core_half * half + j * LANES, 128), LANES)
        out = dot_tn(x, right[:, columns])
        yield out.reshape(n, out.shape[0] // n, LANES)


def away_kernel(n, n_pairs, *refs):
    pairs, outs = refs[: 2 * n_pairs], refs[2 * n_pairs :]
    other = 1 - lax.axis_index("gx") % 2
    (out,) = outs
    row = 0
    for p in range(n_pairs):
        for block in product_blocks(pairs[2 * p], pairs[2 * p + 1], other, n):
            out[:, row : row + block.shape[1], :] = block.astype(BF16)
            row += block.shape[1]


def home_kernel(n, n_pairs, x_first, n_small, *refs):
    pairs = refs[: 2 * n_pairs]
    arrived = refs[2 * n_pairs]
    small = refs[2 * n_pairs + 1 : 2 * n_pairs + 1 + n_small]
    send, keep = refs[2 * n_pairs + 1 + n_small :]
    core = lax.axis_index("gx") % 2
    bit = lax.axis_index("gx") // 2 if x_first else lax.axis_index("gy") % 2
    low = bit == 0
    row = half_row = 0

    def put(first, second, start, rows):
        if x_first:
            span = slice(start, start + rows)
            send[:, span, :] = jnp.where(low, second, first)
            keep[:, span, :] = jnp.where(low, first, second)
        else:
            for half, value in ((0, first), (1, second)):
                value = value.reshape(n // 2, 2, rows, LANES)
                send[:, half, start : start + rows, :] = jnp.where(low, value[:, 1], value[:, 0])
                keep[:, half, start : start + rows, :] = jnp.where(low, value[:, 0], value[:, 1])

    for p in range(n_pairs):
        for block in product_blocks(pairs[2 * p], pairs[2 * p + 1], core, n):
            r = block.shape[1]
            block = (block + arrived[:, row : row + r, :].astype(F32)).astype(BF16)
            put(block[:, : r // 2], block[:, r // 2 :], half_row, r // 2)
            row += r
            half_row += r // 2
    for ref in small:
        put(ref[...], jnp.zeros(ref.shape, BF16), half_row, ref.shape[1])
        half_row += ref.shape[1]


def away(pairs, n, name):
    arrays = [x for pair in pairs for x in pair]
    rows = sum(b.shape[1] // 2 // LANES * a.shape[1] // n for a, b in pairs)
    outs = [(sds((n, rows, LANES), BF16), VMEM)]
    return call(functools.partial(away_kernel, n, len(pairs)), plain(*arrays), outs, name, cost=3.0)[0]


def home(pairs, n, arrived, x_first, name, small=(), after=()):
    arrays = [x for pair in pairs for x in pair] + [arrived] + list(small)
    rows = arrived.shape[1] // 2 + sum(s.shape[1] for s in small)
    shape = (n, rows, LANES) if x_first else (n // 2, 2, rows, LANES)
    outs = [(sds(shape, BF16), VMEM)] * 2
    kernel = functools.partial(home_kernel, n, len(pairs), x_first, len(small))
    return call(kernel, plain(*arrays), outs, name, cost=3.0, after=after)


def next_step(keep, arrived, axis, bit, dim):
    mine = bit_of(axis, bit)
    pick = lambda x, i: lax.dynamic_index_in_dim(x, i, dim, keepdims=False)
    return pick(keep, 1 - mine) + pick(arrived, 1 - mine), pick(keep, mine) + pick(arrived, mine)


def steps_of(x_first):
    second = ("gy", 1, 2) if x_first else ("gx", 2, 2)
    return [second, ("gy", 2, 1), ("gy", 4, 0)]


def shards(
    pixels,
    frame_index,
    patch_cell,
    tile_id,
    halo_index,
    w_patch,
    first_gain,
    first_bias,
    w_project,
    project_bias,
    w_output,
    merge_bias,
    second_gain,
    second_bias,
    w_up,
    up_bias,
    w_down,
    down_bias,
    w_head,
    cotangent,
):
    n_gx, n_gy = lax.axis_size("gx"), lax.axis_size("gy")
    own, rim = pixels.shape[0], halo_index.shape[0]
    width, hidden, depth = w_output.shape[0], w_up.shape[1], pixels.shape[1]
    key_rows = SHARED + rim
    idc, idr = tile_id.reshape(own, 1), tile_id.reshape(1, own)
    live = jnp.broadcast_to(jnp.where(lax.axis_index("gx") > 0, 1.0, 0.0).astype(F32), (8, 128))
    halo = halo_index.reshape(1, rim)
    row = lambda v: v.reshape(1, -1)
    mat = lambda rows, columns, dtype: (sds((rows, columns), dtype), VMEM)

    high, low = position_table(width)
    stream, outgoing, own_low = call(
        embed_kernel,
        plain(
            pixels, w_patch, row(frame_index), patch_cell, halo, high, low, row(first_gain), row(first_bias)
        ),
        [mat(own, width, F32), mat(rim, width, BF16), mat(own, width, BF16)],
        "embed",
    )
    arrived = shifted(outgoing, "gx", 1)
    unit, first_low = call(
        unit_kernel,
        plain(own_low, arrived, row(first_gain), row(first_bias), idr, live),
        [mat(key_rows + MARKS, width, BF16), mat(own + rim, width, BF16)],
        "unit",
        cost=1.0,
    )
    groups = gather_column(unit)
    shift = row(project_bias)
    kvs, kvown, q, mixed, lse = attend(groups, first_low, w_project, shift, idc, idr, key_rows)

    mlp_grad = dot_nt(cotangent, w_head)
    down_bias_grad = jnp.sum(mlp_grad, axis=0)
    mlp_low = mlp_grad.astype(BF16)
    act_grad = dot_nt(mlp_low, w_down)
    (
        predicted, act_low, pre_grad, second_low, mixed_low, attn_low, final_low, attn_grad, mixed_grad, grad_unit,
        own_stats, up_sum, second_gain_sum, second_bias_sum, merge_sum,
    ) = call(
        middle_kernel,
        plain(
            mixed, lse, stream, mlp_grad, act_grad, idc, w_output, row(merge_bias), row(second_gain),
            row(second_bias), w_up, row(up_bias), w_down, row(down_bias), w_head,
        ),
        [mat(own, depth, BF16), mat(own, hidden, BF16), mat(own, hidden, BF16)]
        + [mat(own, width, BF16)] * 4
        + [mat(own, width, F32), mat(own, width, BF16), mat(SHARED + MARKS, width, BF16)]
        + [(sds((2, MARKS, own), F32), VMEM), mat(1, hidden, F32)]
        + [mat(1, width, F32)] * 3,
        "middle",
        cost=15.0,
    )
    special = n_gx == 4 and n_gy == 8
    head_pair, down_pair = (final_low, cotangent), (act_low, mlp_low)
    up_pair, output_pair = (second_low, pre_grad), (mixed_low, attn_low)
    grads = gather_column(grad_unit)
    sums, gone = {}, {}
    early = {"a": ([head_pair, down_pair], True), "b": ([up_pair, output_pair], False)}
    after = ()
    if special:
        shares = {k: away(pairs, n_gy, "away") for k, (pairs, _) in early.items()}
        gone = {k: swap(share, "gx", 1) for k, share in shares.items()}
        after = tuple(shares.values())
    q_parts, k_parts = [], []
    for place, first in enumerate((0, 2, 4)):
        q_parts.append(
            query_back(groups, kvs, kvown, q, mixed_grad, mixed, lse, w_project, shift, idc, idr, key_rows, first, 2, after)
        )
        after = (q_parts[-1][0],)
        if special and place == 0:
            for k, (pairs, x_first) in early.items():
                send, keep = home(pairs, n_gy, gone[k], x_first, "home", after=after)
                axis, bit = ("gx", 2) if x_first else ("gy", 1)
                sums[k] = (keep, swap(send, axis, bit))
                after += (send,)
    for place in range(3):
        k_parts.append(
            key_back(grads, kvown, q_parts[place][1], q, mixed_grad, own_stats, idc, idr, live, 2 * place, 2, after)
        )
        after = (k_parts[-1][0],)
    dq = jnp.concatenate([p[0] for p in q_parts], axis=1)
    dk = jnp.concatenate([p[0] for p in k_parts], axis=1)
    dv = jnp.concatenate([p[1] for p in k_parts], axis=1)
    rim_grad, partial, joint_grad, first_sums = call(
        input_kernel,
        plain(dq, dk, dv, w_project, stream, arrived, row(first_gain), attn_grad),
        [mat(rim, width, BF16), mat(own, width, F32), mat(own + rim, 3 * width, BF16), mat(8, width, F32)],
        "input",
        cost=6.0,
    )
    returned = shifted(rim_grad, "gx", -1)
    project_pair = (first_low, joint_grad)
    if special:
        gone["c"] = swap(away([project_pair], n_gy, "away"), "gx", 1)
    embed_low, pixel_grad = call(
        pixel_kernel,
        plain(partial, returned, halo, w_patch),
        [mat(own, width, BF16), mat(own, depth, BF16)],
        "pixel",
        cost=3.0,
    )
    patch_pair = (pixels, embed_low)

    vectors = [
        first_sums[0],
        first_sums[1],
        first_sums[2:4].reshape(-1),
        merge_sum[0],
        second_gain_sum[0],
        second_bias_sum[0],
        up_sum[0],
        down_bias_grad,
    ]
    sizes = [v.shape[0] // n_gy for v in vectors]
    flat = jnp.concatenate([v.reshape(n_gy, -1) for v in vectors], axis=1).astype(BF16)
    if special:
        core, x_bit = bit_of("gx", 1), bit_of("gx", 2)
        half = sum(sizes) // 2
        flat = flat.reshape(n_gy, 2, half)
        mine = lax.dynamic_index_in_dim(flat, core, 1, keepdims=False)
        other = lax.dynamic_index_in_dim(flat, 1 - core, 1, keepdims=False)
        small = mine + swap(other, "gx", 1)
        small = jnp.pad(small, ((0, 0), (0, MARKS * LANES - half))).reshape(n_gy, MARKS, LANES)
        gone["d"] = swap(away([patch_pair], n_gy, "away"), "gx", 1)
        send, keep = home([project_pair], n_gy, gone["c"], True, "home")
        sums["c"] = (keep, swap(send, "gx", 2))
        send, keep = home([patch_pair], n_gy, gone["d"], False, "home", small=[small])
        sums["d"] = (keep, swap(send, "gy", 1))
        orders = {"a": True, "b": False, "c": True, "d": False}
        for k, x_first in orders.items():
            keep, got = sums[k]
            lead_shape = (2, 2, 2) if x_first else (2, 2)
            tail_shape = keep.shape[1:] if x_first else keep.shape[1:]
            keep, got = keep.reshape(lead_shape + tail_shape), got.reshape(lead_shape + tail_shape)
            for axis, bit, dim in steps_of(x_first):
                send, keep = next_step(keep, got, axis, bit, dim)
                got = swap(send, axis, bit)
            part = keep + got
            over = swap(part, "gx", 2)
            both = jnp.stack([jnp.where(x_bit == 0, part, over), jnp.where(x_bit == 0, over, part)])
            across = swap(both, "gx", 1)
            sums[k] = [jnp.where(core == 0, both, across), jnp.where(core == 0, across, both)]

        def cut(key, pairs):
            outs, start = [], 0
            for a, b in pairs:
                r, blocks = a.shape[1] // n_gy, b.shape[1] // 2 // LANES
                halves = []
                for side in sums[key]:
                    piece = side[:, start : start + blocks * r // 2].reshape(2, blocks, r // 2, LANES)
                    halves.append(piece.transpose(0, 2, 1, 3).reshape(r, blocks * LANES))
                start += blocks * r // 2
                outs.append(jnp.concatenate(halves, axis=1).astype(F32))
            return outs, start

        (head_grad, down_grad), _ = cut("a", early["a"][0])
        (up_grad, output_grad), _ = cut("b", early["b"][0])
        (project_grad,), _ = cut("c", [project_pair])
        (patch_grad,), start = cut("d", [patch_pair])
        tail = [side[0, start:].reshape(-1)[:half] for side in sums["d"]]
        tail = jnp.concatenate(tail).astype(F32)
    else:

        def total(x):
            part = lax.psum_scatter(x.astype(BF16), "gy", scatter_dimension=0, tiled=True)
            return lax.psum(part, "gx").astype(F32)

        pairs = [head_pair, down_pair, up_pair, output_pair, project_pair, patch_pair]
        head_grad, down_grad, up_grad, output_grad, project_grad, patch_grad = [total(dot_tn(a, b)) for a, b in pairs]
        tail = total(flat).reshape(-1)
    starts = [sum(sizes[:i]) for i in range(len(sizes))]
    small_outs = [tail[s : s + z] for s, z in zip(starts, sizes)]
    return (
        predicted,
        pixel_grad,
        patch_grad,
        small_outs[0],
        small_outs[1],
        project_grad,
        small_outs[2],
        output_grad,
        small_outs[3],
        small_outs[4],
        small_outs[5],
        up_grad,
        small_outs[6],
        down_grad,
        small_outs[7],
        head_grad,
    )


def solution(mesh):
    tokens = P(("gx", "gy"))
    rows = P(("gx", "gy"), None)
    in_specs = (rows, tokens, P(None, ("gx", "gy")), tokens, tokens) + (P(),) * 14 + (rows,)
    matrix, vector = P("gy", None), P("gy")
    out_specs = (
        rows,
        rows,
        matrix,
        vector,
        vector,
        matrix,
        vector,
        matrix,
        vector,
        vector,
        vector,
        matrix,
        vector,
        matrix,
        vector,
        matrix,
    )
    return jax.shard_map(shards, mesh=mesh, in_specs=in_specs, out_specs=out_specs, check_vma=False)
```

time: 513 us -> 381 us (0.74)
  Pallas kernels: 75.1 us -> 168 us
  waiting for transfers between devices: 159 us -> 93.2 us
  local copies, waits for them, and re-layouts: 81.8 us -> 16.4 us
  matrix products: 65.7 us -> 6.1 us
  other arithmetic: 51.2 us -> 26.7 us
  starting transfers between devices: 69.8 us -> 60.9 us
    pallas_call x3 -> x22, Pallas kernels: 75.1 us -> 168 us  [call(): pl.pallas_call(body, grid=grid or (), in_specs=specs, out_specs=tuple((sp...]
    ppermute x39 -> x37, waiting for transfers between devices: 116 us -> 55.2 us  [swap(): return lax.ppermute(x, axis, [(i, i ^ bit) for i in range(length)])]
    dot_general x24 -> x2, matrix products: 65.7 us -> 6.1 us  [dot_nt(): lax.dot_general(a, b, (((1,), (1,)), ((), ())), preferred_element_type=F3...]
    ppermute x10, starting transfers between devices: 30.1 us -> 12.1 us  [along(): return lax.ppermute(x, 'gy', pairs)]
    slice x26 -> x16, local copies, waits for them, and re-layouts: 15.5 us -> 0.26 us  [the longest x10 0.21 us: cut(): side[:, start:start + blocks * r // 2].reshape(2, blocks, r // 2, LANES)]
    reshape x18 -> x12, local copies, waits for them, and re-layouts: 19 us -> 6.72 us  [the longest x7 5.46 us: shards(): row = lambda v: v.reshape(1, -1)]
    concatenate x19 -> x2, other arithmetic: 14.2 us -> 3.81 us  [the longest x1 2.11 us: shards(): dk = jnp.concatenate([p[0] for p in k_parts], axis=1)]
    ppermute x39 -> x37, starting transfers between devices: 35.9 us -> 45.2 us  [swap(): return lax.ppermute(x, axis, [(i, i ^ bit) for i in range(length)])]
  transfers between devices with their start and end apart: 51 -> 49, of which waited for: 20 -> 22; matrix products, arithmetic and copies ran while one was open for 29% -> 9% of each run, Pallas kernels for 9% -> 26%
where the time goes in v2:
time: 381 us; the launch traced here: 374 us
  Pallas kernels  168 us (44%)
  waiting for transfers between devices  93.2 us (24%)
  starting transfers between devices  60.9 us (16%)
  other arithmetic  26.7 us (7%)
  local copies, waits for them, and re-layouts  16.4 us (4%)
  matrix products  6.1 us (2%)
    pallas_call x22, Pallas kernels, call(): pl.pallas_call(body, grid=grid or (), in_specs=specs, out_specs=tuple((sp...  168 us
    ppermute x37, waiting for transfers between devices, swap(): return lax.ppermute(x, axis, [(i, i ^ bit) for i in range(length)])  55.2 us
    ppermute x37, starting transfers between devices, swap(): return lax.ppermute(x, axis, [(i, i ^ bit) for i in range(length)])  45.2 us
    ppermute x10, waiting for transfers between devices, along(): return lax.ppermute(x, 'gy', pairs)  36.8 us
    add x8, other arithmetic, next_step(): pick(keep, mine) + pick(arrived, mine)  13.2 us
    ppermute x10, starting transfers between devices, along(): return lax.ppermute(x, 'gy', pairs)  12.1 us
    unnamed x102, local copies, waits for them, and re-layouts  7.65 us
  transfers between devices with their start and end apart: 49, of which 22 were waited for; matrix products, arithmetic and copies ran while one was open for 9% of the time, Pallas kernels for 26%

profile of v2, /device:TPU:0, one launch (start us, length us, event | category | flops | bytes accessed | tf_op | source)
XLA Modules:
  0.0 373.7 jit_solution(16675126762111942229)
XLA Ops:
  3.2 4.3 %embed.1 = (f32[256,768]{1,0:T(8,128)}, bf16[128,768]{1,0:T(8,128)(2,1)}, bf16[256,768]{1,0:T(8,128)(2,1)}) custom-call(bf16[256,1536]{1,0:T(8,128)(2,1)} %refs_0_.5, bf16[1536,768]{1,0:T(8,128)(2,1)} %refs_3_.11, s32[1,256]{1,0:T(1,128)} %bitcast.310, s32[2,256]{1,0:T(2,128)} %refs_3_.6, s32[1,128]{1,0:T(1,128)} %bitcast.308, ...), custom_call_target="tpu_custom_call" | custom-call | flops 400000000 | bytes 1200000 | tf_op jit(solution)/shard_map/embed/pallas_call | solution.py:98
  7.5 2.4 collective-permute-start
  11.8 2.4 unit.1
  14.1 2.4 collective-permute-start.3
  17.2 9.2 %collective-permute-done.3 = bf16[336,768]{1,0:T(8,128)(2,1)S(1)} collective-permute-done((bf16[336,768]{1,0:T(8,128)(2,1)}, bf16[336,768]{1,0:T(8,128)(2,1)S(1)}, u32[]{:S(2)}, u32[]{:S(2)}) %collective-permute-start.3) | collective-permute-done | bytes 516128 | tf_op jit(solution)/shard_map/ppermute | solution.py:64
  34.4 3.0 fusion.11
  37.4 2.3 collective-permute-start.8
  39.8 4.8 %collective-permute-done.2 = bf16[336,768]{1,0:T(8,128)(2,1)} collective-permute-done((bf16[336,768]{1,0:T(8,128)(2,1)S(1)}, bf16[336,768]{1,0:T(8,128)(2,1)}, u32[]{:S(2)}, u32[]{:S(2)}) %collective-permute-start.2) | collective-permute-done | bytes 516128 | tf_op jit(solution)/shard_map/ppermute | solution.py:64
  45.7 1.6 collective-permute-start.5
  47.3 10.0 %collective-permute-done.6 = bf16[336,768]{1,0:T(8,128)(2,1)S(1)} collective-permute-done((bf16[336,768]{1,0:T(8,128)(2,1)}, bf16[336,768]{1,0:T(8,128)(2,1)S(1)}, u32[]{:S(2)}, u32[]{:S(2)}) %collective-permute-start.6) | collective-permute-done | bytes 516128 | tf_op jit(solution)/shard_map/ppermute | solution.py:64
  57.3 1.6 collective-permute-start.7
  58.9 3.1 fusion.12.refs_4_
  62.9 15.9 %attend.3 = (bf16[6,960,256]{2,1,0:T(8,128)(2,1)}, bf16[6,256,128]{2,1,0:T(8,128)(2,1)}, bf16[6,384,256]{2,1,0:T(8,128)(2,1)}, f32[256,768]{1,0:T(8,128)}, f32[2...) custom-call(bf16[1,336,768]{2,1,0:T(8,128)(2,1)} %bitcast.242, ...), custom_call_target="tpu_custom_call" | custom-call | flops 600000000 | bytes 1800000 | tf_op jit(solution)/shard_map/attend/pallas_call | solution.py:98
  79.6 14.7 %attend.4 = (bf16[6,960,256]{2,1,0:T(8,128)(2,1)}, f32[192,768]{1,0:T(8,128)}, f32[192,768]{1,0:T(8,128)}, f32[192,768]{1,0:T(8,128)}) custom-call(bf16[1,336,768]{2,1,0:T(8,128)(2,1)} %bitcast.254, bf16[1,336,768]{2,1,0:T(8,128)(2,1)} %bitcast.198, bf16[1,336,768]{2,1,0:T(8,128)(2,1)} %bitcast.202, bf16[768,2304]{1,0:T(8,128)(2,1)} %refs_3_.10, ...), custom_call_target="tpu_custom_call" | custom-call | flops 600000000 | bytes 1800000 | tf_op jit(solution)/shard_map/attend/pallas_call | solution.py:98
  95.4 12.2 %attend.5 = (bf16[6,640,256]{2,1,0:T(8,128)(2,1)}, f32[256,768]{1,0:T(8,128)}, f32[256,768]{1,0:T(8,128)}) custom-call(bf16[1,336,768]{2,1,0:T(8,128)(2,1)} %bitcast.258, bf16[1,336,768]{2,1,0:T(8,128)(2,1)} %bitcast.262, bf16[768,2304]{1,0:T(8,128)(2,1)} %refs_3_.10, bf16[768,2304]{1,0:T(8,128)(2,1)} %refs_3_.10, ...), custom_call_target="tpu_custom_call" | custom-call | flops 400000000 | bytes 1200000 | tf_op jit(solution)/shard_map/attend/pallas_call | solution.py:98
  107.6 18.0 %middle.1 = (bf16[256,1536]{1,0:T(8,128)(2,1)}, bf16[256,3072]{1,0:T(8,128)(2,1)}, bf16[256,3072]{1,0:T(8,128)(2,1)}, bf16[256,768]{1,0:T(8,128)(2,1)}, bf16[256...) custom-call(f32[256,768]{1,0:T(8,128)} %get-tuple-element.90.refs_0_, ...), custom_call_target="tpu_custom_call" | custom-call | flops 1500000000 | bytes 4500000 | tf_op jit(solution)/shard_map/middle/pallas_call | solution.py:98
  125.6 5.0 %away.4.refs_20_ = bf16[8,576,384]{2,1,0:T(8,128)(2,1)} custom-call(bf16[256,768]{1,0:T(8,128)(2,1)} %get-tuple-element.99.refs_0_, bf16[256,1536]{1,0:T(8,128)(2,1)} %refs_1_.5, bf16[256,3072]{1,0:T(8,128)(2,1)} %get-tuple-element.100.refs_2_, bf16[256,768]{1,0:T(8,128)(2,1)} %copy-done.19), custom_call_target="tpu_custom_call" | custom-call | flops 300000000 | bytes 900000 | tf_op jit(solution)/shard_map/away/pallas_call | solution.py:98
  131.2 4.7 %away.5.refs_21_ = bf16[8,480,384]{2,1,0:T(8,128)(2,1)} custom-call(bf16[256,768]{1,0:T(8,128)(2,1)} %get-tuple-element.101.refs_0_, bf16[256,3072]{1,0:T(8,128)(2,1)} %get-tuple-element.102.refs_1_, bf16[256,768]{1,0:T(8,128)(2,1)} %get-tuple-element.103.refs_2_, bf16[256,768]{1,0:T(8,128)(2,1)} %get-tuple-element.104.refs_3_), custom_call_target="tpu_custom_call" | custom-call | flops 300000000 | bytes 900000 | tf_op jit(solution)/shard_map/away/pallas_call | solution.py:98
  137.7 8.3 %collective-permute-done.12 = bf16[208,768]{1,0:T(8,128)(2,1)S(1)} collective-permute-done((bf16[208,768]{1,0:T(8,128)(2,1)S(1)}, bf16[208,768]{1,0:T(8,128)(2,1)S(1)}, u32[]{:S(2)}, u32[]{:S(2)}) %collective-permute-start.12) | collective-permute-done | bytes 319520 | tf_op jit(solution)/shard_map/ppermute | solution.py:64
  149.9 10.1 %query_back.3 = (bf16[256,256]{1,0:T(8,128)(2,1)}, bf16[2,1536,128]{2,1,0:T(8,128)(2,1)}) custom-call(bf16[1,336,768]{2,1,0:T(8,128)(2,1)} %bitcast.243, bf16[1,336,768]{2,1,0:T(8,128)(2,1)} %bitcast.247, bf16[1,336,768]{2,1,0:T(8,128)(2,1)} %bitcast.251, bf16[1,336,768]{2,1,0:T(8,128)(2,1)} %bitcast.255, bf16[1,336,768]{2,1,0:T(8,128)(2,1)} %bitcast.199, ...), custom_call_target="tpu_custom_call" | custom-call | flops 800000000 | bytes 2400000 | tf_op jit(solution)/shard_map/query_back/pallas_call | solution.py:98
  160.0 1.5 collective-permute-start.14
  161.6 4.5 %collective-permute-done.18 = bf16[208,768]{1,0:T(8,128)(2,1)S(1)} collective-permute-done((bf16[208,768]{1,0:T(8,128)(2,1)S(1)}, bf16[208,768]{1,0:T(8,128)(2,1)S(1)}, u32[]{:S(2)}, u32[]{:S(2)}) %collective-permute-start.18) | collective-permute-done | bytes 319520 | tf_op jit(solution)/shard_map/ppermute | solution.py:64
  166.1 1.5 collective-permute-start.19
  169.5 6.2 %home.4 = (bf16[8,288,384]{2,1,0:T(8,128)(2,1)}, bf16[8,288,384]{2,1,0:T(8,128)(2,1)}) custom-call(bf16[256,768]{1,0:T(8,128)(2,1)} %get-tuple-element.99.refs_0_, bf16[256,1536]{1,0:T(8,128)(2,1)} %refs_1_.5, bf16[256,3072]{1,0:T(8,128)(2,1)} %get-tuple-element.100.refs_2_, bf16[256,768]{1,0:T(8,128)(2,1)} %copy-done.19, bf16[8,576,384]{2,1,0:T(8,128)(2,1)} %copy-done.20, ...), custom_call_target="tpu_custom_call" | custom-call | flops 300000000 | bytes 900000 | tf_op jit(solution)/shard_map/home/pallas_call | solution.py:98
  175.7 5.5 %home.5 = (bf16[4,2,240,384]{3,2,1,0:T(8,128)(2,1)}, bf16[4,2,240,384]{3,2,1,0:T(8,128)(2,1)}) custom-call(bf16[256,768]{1,0:T(8,128)(2,1)} %get-tuple-element.101.refs_0_, bf16[256,3072]{1,0:T(8,128)(2,1)} %get-tuple-element.102.refs_1_, bf16[256,768]{1,0:T(8,128)(2,1)} %get-tuple-element.103.refs_2_, bf16[256,768]{1,0:T(8,128)(2,1)} %get-tuple-element.104.refs_3_, ...), custom_call_target="tpu_custom_call" | custom-call | flops 300000000 | bytes 900000 | tf_op jit(solution)/shard_map/home/pallas_call | solution.py:98
  181.2 10.0 %query_back.4 = (bf16[256,256]{1,0:T(8,128)(2,1)}, bf16[2,1536,128]{2,1,0:T(8,128)(2,1)}) custom-call(bf16[1,336,768]{2,1,0:T(8,128)(2,1)} %bitcast.244, bf16[1,336,768]{2,1,0:T(8,128)(2,1)} %bitcast.248, bf16[1,336,768]{2,1,0:T(8,128)(2,1)} %bitcast.252, bf16[1,336,768]{2,1,0:T(8,128)(2,1)} %bitcast.256, bf16[1,336,768]{2,1,0:T(8,128)(2,1)} %bitcast.200, ...), custom_call_target="tpu_custom_call" | custom-call | flops 800000000 | bytes 2400000 | tf_op jit(solution)/shard_map/query_back/pallas_call | solution.py:98
  191.3 10.3 %query_back.5 = (bf16[256,256]{1,0:T(8,128)(2,1)}, bf16[2,1536,128]{2,1,0:T(8,128)(2,1)}) custom-call(bf16[1,336,768]{2,1,0:T(8,128)(2,1)} %bitcast.245, bf16[1,336,768]{2,1,0:T(8,128)(2,1)} %bitcast.249, bf16[1,336,768]{2,1,0:T(8,128)(2,1)} %bitcast.253, bf16[1,336,768]{2,1,0:T(8,128)(2,1)} %bitcast.257, bf16[1,336,768]{2,1,0:T(8,128)(2,1)} %bitcast.201, ...), custom_call_target="tpu_custom_call" | custom-call | flops 800000000 | bytes 2400000 | tf_op jit(solution)/shard_map/query_back/pallas_call | solution.py:98
  201.6 1.7 pad_maximum_fusion.3.refs_0_
  204.3 7.7 %key_back.3 = (bf16[384,256]{1,0:T(8,128)(2,1)}, bf16[384,256]{1,0:T(8,128)(2,1)}) custom-call(bf16[1,208,768]{2,1,0:T(8,128)(2,1)} %bitcast.206, bf16[1,208,768]{2,1,0:T(8,128)(2,1)} %bitcast.212, bf16[1,208,768]{2,1,0:T(8,128)(2,1)} %bitcast.218, bf16[1,208,768]{2,1,0:T(8,128)(2,1)} %bitcast.224, bf16[1,208,768]{2,1,0:T(8,128)(2,1)} %bitcast.186, ...), custom_call_target="tpu_custom_call" | custom-call | flops 600000000 | bytes 1800000 | tf_op jit(solution)/shard_map/key_back/pallas_call | solution.py:98
  212.0 7.6 %key_back.4 = (bf16[384,256]{1,0:T(8,128)(2,1)}, bf16[384,256]{1,0:T(8,128)(2,1)}) custom-call(bf16[1,208,768]{2,1,0:T(8,128)(2,1)} %bitcast.208, bf16[1,208,768]{2,1,0:T(8,128)(2,1)} %bitcast.214, bf16[1,208,768]{2,1,0:T(8,128)(2,1)} %bitcast.220, bf16[1,208,768]{2,1,0:T(8,128)(2,1)} %bitcast.226, bf16[1,208,768]{2,1,0:T(8,128)(2,1)} %bitcast.188, ...), custom_call_target="tpu_custom_call" | custom-call | flops 600000000 | bytes 1800000 | tf_op jit(solution)/shard_map/key_back/pallas_call | solution.py:98
  219.7 8.0 %key_back.5 = (bf16[384,256]{1,0:T(8,128)(2,1)}, bf16[384,256]{1,0:T(8,128)(2,1)}) custom-call(bf16[1,208,768]{2,1,0:T(8,128)(2,1)} %bitcast.210, bf16[1,208,768]{2,1,0:T(8,128)(2,1)} %bitcast.216, bf16[1,208,768]{2,1,0:T(8,128)(2,1)} %bitcast.222, bf16[1,208,768]{2,1,0:T(8,128)(2,1)} %bitcast.228, bf16[1,208,768]{2,1,0:T(8,128)(2,1)} %bitcast.190, ...), custom_call_target="tpu_custom_call" | custom-call | flops 600000000 | bytes 1800000 | tf_op jit(solution)/shard_map/key_back/pallas_call | solution.py:98
  227.7 2.1 pad_maximum_fusion
  229.8 6.7 %input.1 = (bf16[128,768]{1,0:T(8,128)(2,1)}, f32[256,768]{1,0:T(8,128)}, bf16[384,2304]{1,0:T(8,128)(2,1)}, f32[8,768]{1,0:T(8,128)}) custom-call(bf16[256,768]{1,0:T(8,128)(2,1)} %pad_maximum_fusion.3.refs_0_, bf16[384,768]{1,0:T(8,128)(2,1)} %get-tuple-element.186.refs_1_, bf16[384,768]{1,0:T(8,128)(2,1)} %get-tuple-element.187.refs_2_, ...), custom_call_target="tpu_custom_call" | custom-call | flops 600000000 | bytes 1800000 | tf_op jit(solution)/shard_map/input/pallas_call | solution.py:98
  238.3 1.9 collective-permute-start.43
  240.9 3.8 %pixel.1 = (bf16[256,768]{1,0:T(8,128)(2,1)}, bf16[256,1536]{1,0:T(8,128)(2,1)}) custom-call(f32[256,768]{1,0:T(8,128)} %get-tuple-element.122.refs_0_, bf16[128,768]{1,0:T(8,128)(2,1)} %copy-done.33, s32[1,128]{1,0:T(1,128)} %bitcast.309, bf16[1536,768]{1,0:T(8,128)(2,1)} %refs_3_.11), custom_call_target="tpu_custom_call" | custom-call | flops 300000000 | bytes 900000 | tf_op jit(solution)/shard_map/pixel/pallas_call | solution.py:98
  244.7 2.8 away.6
  247.5 5.1 %collective-permute-start.22 = (bf16[8,192,384]{2,1,0:T(8,128)(2,1)}, bf16[8,192,384]{2,1,0:T(8,128)(2,1)}, u32[]{:S(2)}, u32[]{:S(2)}) collective-permute-start(bf16[8,192,384]{2,1,0:T(8,128)(2,1)} %away.6), channel_id=1, source_target_pairs={{0,8},{8,0},{16,24},{24,16},{1,9},{9,1},{17,25},{25,17},{2,10},{10... | collective-permute-start | bytes 3538952 | tf_op jit(solution)/shard_map/ppermute | solution.py:51
  252.7 4.2 %away.7 = bf16[8,288,384]{2,1,0:T(8,128)(2,1)} custom-call(bf16[384,768]{1,0:T(8,128)(2,1)} %get-tuple-element.80.refs_6_.refs_0_, bf16[384,2304]{1,0:T(8,128)(2,1)} %get-tuple-element.133.refs_1_), custom_call_target="tpu_custom_call" | custom-call | flops 300000000 | bytes 900000 | tf_op jit(solution)/shard_map/away/pallas_call | solution.py:98
  258.6 2.1 collective-permute-done.23
  261.3 3.3 home.6
  264.6 8.4 %collective-permute-done.37 = bf16[4,2,240,384]{3,2,1,0:T(8,128)(2,1)S(1)} collective-permute-done((bf16[4,2,240,384]{3,2,1,0:T(8,128)(2,1)}, bf16[4,2,240,384]{3,2,1,0:T(8,128)(2,1)S(1)}, u32[]{:S(2)}, u32[]{:S(2)}) %collective-permute-start.37) | collective-permute-done | bytes 1474592 | tf_op jit(solution)/shard_map/ppermute | solution.py:51
  274.2 2.8 dynamic-slice_add_fusion.1
  277.0 2.0 collective-permute-start.38
  278.9 3.6 collective-permute-done.43
  282.5 3.1 dynamic-slice_add_fusion
  285.8 2.1 collective-permute-done.24
  287.9 1.9 dynamic-slice_add_fusion.3
  289.8 1.9 collective-permute-start.25
  291.8 4.7 %home.7 = (bf16[8,144,384]{2,1,0:T(8,128)(2,1)}, bf16[8,144,384]{2,1,0:T(8,128)(2,1)}) custom-call(bf16[384,768]{1,0:T(8,128)(2,1)} %get-tuple-element.80.refs_6_.refs_0_, bf16[384,2304]{1,0:T(8,128)(2,1)} %get-tuple-element.133.refs_1_, bf16[8,288,384]{2,1,0:T(8,128)(2,1)} %collective-permute-done.30.refs_2_), custom_call_target="tpu_custom_call" | custom-call | flops 300000000 | bytes 900000 | tf_op jit(solution)/shard_map/home/pallas_call | solution.py:98
  296.6 1.7 collective-permute-done.38
  298.3 1.9 bitcast_add_fusion.3
  300.2 3.8 %collective-permute-start.39 = (bf16[2,240,384]{2,1,0:T(8,128)(2,1)}, bf16[2,240,384]{2,1,0:T(8,128)(2,1)S(1)}, u32[]{:S(2)}, u32[]{:S(2)}) collective-permute-start(bf16[2,240,384]{2,1,0:T(8,128)(2,1)} %get-tuple-element.147), channel_id=1, source_target_pairs={{0,2},{1,3},{2,0},{3,1},{4,6},{5,7},{6,4},{7,5},{8,10},{9,11},{10,... | collective-permute-start | bytes 1105928 | tf_op jit(solution)/shard_map/ppermute | solution.py:51
  304.1 1.6 collective-permute-done.25
  306.7 3.9 %collective-permute-start.26 = (bf16[2,112,384]{2,1,0:T(8,128)(2,1)S(1)}, bf16[2,112,384]{2,1,0:T(8,128)(2,1)S(1)}, u32[]{:S(2)}, u32[]{:S(2)}) collective-permute-start(bf16[2,112,384]{2,1,0:T(8,128)(2,1)S(1)} %get-tuple-element.162), channel_id=1, source_target_pairs={{0,2},{1,3},{2,0},{3,1},{4,6},{5,7},{6,4},{7,5},{8,10},{9,11},{10,... | collective-permute-start | bytes 516104 | tf_op jit(solution)/shard_map/ppermute | solution.py:51
  310.7 5.0 %collective-permute-done.26 = bf16[2,112,384]{2,1,0:T(8,128)(2,1)S(1)} collective-permute-done((bf16[2,112,384]{2,1,0:T(8,128)(2,1)S(1)}, bf16[2,112,384]{2,1,0:T(8,128)(2,1)S(1)}, u32[]{:S(2)}, u32[]{:S(2)}) %collective-permute-start.26) | collective-permute-done | bytes 172064 | tf_op jit(solution)/shard_map/ppermute | solution.py:51
  315.7 3.0 collective-permute-start.27
  319.7 1.7 collective-permute-start.45
  321.4 2.2 collective-permute-done.31
  328.0 2.7 collective-permute-done.28
  333.7 4.4 %collective-permute-done.41 = bf16[240,384]{1,0:T(8,128)(2,1)S(1)} collective-permute-done((bf16[240,384]{1,0:T(8,128)(2,1)S(1)}, bf16[240,384]{1,0:T(8,128)(2,1)S(1)}, u32[]{:S(2)}, u32[]{:S(2)}) %collective-permute-start.41) | collective-permute-done | bytes 184352 | tf_op jit(solution)/shard_map/ppermute | solution.py:51
  339.8 4.3 %collective-permute-start.46 = (bf16[288,384]{1,0:T(8,128)(2,1)S(1)}, bf16[288,384]{1,0:T(8,128)(2,1)S(1)}, u32[]{:S(2)}, u32[]{:S(2)}) collective-permute-start(bf16[288,384]{1,0:T(8,128)(2,1)S(1)} %fusion.3), channel_id=1, source_target_pairs={{0,4},{1,5},{2,6},{3,7},{4,0},{5,1},{6,2},{7,3},{8,12},{9,13},{10,... | collective-permute-start | bytes 663560 | tf_op jit(solution)/shard_map/ppermute | solution.py:51
  344.8 10.7 %collective-permute-done.33 = bf16[2,144,384]{2,1,0:T(8,128)(2,1)S(1)} collective-permute-done((bf16[2,144,384]{2,1,0:T(8,128)(2,1)S(1)}, bf16[2,144,384]{2,1,0:T(8,128)(2,1)S(1)}, u32[]{:S(2)}, u32[]{:S(2)}) %collective-permute-start.33) | collective-permute-done | bytes 221216 | tf_op jit(solution)/shard_map/ppermute | solution.py:51
  358.4 4.6 %collective-permute-done.34 = bf16[144,384]{1,0:T(8,128)(2,1)S(1)} collective-permute-done((bf16[144,384]{1,0:T(8,128)(2,1)S(1)}, bf16[144,384]{1,0:T(8,128)(2,1)S(1)}, u32[]{:S(2)}, u32[]{:S(2)}) %collective-permute-start.34) | collective-permute-done | bytes 110624 | tf_op jit(solution)/shard_map/ppermute | solution.py:51
  364.4 3.4 collective-permute-done.35
  (254 shorter events, 53.4 us)
Async XLA Ops:
  3.2 26.1 %copy-start.36 = (s32[256]{0:T(256)S(1)}, s32[256]{0:T(256)}, u32[]{:S(2)}) copy-start(s32[256]{0:T(256)} %param.25) | copy-start | bytes 3076
  3.2 26.9 %copy-start.39 = (f32[1536]{0:T(1024)S(1)}, f32[1536]{0:T(1024)}, u32[]{:S(2)}) copy-start(f32[1536]{0:T(1024)} %param.31) | copy-start | bytes 18436
  3.2 27.5 %copy-start.40 = (f32[768]{0:T(1024)S(1)}, f32[768]{0:T(1024)}, u32[]{:S(2)}) copy-start(f32[768]{0:T(1024)} %param.33) | copy-start | bytes 9220
  3.2 28.1 %copy-start.41 = (f32[768]{0:T(1024)S(1)}, f32[768]{0:T(1024)}, u32[]{:S(2)}) copy-start(f32[768]{0:T(1024)} %param.34) | copy-start | bytes 9220
  3.2 28.6 %copy-start.42 = (f32[768]{0:T(1024)S(1)}, f32[768]{0:T(1024)}, u32[]{:S(2)}) copy-start(f32[768]{0:T(1024)} %param.35) | copy-start | bytes 9220
  3.2 29.2 %copy-start.43 = (f32[768]{0:T(1024)S(1)}, f32[768]{0:T(1024)}, u32[]{:S(2)}) copy-start(f32[768]{0:T(1024)} %param.39) | copy-start | bytes 9220
  3.2 31.2 %copy-start.11 = (bf16[768,1536]{1,0:T(8,128)(2,1)S(1)}, bf16[768,1536]{1,0:T(8,128)(2,1)}, u32[]{:S(2)}) copy-start(bf16[768,1536]{1,0:T(8,128)(2,1)} %refs_14_.1) | copy-start | bytes 7077892
  7.5 3.6 collective-permute-start
  14.1 12.3 %collective-permute-start.3 = (bf16[336,768]{1,0:T(8,128)(2,1)}, bf16[336,768]{1,0:T(8,128)(2,1)S(1)}, u32[]{:S(2)}, u32[]{:S(2)}) collective-permute-start(bf16[336,768]{1,0:T(8,128)(2,1)} %get-tuple-element.79), channel_id=1, source_target_pairs={{0,2},{1,3},{2,0},{3,1},{4,6},{5,7},{6,4},{7,5},{8,10},{9,11},{10,... | collective-permute-start | bytes 1548296 | tf_op jit(solution)/shard_map/ppermute | solution.py:64
  16.6 11.4 %collective-permute-start.1 = (bf16[336,768]{1,0:T(8,128)(2,1)}, bf16[336,768]{1,0:T(8,128)(2,1)S(1)}, u32[]{:S(2)}, u32[]{:S(2)}) collective-permute-start(bf16[336,768]{1,0:T(8,128)(2,1)} %get-tuple-element.79), channel_id=1, source_target_pairs={{2,4},{3,5},{4,2},{5,3},{10,12},{11,13},{12,10},{13,11},{18,20},{1... | collective-permute-start | bytes 1548296 | tf_op jit(solution)/shard_map/ppermute | solution.py:64
  26.5 13.3 %copy-start.13 = (bf16[336,768]{1,0:T(8,128)(2,1)}, bf16[336,768]{1,0:T(8,128)(2,1)S(1)}, u32[]{:S(2)}) copy-start(bf16[336,768]{1,0:T(8,128)(2,1)S(1)} %collective-permute-done.3) | copy-start | bytes 1548292
  26.5 6.5 %collective-permute-start.4 = (bf16[336,768]{1,0:T(8,128)(2,1)S(1)}, bf16[336,768]{1,0:T(8,128)(2,1)}, u32[]{:S(2)}, u32[]{:S(2)}) collective-permute-start(bf16[336,768]{1,0:T(8,128)(2,1)S(1)} %collective-permute-done.3), channel_id=1, source_target_pairs={{2,4},{3,5},{4,2},{5,3},{10,12},{11,13},{12,10},{13,11},{18,20},{1... | collective-permute-start | bytes 1548296 | tf_op jit(solution)/shard_map/ppermute | solution.py:64
  27.9 16.7 %collective-permute-start.2 = (bf16[336,768]{1,0:T(8,128)(2,1)S(1)}, bf16[336,768]{1,0:T(8,128)(2,1)}, u32[]{:S(2)}, u32[]{:S(2)}) collective-permute-start(bf16[336,768]{1,0:T(8,128)(2,1)S(1)} %collective-permute-done.1), channel_id=1, source_target_pairs={{2,0},{3,1},{4,6},{5,7},{10,8},{11,9},{12,14},{13,15},{18,16},{19,... | collective-permute-start | bytes 1548296 | tf_op jit(solution)/shard_map/ppermute | solution.py:64
  33.0 24.3 %collective-permute-start.6 = (bf16[336,768]{1,0:T(8,128)(2,1)}, bf16[336,768]{1,0:T(8,128)(2,1)S(1)}, u32[]{:S(2)}, u32[]{:S(2)}) collective-permute-start(bf16[336,768]{1,0:T(8,128)(2,1)} %collective-permute-done.4), channel_id=1, source_target_pairs={{2,0},{3,1},{4,6},{5,7},{10,8},{11,9},{12,14},{13,15},{18,16},{19,... | collective-permute-start | bytes 1548296 | tf_op jit(solution)/shard_map/ppermute | solution.py:64
  34.4 24.5 %copy-start = (bf16[3072,768]{1,0:T(8,128)(2,1)S(1)}, bf16[3072,768]{1,0:T(8,128)(2,1)}, u32[]{:S(2)}) copy-start(bf16[3072,768]{1,0:T(8,128)(2,1)} %refs_12_.1) | copy-start | bytes 14155780
  37.4 24.6 %copy-start.19 = (bf16[256,768]{1,0:T(8,128)(2,1)}, bf16[256,768]{1,0:T(8,128)(2,1)S(1)}, u32[]{:S(2)}) copy-start(bf16[256,768]{1,0:T(8,128)(2,1)S(1)} %get-tuple-element.158.refs_3_) | copy-start | bytes 1179652
  37.4 24.6 %collective-permute-start.8 = (bf16[336,768]{1,0:T(8,128)(2,1)S(1)}, bf16[336,768]{1,0:T(8,128)(2,1)S(1)}, u32[]{:S(2)}, u32[]{:S(2)}) collective-permute-start(bf16[336,768]{1,0:T(8,128)(2,1)S(1)} %copy-done.12), channel_id=1, source_target_pairs={{0,1},{1,0},{2,3},{3,2},{4,5},{5,4},{6,7},{7,6},{8,9},{9,8},{10,11... | collective-permute-start | bytes 1548296 | tf_op jit(solution)/shard_map/ppermute | solution.py:51
  39.8 39.0 %collective-permute-start.9 = (bf16[336,768]{1,0:T(8,128)(2,1)S(1)}, bf16[336,768]{1,0:T(8,128)(2,1)S(1)}, u32[]{:S(2)}, u32[]{:S(2)}) collective-permute-start(bf16[336,768]{1,0:T(8,128)(2,1)S(1)} %collective-permute-done.3), channel_id=1, source_target_pairs={{0,1},{1,0},{2,3},{3,2},{4,5},{5,4},{6,7},{7,6},{8,9},{9,8},{10,11... | collective-permute-start | bytes 1548296 | tf_op jit(solution)/shard_map/ppermute | solution.py:51
  45.7 16.3 %copy-start.3 = (bf16[336,768]{1,0:T(8,128)(2,1)}, bf16[336,768]{1,0:T(8,128)(2,1)S(1)}, u32[]{:S(2)}) copy-start(bf16[336,768]{1,0:T(8,128)(2,1)S(1)} %broadcast_select_fusion.1) | copy-start | bytes 1548292
  45.7 48.7 %collective-permute-start.5 = (bf16[336,768]{1,0:T(8,128)(2,1)S(1)}, bf16[336,768]{1,0:T(8,128)(2,1)S(1)}, u32[]{:S(2)}, u32[]{:S(2)}) collective-permute-start(bf16[336,768]{1,0:T(8,128)(2,1)S(1)} %broadcast_select_fusion.1), channel_id=1, source_target_pairs={{0,1},{1,0},{2,3},{3,2},{4,5},{5,4},{6,7},{7,6},{8,9},{9,8},{10,11... | collective-permute-start | bytes 1548296 | tf_op jit(solution)/shard_map/ppermute | solution.py:51
  57.3 37.1 %collective-permute-start.7 = (bf16[336,768]{1,0:T(8,128)(2,1)S(1)}, bf16[336,768]{1,0:T(8,128)(2,1)S(1)}, u32[]{:S(2)}, u32[]{:S(2)}) collective-permute-start(bf16[336,768]{1,0:T(8,128)(2,1)S(1)} %broadcast_select_fusion), channel_id=1, source_target_pairs={{0,1},{1,0},{2,3},{3,2},{4,5},{5,4},{6,7},{7,6},{8,9},{9,8},{10,11... | collective-permute-start | bytes 1548296 | tf_op jit(solution)/shard_map/ppermute | solution.py:51
  130.6 37.0 %collective-permute-start.10 = (bf16[8,576,384]{2,1,0:T(8,128)(2,1)}, bf16[8,576,384]{2,1,0:T(8,128)(2,1)S(1)}, u32[]{:S(2)}, u32[]{:S(2)}) collective-permute-start(bf16[8,576,384]{2,1,0:T(8,128)(2,1)} %away.4.refs_20_), channel_id=1, source_target_pairs={{0,8},{8,0},{16,24},{24,16},{1,9},{9,1},{17,25},{25,17},{2,10},{10... | collective-permute-start | bytes 10616840 | tf_op jit(solution)/shard_map/ppermute | solution.py:51
  136.0 39.7 %collective-permute-start.11 = (bf16[8,480,384]{2,1,0:T(8,128)(2,1)}, bf16[8,480,384]{2,1,0:T(8,128)(2,1)}, u32[]{:S(2)}, u32[]{:S(2)}) collective-permute-start(bf16[8,480,384]{2,1,0:T(8,128)(2,1)} %away.5.refs_21_), channel_id=1, source_target_pairs={{0,8},{8,0},{16,24},{24,16},{1,9},{9,1},{17,25},{25,17},{2,10},{10... | collective-permute-start | bytes 8847368 | tf_op jit(solution)/shard_map/ppermute | solution.py:51
  136.0 9.9 %collective-permute-start.12 = (bf16[208,768]{1,0:T(8,128)(2,1)S(1)}, bf16[208,768]{1,0:T(8,128)(2,1)S(1)}, u32[]{:S(2)}, u32[]{:S(2)}) collective-permute-start(bf16[208,768]{1,0:T(8,128)(2,1)S(1)} %copy-done.5), channel_id=1, source_target_pairs={{0,2},{1,3},{2,0},{3,1},{4,6},{5,7},{6,4},{7,5},{8,10},{9,11},{10,... | collective-permute-start | bytes 958472 | tf_op jit(solution)/shard_map/ppermute | solution.py:64
  137.0 9.6 %collective-permute-start.15 = (bf16[208,768]{1,0:T(8,128)(2,1)S(1)}, bf16[208,768]{1,0:T(8,128)(2,1)S(1)}, u32[]{:S(2)}, u32[]{:S(2)}) collective-permute-start(bf16[208,768]{1,0:T(8,128)(2,1)S(1)} %copy-done.5), channel_id=1, source_target_pairs={{2,4},{3,5},{4,2},{5,3},{10,12},{11,13},{12,10},{13,11},{18,20},{1... | collective-permute-start | bytes 958472 | tf_op jit(solution)/shard_map/ppermute | solution.py:64
  145.9 14.0 %copy-start.6 = (bf16[208,768]{1,0:T(8,128)(2,1)}, bf16[208,768]{1,0:T(8,128)(2,1)S(1)}, u32[]{:S(2)}) copy-start(bf16[208,768]{1,0:T(8,128)(2,1)S(1)} %collective-permute-done.12) | copy-start | bytes 958468
  145.9 2.6 collective-permute-start.17
  146.6 13.3 %collective-permute-start.16 = (bf16[208,768]{1,0:T(8,128)(2,1)S(1)}, bf16[208,768]{1,0:T(8,128)(2,1)S(1)}, u32[]{:S(2)}, u32[]{:S(2)}) collective-permute-start(bf16[208,768]{1,0:T(8,128)(2,1)S(1)} %collective-permute-done.15), channel_id=1, source_target_pairs={{2,0},{3,1},{4,6},{5,7},{10,8},{11,9},{12,14},{13,15},{18,16},{19,... | collective-permute-start | bytes 958472 | tf_op jit(solution)/shard_map/ppermute | solution.py:64
  147.9 55.4 %collective-permute-start.13 = (bf16[208,768]{1,0:T(8,128)(2,1)S(1)}, bf16[208,768]{1,0:T(8,128)(2,1)S(1)}, u32[]{:S(2)}, u32[]{:S(2)}) collective-permute-start(bf16[208,768]{1,0:T(8,128)(2,1)S(1)} %copy-done.5), channel_id=1, source_target_pairs={{0,1},{1,0},{2,3},{3,2},{4,5},{5,4},{6,7},{7,6},{8,9},{9,8},{10,11... | collective-permute-start | bytes 958472 | tf_op jit(solution)/shard_map/ppermute | solution.py:51
  148.6 17.5 %collective-permute-start.18 = (bf16[208,768]{1,0:T(8,128)(2,1)S(1)}, bf16[208,768]{1,0:T(8,128)(2,1)S(1)}, u32[]{:S(2)}, u32[]{:S(2)}) collective-permute-start(bf16[208,768]{1,0:T(8,128)(2,1)S(1)} %collective-permute-done.17), channel_id=1, source_target_pairs={{2,0},{3,1},{4,6},{5,7},{10,8},{11,9},{12,14},{13,15},{18,16},{19,... | collective-permute-start | bytes 958472 | tf_op jit(solution)/shard_map/ppermute | solution.py:64
  160.0 43.3 %collective-permute-start.14 = (bf16[208,768]{1,0:T(8,128)(2,1)S(1)}, bf16[208,768]{1,0:T(8,128)(2,1)S(1)}, u32[]{:S(2)}, u32[]{:S(2)}) collective-permute-start(bf16[208,768]{1,0:T(8,128)(2,1)S(1)} %collective-permute-done.12), channel_id=1, source_target_pairs={{0,1},{1,0},{2,3},{3,2},{4,5},{5,4},{6,7},{7,6},{8,9},{9,8},{10,11... | collective-permute-start | bytes 958472 | tf_op jit(solution)/shard_map/ppermute | solution.py:51
  161.5 14.2 %copy-start.1 = (bf16[208,768]{1,0:T(8,128)(2,1)}, bf16[208,768]{1,0:T(8,128)(2,1)S(1)}, u32[]{:S(2)}) copy-start(bf16[208,768]{1,0:T(8,128)(2,1)S(1)} %broadcast_select_fusion.7) | copy-start | bytes 958468
  166.1 37.2 %collective-permute-start.19 = (bf16[208,768]{1,0:T(8,128)(2,1)S(1)}, bf16[208,768]{1,0:T(8,128)(2,1)S(1)}, u32[]{:S(2)}, u32[]{:S(2)}) collective-permute-start(bf16[208,768]{1,0:T(8,128)(2,1)S(1)} %broadcast_select_fusion.7), channel_id=1, source_target_pairs={{0,1},{1,0},{2,3},{3,2},{4,5},{5,4},{6,7},{7,6},{8,9},{9,8},{10,11... | collective-permute-start | bytes 958472 | tf_op jit(solution)/shard_map/ppermute | solution.py:51
  167.7 35.6 %collective-permute-start.20 = (bf16[208,768]{1,0:T(8,128)(2,1)S(1)}, bf16[208,768]{1,0:T(8,128)(2,1)S(1)}, u32[]{:S(2)}, u32[]{:S(2)}) collective-permute-start(bf16[208,768]{1,0:T(8,128)(2,1)S(1)} %broadcast_select_fusion.6), channel_id=1, source_target_pairs={{0,1},{1,0},{2,3},{3,2},{4,5},{5,4},{6,7},{7,6},{8,9},{9,8},{10,11... | collective-permute-start | bytes 958472 | tf_op jit(solution)/shard_map/ppermute | solution.py:51
  191.3 10.3 %copy-start.21 = (bf16[256,256]{1,0:T(8,128)(2,1)S(1)}, bf16[256,256]{1,0:T(8,128)(2,1)}, u32[]{:S(2)}) copy-start(bf16[256,256]{1,0:T(8,128)(2,1)} %get-tuple-element.105.refs_5_.refs_20_) | copy-start | bytes 393220
  191.3 10.3 %copy-start.28 = (bf16[256,256]{1,0:T(8,128)(2,1)S(1)}, bf16[256,256]{1,0:T(8,128)(2,1)}, u32[]{:S(2)}) copy-start(bf16[256,256]{1,0:T(8,128)(2,1)} %get-tuple-element.108.refs_20_) | copy-start | bytes 393220
  236.5 3.7 %collective-permute-start.21 = (bf16[128,768]{1,0:T(8,128)(2,1)}, bf16[128,768]{1,0:T(8,128)(2,1)S(1)}, u32[]{:S(2)}, u32[]{:S(2)}) collective-permute-start(bf16[128,768]{1,0:T(8,128)(2,1)} %get-tuple-element.123), channel_id=1, source_target_pairs={{8,0},{16,8},{24,16},{9,1},{17,9},{25,17},{10,2},{18,10},{26,18},{... | collective-permute-start | bytes 589832 | tf_op jit(solution)/shard_map/ppermute | solution.py:46
  237.8 35.3 %collective-permute-start.37 = (bf16[4,2,240,384]{3,2,1,0:T(8,128)(2,1)}, bf16[4,2,240,384]{3,2,1,0:T(8,128)(2,1)S(1)}, u32[]{:S(2)}, u32[]{:S(2)}) collective-permute-start(bf16[4,2,240,384]{3,2,1,0:T(8,128)(2,1)} %get-tuple-element.107.refs_22_), channel_id=1, source_target_pairs={{0,1},{1,0},{2,3},{3,2},{4,5},{5,4},{6,7},{7,6},{8,9},{9,8},{10,11... | collective-permute-start | bytes 4423688 | tf_op jit(solution)/shard_map/ppermute | solution.py:51
  238.3 44.2 %collective-permute-start.43 = (bf16[8,288,384]{2,1,0:T(8,128)(2,1)S(1)}, bf16[8,288,384]{2,1,0:T(8,128)(2,1)}, u32[]{:S(2)}, u32[]{:S(2)}) collective-permute-start(bf16[8,288,384]{2,1,0:T(8,128)(2,1)S(1)} %copy-done.18), channel_id=1, source_target_pairs={{0,16},{8,24},{16,0},{24,8},{1,17},{9,25},{17,1},{25,9},{2,18},{10... | collective-permute-start | bytes 5308424 | tf_op jit(solution)/shard_map/ppermute | solution.py:51
  247.5 13.8 %collective-permute-start.22 = (bf16[8,192,384]{2,1,0:T(8,128)(2,1)}, bf16[8,192,384]{2,1,0:T(8,128)(2,1)}, u32[]{:S(2)}, u32[]{:S(2)}) collective-permute-start(bf16[8,192,384]{2,1,0:T(8,128)(2,1)} %away.6), channel_id=1, source_target_pairs={{0,8},{8,0},{16,24},{24,16},{1,9},{9,1},{17,25},{25,17},{2,10},{10... | collective-permute-start | bytes 3538952 | tf_op jit(solution)/shard_map/ppermute | solution.py:51
  256.9 34.8 %collective-permute-start.30 = (bf16[8,288,384]{2,1,0:T(8,128)(2,1)}, bf16[8,288,384]{2,1,0:T(8,128)(2,1)}, u32[]{:S(2)}, u32[]{:S(2)}) collective-permute-start(bf16[8,288,384]{2,1,0:T(8,128)(2,1)} %away.7), channel_id=1, source_target_pairs={{0,8},{8,0},{16,24},{24,16},{1,9},{9,1},{17,25},{25,17},{2,10},{10... | collective-permute-start | bytes 5308424 | tf_op jit(solution)/shard_map/ppermute | solution.py:51
  258.0 2.6 collective-permute-start.23
  264.6 23.3 %collective-permute-start.24 = (bf16[4,2,112,384]{3,2,1,0:T(8,128)(2,1)}, bf16[4,2,112,384]{3,2,1,0:T(8,128)(2,1)}, u32[]{:S(2)}, u32[]{:S(2)}) collective-permute-start(bf16[4,2,112,384]{3,2,1,0:T(8,128)(2,1)} %get-tuple-element.132), channel_id=1, source_target_pairs={{0,1},{1,0},{2,3},{3,2},{4,5},{5,4},{6,7},{7,6},{8,9},{9,8},{10,11... | collective-permute-start | bytes 2064392 | tf_op jit(solution)/shard_map/ppermute | solution.py:51
  277.0 21.3 %collective-permute-start.38 = (bf16[2,2,240,384]{3,2,1,0:T(8,128)(2,1)}, bf16[2,2,240,384]{3,2,1,0:T(8,128)(2,1)}, u32[]{:S(2)}, u32[]{:S(2)}) collective-permute-start(bf16[2,2,240,384]{3,2,1,0:T(8,128)(2,1)} %get-tuple-element.143), channel_id=1, source_target_pairs={{0,16},{8,24},{16,0},{24,8},{1,17},{9,25},{17,1},{25,9},{2,18},{10... | collective-permute-start | bytes 2211848 | tf_op jit(solution)/shard_map/ppermute | solution.py:51
  285.6 33.2 %collective-permute-start.44 = (bf16[2,2,288,384]{3,2,1,0:T(8,128)(2,1)}, bf16[2,2,288,384]{3,2,1,0:T(8,128)(2,1)S(1)}, u32[]{:S(2)}, u32[]{:S(2)}) collective-permute-start(bf16[2,2,288,384]{3,2,1,0:T(8,128)(2,1)} %get-tuple-element.141), channel_id=1, source_target_pairs={{0,1},{1,0},{2,3},{3,2},{4,5},{5,4},{6,7},{7,6},{8,9},{9,8},{10,11... | collective-permute-start | bytes 2654216 | tf_op jit(solution)/shard_map/ppermute | solution.py:51
  289.8 15.8 %collective-permute-start.25 = (bf16[2,2,112,384]{3,2,1,0:T(8,128)(2,1)}, bf16[2,2,112,384]{3,2,1,0:T(8,128)(2,1)}, u32[]{:S(2)}, u32[]{:S(2)}) collective-permute-start(bf16[2,2,112,384]{3,2,1,0:T(8,128)(2,1)} %get-tuple-element.149), channel_id=1, source_target_pairs={{0,16},{8,24},{16,0},{24,8},{1,17},{9,25},{17,1},{25,9},{2,18},{10... | collective-permute-start | bytes 1032200 | tf_op jit(solution)/shard_map/ppermute | solution.py:51
  296.5 27.1 %collective-permute-start.31 = (bf16[8,144,384]{2,1,0:T(8,128)(2,1)}, bf16[8,144,384]{2,1,0:T(8,128)(2,1)}, u32[]{:S(2)}, u32[]{:S(2)}) collective-permute-start(bf16[8,144,384]{2,1,0:T(8,128)(2,1)} %get-tuple-element.135), channel_id=1, source_target_pairs={{0,16},{8,24},{16,0},{24,8},{1,17},{9,25},{17,1},{25,9},{2,18},{10... | collective-permute-start | bytes 2654216 | tf_op jit(solution)/shard_map/ppermute | solution.py:51
  300.2 18.4 %collective-permute-start.39 = (bf16[2,240,384]{2,1,0:T(8,128)(2,1)}, bf16[2,240,384]{2,1,0:T(8,128)(2,1)S(1)}, u32[]{:S(2)}, u32[]{:S(2)}) collective-permute-start(bf16[2,240,384]{2,1,0:T(8,128)(2,1)} %get-tuple-element.147), channel_id=1, source_target_pairs={{0,2},{1,3},{2,0},{3,1},{4,6},{5,7},{6,4},{7,5},{8,10},{9,11},{10,... | collective-permute-start | bytes 1105928 | tf_op jit(solution)/shard_map/ppermute | solution.py:51
  306.7 8.9 %collective-permute-start.26 = (bf16[2,112,384]{2,1,0:T(8,128)(2,1)S(1)}, bf16[2,112,384]{2,1,0:T(8,128)(2,1)S(1)}, u32[]{:S(2)}, u32[]{:S(2)}) collective-permute-start(bf16[2,112,384]{2,1,0:T(8,128)(2,1)S(1)} %get-tuple-element.162), channel_id=1, source_target_pairs={{0,2},{1,3},{2,0},{3,1},{4,6},{5,7},{6,4},{7,5},{8,10},{9,11},{10,... | collective-permute-start | bytes 516104 | tf_op jit(solution)/shard_map/ppermute | solution.py:51
  315.7 10.6 %collective-permute-start.27 = (bf16[112,384]{1,0:T(8,128)(2,1)S(1)}, bf16[112,384]{1,0:T(8,128)(2,1)S(1)}, u32[]{:S(2)}, u32[]{:S(2)}) collective-permute-start(bf16[112,384]{1,0:T(8,128)(2,1)S(1)} %fusion.8), channel_id=1, source_target_pairs={{0,4},{1,5},{2,6},{3,7},{4,0},{5,1},{6,2},{7,3},{8,12},{9,13},{10,... | collective-permute-start | bytes 258056 | tf_op jit(solution)/shard_map/ppermute | solution.py:51
  318.7 12.2 %collective-permute-start.40 = (bf16[240,384]{1,0:T(8,128)(2,1)S(1)}, bf16[240,384]{1,0:T(8,128)(2,1)S(1)}, u32[]{:S(2)}, u32[]{:S(2)}) collective-permute-start(bf16[240,384]{1,0:T(8,128)(2,1)S(1)} %fusion.5), channel_id=1, source_target_pairs={{0,4},{1,5},{2,6},{3,7},{4,0},{5,1},{6,2},{7,3},{8,12},{9,13},{10,... | collective-permute-start | bytes 552968 | tf_op jit(solution)/shard_map/ppermute | solution.py:51
  319.7 20.1 %collective-permute-start.45 = (bf16[2,288,384]{2,1,0:T(8,128)(2,1)}, bf16[2,288,384]{2,1,0:T(8,128)(2,1)S(1)}, u32[]{:S(2)}, u32[]{:S(2)}) collective-permute-start(bf16[2,288,384]{2,1,0:T(8,128)(2,1)} %get-tuple-element.145), channel_id=1, source_target_pairs={{0,2},{1,3},{2,0},{3,1},{4,6},{5,7},{6,4},{7,5},{8,10},{9,11},{10,... | collective-permute-start | bytes 1327112 | tf_op jit(solution)/shard_map/ppermute | solution.py:51
  326.2 4.6 %collective-permute-start.28 = (bf16[112,384]{1,0:T(8,128)(2,1)S(1)}, bf16[112,384]{1,0:T(8,128)(2,1)S(1)}, u32[]{:S(2)}, u32[]{:S(2)}) collective-permute-start(bf16[112,384]{1,0:T(8,128)(2,1)S(1)} %bitcast_add_fusion.18), channel_id=1, source_target_pairs={{0,16},{8,24},{16,0},{24,8},{1,17},{9,25},{17,1},{25,9},{2,18},{10... | collective-permute-start | bytes 258056 | tf_op jit(solution)/shard_map/ppermute | solution.py:51
  327.1 17.0 %collective-permute-start.32 = (bf16[2,2,144,384]{3,2,0,1:T(8,128)(2,1)S(1)}, bf16[2,2,144,384]{3,2,0,1:T(8,128)(2,1)S(1)}, u32[]{:S(2)}, u32[]{:S(2)}) collective-permute-start(bf16[2,2,144,384]{3,2,0,1:T(8,128)(2,1)S(1)} %fusion), channel_id=1, source_target_pairs={{0,1},{1,0},{2,3},{3,2},{4,5},{5,4},{6,7},{7,6},{8,9},{9,8},{10,11... | collective-permute-start | bytes 1327112 | tf_op jit(solution)/shard_map/ppermute | solution.py:51
  330.8 1.5 collective-permute-start.29
  331.0 7.1 %collective-permute-start.41 = (bf16[240,384]{1,0:T(8,128)(2,1)S(1)}, bf16[240,384]{1,0:T(8,128)(2,1)S(1)}, u32[]{:S(2)}, u32[]{:S(2)}) collective-permute-start(bf16[240,384]{1,0:T(8,128)(2,1)S(1)} %bitcast_add_fusion.10), channel_id=1, source_target_pairs={{0,16},{8,24},{16,0},{24,8},{1,17},{9,25},{17,1},{25,9},{2,18},{10... | collective-permute-start | bytes 552968 | tf_op jit(solution)/shard_map/ppermute | solution.py:51
  338.2 6.1 %collective-permute-start.42 = (bf16[2,240,384]{2,1,0:T(8,128)(2,1)S(1)}, bf16[2,240,384]{2,1,0:T(8,128)(2,1)S(1)}, u32[]{:S(2)}, u32[]{:S(2)}) collective-permute-start(bf16[2,240,384]{2,1,0:T(8,128)(2,1)S(1)} %pad_maximum_fusion.4), channel_id=1, source_target_pairs={{0,8},{8,0},{16,24},{24,16},{1,9},{9,1},{17,25},{25,17},{2,10},{10... | collective-permute-start | bytes 1105928 | tf_op jit(solution)/shard_map/ppermute | solution.py:51
  339.8 17.8 %collective-permute-start.46 = (bf16[288,384]{1,0:T(8,128)(2,1)S(1)}, bf16[288,384]{1,0:T(8,128)(2,1)S(1)}, u32[]{:S(2)}, u32[]{:S(2)}) collective-permute-start(bf16[288,384]{1,0:T(8,128)(2,1)S(1)} %fusion.3), channel_id=1, source_target_pairs={{0,4},{1,5},{2,6},{3,7},{4,0},{5,1},{6,2},{7,3},{8,12},{9,13},{10,... | collective-permute-start | bytes 663560 | tf_op jit(solution)/shard_map/ppermute | solution.py:51
  344.2 11.3 %collective-permute-start.33 = (bf16[2,144,384]{2,1,0:T(8,128)(2,1)S(1)}, bf16[2,144,384]{2,1,0:T(8,128)(2,1)S(1)}, u32[]{:S(2)}, u32[]{:S(2)}) collective-permute-start(bf16[2,144,384]{2,1,0:T(8,128)(2,1)S(1)} %get-tuple-element.153), channel_id=1, source_target_pairs={{0,2},{1,3},{2,0},{3,1},{4,6},{5,7},{6,4},{7,5},{8,10},{9,11},{10,... | collective-permute-start | bytes 663560 | tf_op jit(solution)/shard_map/ppermute | solution.py:51
  355.5 7.5 %collective-permute-start.34 = (bf16[144,384]{1,0:T(8,128)(2,1)S(1)}, bf16[144,384]{1,0:T(8,128)(2,1)S(1)}, u32[]{:S(2)}, u32[]{:S(2)}) collective-permute-start(bf16[144,384]{1,0:T(8,128)(2,1)S(1)} %fusion.7), channel_id=1, source_target_pairs={{0,4},{1,5},{2,6},{3,7},{4,0},{5,1},{6,2},{7,3},{8,12},{9,13},{10,... | collective-permute-start | bytes 331784 | tf_op jit(solution)/shard_map/ppermute | solution.py:51
  357.7 10.3 %collective-permute-start.47 = (bf16[288,384]{1,0:T(8,128)(2,1)S(1)}, bf16[288,384]{1,0:T(8,128)(2,1)S(1)}, u32[]{:S(2)}, u32[]{:S(2)}) collective-permute-start(bf16[288,384]{1,0:T(8,128)(2,1)S(1)} %bitcast_add_fusion.5), channel_id=1, source_target_pairs={{0,16},{8,24},{16,0},{24,8},{1,17},{9,25},{17,1},{25,9},{2,18},{10... | collective-permute-start | bytes 663560 | tf_op jit(solution)/shard_map/ppermute | solution.py:51
  363.0 4.8 %collective-permute-start.35 = (bf16[144,384]{1,0:T(8,128)(2,1)S(1)}, bf16[144,384]{1,0:T(8,128)(2,1)S(1)}, u32[]{:S(2)}, u32[]{:S(2)}) collective-permute-start(bf16[144,384]{1,0:T(8,128)(2,1)S(1)} %bitcast_add_fusion.15), channel_id=1, source_target_pairs={{0,16},{8,24},{16,0},{24,8},{1,17},{9,25},{17,1},{25,9},{2,18},{10... | collective-permute-start | bytes 331784 | tf_op jit(solution)/shard_map/ppermute | solution.py:51
  367.9 1.5 collective-permute-start.36
  368.1 2.7 collective-permute-start.48
  (32 other events, 123.2 us)

commit v3 on v2

v3 whole, which is shorter than its diff:
```python
import functools

import jax
import jax.numpy as jnp
import numpy as np
from jax import lax
from jax.experimental import pallas as pl
from jax.experimental.pallas import tpu as pltpu
from jax.sharding import PartitionSpec as P

HEADS = 12
HEAD_DIM = 64
PAIR = 2 * HEAD_DIM
PAIRS = HEADS // 2
SCALE = HEAD_DIM**-0.5
LANES = 384
SHARED = 192
MARKS = 16
GRID_SIDE = 56
EPS = 1e-06
NEG = -1e30
F32 = jnp.float32
BF16 = jnp.bfloat16
VMEM_LIMIT = 56
CFG = dict(qp=(3, 3), kp=(3, 3), home=1, gate=0, b="yx", c="x", d="z", ab2=None, ab3=None, merged=False, direct=False, sc=False, limit=56, limits={}, chain=False, away_first=True, early=False, join=False)
PACE = 1.0


def dot(a, b):
    return jnp.dot(a, b, preferred_element_type=F32)


def dot_nt(a, b, precision=None):
    return lax.dot_general(a, b, (((1,), (1,)), ((), ())), preferred_element_type=F32, precision=precision)


def dot_tn(a, b):
    return lax.dot_general(a, b, (((0,), (0,)), ((), ())), preferred_element_type=F32)


def sds(shape, dtype):
    return jax.ShapeDtypeStruct(tuple(shape), dtype)


def shifted(x, axis, by):
    length = lax.axis_size(axis)
    pairs = [(i, i + by) for i in range(length) if 0 <= i + by < length]
    return lax.ppermute(x, axis, pairs)


def swap(x, axis, bit):
    length = lax.axis_size(axis)
    return lax.ppermute(x, axis, [(i, i ^ bit) for i in range(length)])


def swap_chip(x, dx, dz, dy):
    n_gx, n_gy = lax.axis_size("gx"), lax.axis_size("gy")
    flip = 2 * dx * n_gy + 2 * dz + dy
    return lax.ppermute(x, ("gx", "gy"), [(i, i ^ flip) for i in range(n_gx * n_gy)])


class ColumnGather:
    def __init__(self, unit):
        self.unit = unit
        self.direct = lax.axis_size("gy") == 8
        if not self.direct:
            self.groups = [[lax.all_gather(unit, "gy", axis=0, tiled=False)]]
            return
        self.y0 = self.across(unit)
        self.near = self.along(unit, [(0, 1), (1, 0), (2, 3), (3, 2)])
        self.mid = self.along(unit, [(1, 2), (2, 1)])

    def along(self, x, hops):
        return lax.ppermute(x, "gy", [(2 * a + y, 2 * b + y) for a, b in hops for y in (0, 1)])

    def across(self, x):
        return swap(x, "gy", 1)

    def second(self):
        self.y1 = self.across(self.near)
        self.far_end = self.along(self.mid, [(1, 0), (2, 3)])
        self.far_mid = self.along(self.near, [(1, 2), (2, 1)])

    def third(self, after):
        self.last_end = self.along(self.far_mid, [(1, 0), (2, 3)])
        self.far = choose(self.far_end, self.far_mid, after)
        self.y2 = self.across(self.far)

    def fourth(self, after):
        self.last = choose(self.last_end, self.mid, after)
        self.y3 = self.across(self.last)
        self.group()

    def group(self):
        groups = [[self.unit, self.near, self.y0], [self.y1, self.far], [self.last, self.y2, self.y3]]
        if CFG["early"]:
            groups = [[self.unit, self.near], [self.y0, self.y1, self.far], [self.last, self.y2, self.y3]]
        self.groups = [[part[None] for part in group] for group in groups]


class FreeGather(ColumnGather):
    def __init__(self, unit):
        super().__init__(unit)
        if not self.direct:
            return
        self.second()
        place = lax.axis_index("gy") // 2
        at_end = (place == 0) | (place == 3)
        self.far = jnp.where(at_end, self.far_end, self.far_mid)
        self.y2 = self.across(self.far)
        self.last_end = self.along(self.far_mid, [(1, 0), (2, 3)])
        self.last = jnp.where(at_end, self.last_end, self.mid)
        self.y3 = self.across(self.last)
        self.group()


class DirectGather:
    def __init__(self, unit):
        self.unit = unit
        if lax.axis_size("gy") != 8:
            self.groups = [[lax.all_gather(unit, "gy", axis=0, tiled=False)]]
            return
        self.near, self.y0 = swap_chip(unit, 0, 1, 0), swap_chip(unit, 0, 0, 1)
        self.mid = self.far_end = self.far_mid = self.last_end = self.near
        self.far, self.last = swap_chip(unit, 0, 2, 0), swap_chip(unit, 0, 3, 0)

        self.second()

    def second(self):
        y1, y2, y3 = (swap_chip(x, 0, 0, 1) for x in (self.near, self.far, self.last))
        self.y1, self.y2, self.y3 = y1, y2, y3
        groups = [[self.unit, self.near, self.y0], [y1, self.far], [self.last, y2, y3]]
        self.groups = [[part[None] for part in group] for group in groups]


def choose(at_end, inside, after):
    def kernel(a, b, out):
        place = lax.axis_index("gy") // 2
        out[...] = jnp.where((place == 0) | (place == 3), a[...], b[...])

    return call(kernel, plain(at_end, inside), [(sds(inside.shape, inside.dtype), VMEM)], "choose", cost=2.3, after=after)[0]


def bit_of(axis, bit):
    return (lax.axis_index(axis) // bit) % 2


def call(kernel, ins, outs, name, grid=None, scratch=(), cost=4.0, after=()):
    limit = CFG["limits"].get(name, CFG["limit"]) if lax.axis_size("gy") == 8 else VMEM_LIMIT
    specs = [spec for _, spec in ins] + [pl.BlockSpec(memory_space=pl.ANY)] * len(after)
    count = len(ins)

    def body(*refs):
        kernel(*refs[:count], *refs[count + len(after) :])

    return pl.pallas_call(
        body,
        grid=grid or (),
        in_specs=specs,
        out_specs=tuple(spec for _, spec in outs),
        out_shape=tuple(shape for shape, _ in outs),
        scratch_shapes=list(scratch),
        compiler_params=pltpu.CompilerParams(vmem_limit_bytes=limit * 2**20),
        cost_estimate=pl.CostEstimate(flops=int(cost * 1e8), bytes_accessed=int(cost * 3e5), transcendentals=0),
        name=name,
    )(*[array for array, _ in ins], *after)


VMEM = pl.BlockSpec(memory_space=pltpu.VMEM)


def plain(*arrays):
    return [(a, VMEM) for a in arrays]


def fixed(array):
    zeros = (0,) * len(array.shape)
    return (array, pl.BlockSpec(tuple(array.shape), lambda h: zeros, pipeline_mode=pl.Buffered(1)))


def lead(array, first=0):
    zeros = (0,) * (len(array.shape) - 1)
    return (array, pl.BlockSpec((1,) + tuple(array.shape[1:]), lambda h: (first + h,) + zeros))


def lanes(array, first=0, width=PAIR):
    return (array, pl.BlockSpec((array.shape[0], width), lambda h: (0, first + h)))


def half_mask(rows):
    return lax.broadcasted_iota(jnp.int32, (rows, PAIR), 1) < HEAD_DIM


def only_half(x, head):
    low_half = half_mask(x.shape[0])
    zero = jnp.zeros_like(x)
    return jnp.where(low_half, x, zero) if head == 0 else jnp.where(low_half, zero, x)


def merge_halves(first, second):
    rows = first.shape[0]
    return jnp.where(half_mask(rows), jnp.broadcast_to(first, (rows, PAIR)), jnp.broadcast_to(second, (rows, PAIR)))


def normalise(x):
    centered = x - jnp.mean(x, axis=1, keepdims=True)
    scale = lax.rsqrt(jnp.mean(centered * centered, axis=1, keepdims=True) + EPS)
    return centered * scale, scale


def norm_back(grad, unit_rows, scale, gain):
    g = grad * gain
    inner = jnp.mean(g * unit_rows, axis=1, keepdims=True)
    rows = scale * (g - jnp.mean(g, axis=1, keepdims=True) - unit_rows * inner)
    return rows, jnp.sum(grad * unit_rows, axis=0, keepdims=True), jnp.sum(grad, axis=0, keepdims=True)


def stack_heads(x):
    low_half = half_mask(x.shape[0])
    zero = jnp.zeros_like(x)
    return jnp.concatenate([jnp.where(low_half, x, zero), jnp.where(low_half, zero, x)], axis=0)


def unstack_heads(x):
    rows = x.shape[0] // 2
    return merge_halves(x[:rows], x[rows:])


def twice(x):
    return jnp.concatenate([x, x], axis=0)


def pair_lanes(ref, pair):
    return ref[:, pl.ds(pl.multiple_of(pair * PAIR, PAIR), PAIR)]


def group_blocks(block_refs):
    flat = [(ref, i) for ref in block_refs for i in range(ref.shape[0])]
    return [flat[i : i + 8] for i in range(0, len(flat), 8)]


def key_marks(ref, index, key_rows):
    marks = ref[index, key_rows : key_rows + MARKS, 0:256].astype(F32)
    return marks[0:1, 0:1], marks[0:1, 128:129]


def key_bias(group, key_rows):
    width = len(group) * key_rows
    lane = lax.broadcasted_iota(jnp.int32, (1, width), 1).astype(F32)
    bias = jnp.full((1, width), NEG, F32)
    for place, (ref, index) in enumerate(group):
        count, live = key_marks(ref, index, key_rows)
        local = lane - float(place * key_rows)
        good = (local >= 0.0) & (local < count)
        rim = (local >= float(SHARED)) & (local < float(key_rows)) & (live > 0.5)
        bias = jnp.where(good | rim, 0.0, bias)
    return bias


def key_bias_column(group, key_rows):
    parts = []
    for ref, index in group:
        count, live = key_marks(ref, index, key_rows)
        place = lax.broadcasted_iota(jnp.int32, (key_rows, 1), 0).astype(F32)
        good = (place < count) | ((place >= float(SHARED)) & (live > 0.5))
        parts.append(jnp.where(good, 0.0, NEG))
    return jnp.concatenate(parts, axis=0)


def position_table(width):
    unit_width = width // 16
    table = np.zeros((128, width), np.float32)
    bands = [(0, 8, 0, 4 * unit_width), (8, GRID_SIDE, 4 * unit_width, 6 * unit_width)]
    bands.append((64, GRID_SIDE, 10 * unit_width, 6 * unit_width))
    for row, count, lane, band in bands:
        half = band // 2
        power = np.arange(half, dtype=np.float32) / np.float32(half)
        omegas = np.float32(1.0) / np.power(np.float32(10000.0), power)
        angles = (np.arange(count, dtype=np.float32)[:, None] * omegas[None]).astype(np.float64)
        table[row : row + count, lane : lane + half] = np.sin(angles)
        table[row : row + count, lane + half : lane + band] = np.cos(angles)
    high = table.astype(jnp.bfloat16)
    low = (table - high.astype(np.float32)).astype(jnp.bfloat16)
    return jnp.asarray(high), jnp.asarray(low)


def embed_kernel(pix, weight, frame, cell, halo, high, low, gain, bias, stream_ref, rim_ref, low_ref):
    rows = pix.shape[0]
    code = lax.broadcasted_iota(jnp.int32, (128, rows), 0)
    first, second = cell[0:1, :], cell[1:2, :]
    hot = (code == frame[...]) | (code == first + 8) | (code == second + 64)
    hot = jnp.where(hot, 1.0, 0.0).astype(BF16)
    stream = dot(pix[...], weight[...]) + (dot_tn(hot, high[...]) + dot_tn(hot, low[...]))
    stream_ref[...] = stream
    place = lax.broadcasted_iota(jnp.int32, (rows, halo.shape[1]), 0)
    pick = jnp.where(place == halo[...], 1.0, 0.0).astype(BF16)
    rim_ref[...] = dot_tn(pick, stream.astype(BF16)).astype(BF16)
    unit_rows, _ = normalise(stream)
    low_ref[...] = (unit_rows * gain[...] + bias[...]).astype(BF16)


def unit_kernel(own, arrived, gain, bias, ids, live, unit_ref, joined_ref):
    rows, width = own.shape
    rim = arrived.shape[0]
    unit_rows, _ = normalise(arrived[...].astype(F32))
    rim_low = (unit_rows * gain[...] + bias[...]).astype(BF16)
    joined_ref[0:rows, :] = own[...]
    joined_ref[rows : rows + rim, :] = rim_low
    unit_ref[0:SHARED, :] = own[0:SHARED, :]
    unit_ref[SHARED : SHARED + rim, :] = rim_low
    count = jnp.sum(jnp.where(ids[...] == 0, 1.0, 0.0), axis=1, keepdims=True)
    lane = lax.broadcasted_iota(jnp.int32, (MARKS, width), 1)
    unit_ref[SHARED + rim :, :] = jnp.where(lane < 128, count, live[0:1, 0:1]).astype(BF16)


def attend_kernel(n_blocks, key_rows, first, last, *refs):
    refs = list(refs)

    def take(n):
        out = refs[:n]
        del refs[:n]
        return out

    block_refs = take(n_blocks)
    wk_ref, wv_ref, bias_ref = take(3)
    if first:
        own_ref, wq_ref, idr_ref = take(3)
    else:
        q_ref, acc_in, stat_in = take(3)
        if last:
            out_in, lse_in = take(2)
    idc_ref = take(1)[0]
    kv_ref = take(1)[0]
    if first:
        q_ref, kvown_ref = take(2)
        if not last:
            out_ref, lse_ref = take(2)
    if last:
        mixed_ref, full_lse_ref = take(2)
    else:
        acc_ref, stat_ref = take(2)
    pair = pl.program_id(0)
    own_rows = idc_ref.shape[0]
    groups = group_blocks(block_refs)
    biases = [key_bias_column(group, key_rows) for group in groups]
    here = pl.ds(pl.multiple_of(pair * PAIR, PAIR), PAIR)
    wkv = jnp.concatenate([wk_ref[...], wv_ref[...]], axis=1)
    shift = pair_lanes(bias_ref, PAIRS + pair)
    shift = jnp.concatenate([jnp.zeros_like(shift), shift], axis=1)
    base = 0
    for group in groups:
        for ref, index in group:
            kv_ref[0, base : base + key_rows, :] = (dot(ref[index, 0:key_rows, :], wkv) + shift).astype(BF16)
            base += key_rows
    if first:
        kvown_ref[0] = (dot(own_ref[...], wkv) + shift).astype(BF16)
        q = (dot(own_ref[0:own_rows, :], wq_ref[...]) + pair_lanes(bias_ref, pair)).astype(BF16) * BF16(SCALE)
        q_ref[0] = q
    else:
        q = q_ref[0]
    qs = stack_heads(q[0:SHARED])
    if first:
        peak = weight = total = None
    else:
        total = acc_in[0]
        peak, weight = stat_in[0, 0:1, :], stat_in[0, 8:9, :]
    base = 0
    for group, bias in zip(groups, biases):
        width = len(group) * key_rows
        span = slice(base, base + width)
        keys, values = kv_ref[0, span, 0:PAIR], kv_ref[0, span, PAIR:]
        base += width
        scores = dot_nt(keys, qs) + bias
        new = jnp.max(scores, axis=0, keepdims=True)
        if peak is not None:
            new = jnp.maximum(peak, new)
        probs = jnp.exp(scores - new)
        sums = jnp.sum(probs, axis=0, keepdims=True)
        part = dot_tn(values, probs.astype(BF16))
        if peak is None:
            weight, total = sums, part
        else:
            fade = jnp.exp(peak - new)
            weight = weight * fade + sums
            total = total * fade + part
        peak = new
    if first:
        idc = idc_ref[...]
        allowed = twice((idc == idr_ref[...]) & (idc != 0))
        scores = jnp.where(allowed, dot_nt(stack_heads(q), kvown_ref[0, 0:own_rows, 0:PAIR]), NEG)
        top = jnp.max(scores, axis=1, keepdims=True)
        probs = jnp.exp(scores - top)
        local_weight = jnp.sum(probs, axis=1, keepdims=True)
        local_out = unstack_heads(dot(probs.astype(BF16), kvown_ref[0, 0:own_rows, PAIR:]) / local_weight)
        local_lse = unstack_heads(top + jnp.log(local_weight))
        if not last:
            out_ref[:, here] = local_out
            lse_ref[:, here] = local_lse
    elif last:
        local_out, local_lse = out_in[:, here], lse_in[:, here]
    if last:
        shared_row = idc_ref[0:SHARED, :] == 0
        shared_out = unstack_heads((total / weight).T)
        shared_lse = unstack_heads(jnp.broadcast_to(peak + jnp.log(weight), (8, 2 * SHARED)).T[:, 0:1])
        mixed_ref[0:SHARED, here] = jnp.where(shared_row, shared_out, local_out[0:SHARED])
        mixed_ref[SHARED:, here] = local_out[SHARED:]
        full_lse_ref[0:SHARED, here] = jnp.where(shared_row, shared_lse, local_lse[0:SHARED])
        full_lse_ref[SHARED:, here] = local_lse[SHARED:]
    else:
        acc_ref[0] = total
        stat_ref[0, 0:8, :] = jnp.broadcast_to(peak, (8, 2 * SHARED))
        stat_ref[0, 8:16, :] = jnp.broadcast_to(weight, (8, 2 * SHARED))


class Attention:
    def __init__(self, first_low, weights, project_bias, idc, idr, key_rows):
        self.fixed = first_low, weights, project_bias, idc, idr
        self.key_rows = key_rows
        self.kvs = []

    def piece(self, blocks, last):
        first_low, weights, project_bias, idc, idr = self.fixed
        key_rows = self.key_rows
        own_rows, width = idc.shape[0], first_low.shape[1]
        wide = lambda rows: (sds((rows, width), F32), pl.BlockSpec((rows, width), lambda h: (0, 0)))
        deep = lambda rows, lane, dtype: (
            sds((PAIRS, rows, lane), dtype),
            pl.BlockSpec((1, rows, lane), lambda h: (h, 0, 0)),
        )
        first = not self.kvs
        keys = sum(b.shape[0] for b in blocks) * key_rows
        ins = [fixed(b) for b in blocks] + [lanes(weights, PAIRS), lanes(weights, 2 * PAIRS), fixed(project_bias)]
        if first:
            ins += [fixed(first_low), lanes(weights), fixed(idr)]
        else:
            ins += [lead(self.q)] + [lead(s) for s in self.state]
            if last:
                ins += [fixed(x) for x in self.local]
        ins += [fixed(idc)]
        outs = [deep(keys, 2 * PAIR, BF16)]
        if first:
            outs += [deep(own_rows, PAIR, BF16), deep(first_low.shape[0], 2 * PAIR, BF16)]
            if not last:
                outs += [wide(own_rows)] * 2
        outs += [wide(own_rows)] * 2 if last else [deep(PAIR, 2 * SHARED, F32), deep(16, 2 * SHARED, F32)]
        kernel = functools.partial(attend_kernel, len(blocks), key_rows, first, last)
        got = list(call(kernel, ins, outs, "attend", grid=(PAIRS,), cost=3.0 + keys / 90.0))
        self.kvs.append(got.pop(0))
        if first:
            self.q, self.kvown = got.pop(0), got.pop(0)
            if not last:
                self.local = [got.pop(0), got.pop(0)]
        self.state = got
        return (got[0],)


def erf(x):
    x = jnp.clip(x, -3.832506856900711, 3.832506856900711)
    s = x * x
    top = -2.72614225801306e-10
    for c in (2.77068142495902e-08, -2.10102402082508e-06, -5.69250639462346e-05, -7.34990630326855e-04, -2.95459980854025e-03, -1.60960333262415e-02):
        top = top * s + c
    low = -1.45660718464996e-05
    for c in (-2.13374055278905e-04, -1.68282697438203e-03, -7.37332916720468e-03, -1.42647390514189e-02):
        low = low * s + c
    return x * top / low


def middle_kernel(
    mixed, lse, stream, mlp_grad, act_grad, idc,
    w_output, merge_bias, gain, bias, w_up, up_bias, w_down, down_bias, w_head,
    predicted, act_ref, pre_ref, second_ref, mixed_low_ref, attn_low_ref, final_ref, attn_ref, grad_ref, unit_ref,
    stat_ref, up_sum, gain_sum, bias_sum, merge_sum,
):
    rows, width = mixed.shape
    hidden = w_up.shape[1]
    mixed_low = mixed[...].astype(BF16)
    mixed_low_ref[...] = mixed_low
    after = stream[...] + dot(mixed_low, w_output[...]) + merge_bias[...]
    unit_rows, scale = normalise(after)
    second = (unit_rows * gain[...] + bias[...]).astype(BF16)
    second_ref[...] = second
    out = after + down_bias[...]
    back = jnp.zeros((rows, width), F32)
    step = 768
    for start in range(0, hidden, step):
        part = slice(start, start + step)
        pre = dot(second, w_up[:, part]) + up_bias[:, part]
        cdf = 0.5 + 0.5 * erf(pre * 0.7071067811865476)
        act = (pre * cdf).astype(BF16)
        act_ref[:, part] = act
        slope = cdf + pre * (0.3989422804014327 * jnp.exp(-0.5 * pre * pre))
        grad = (act_grad[:, part] * slope).astype(BF16)
        pre_ref[:, part] = grad
        up_sum[:, part] = jnp.sum(grad.astype(F32), axis=0, keepdims=True)
        out += dot(act, w_down[part, :])
        back += dot_nt(grad, w_up[:, part])
    resid, gain_part, bias_part = norm_back(back, unit_rows, scale, gain[...])
    gain_sum[...] = gain_part
    bias_sum[...] = bias_part
    attn = mlp_grad[...] + resid
    attn_ref[...] = attn
    merge_sum[...] = jnp.sum(attn, axis=0, keepdims=True)
    attn_low = attn.astype(BF16)
    attn_low_ref[...] = attn_low
    grad = dot_nt(attn_low, w_output[...]).astype(BF16)
    grad_ref[...] = grad
    shared_row = idc[0:SHARED, :] == 0
    unit_ref[0:SHARED, :] = jnp.where(shared_row, grad[0:SHARED], jnp.zeros((SHARED, width), BF16))
    lane = lax.broadcasted_iota(jnp.int32, (MARKS, width), 1)
    head = lax.broadcasted_iota(jnp.int32, (MARKS, width), 0)
    ones = jnp.where(lane // HEAD_DIM == head, 1.0, 0.0)
    pick = jnp.where(lane == head * HEAD_DIM, 1.0, 0.0)
    delta = dot_nt(ones, grad.astype(F32) * mixed[...], lax.Precision.HIGHEST)
    turned = dot_nt(pick, lse[...], lax.Precision.HIGHEST)
    stat_ref[0] = turned
    stat_ref[1] = delta
    zeros = jnp.zeros((rows, 128), F32)
    ids = jnp.where(idc[...] == 0, 1.0, 0.0) + zeros
    row_ids = dot_nt(jnp.full((MARKS, 128), 1.0 / 128, F32), ids)
    shared_lane = row_ids[:, 0:SHARED] > 0.5
    sent = []
    for value, other in ((turned, -NEG), (delta, 0.0)):
        value = jnp.where(shared_lane, value[:, 0:SHARED], other)
        high = value.astype(BF16)
        sent += [high, (value - high.astype(F32)).astype(BF16)]
    unit_ref[SHARED:, :] = jnp.concatenate(sent, axis=1)
    final = out.astype(BF16)
    final_ref[...] = final
    predicted[...] = dot(final, w_head[...]).astype(BF16)


def query_kernel(n_blocks, n_kvs, key_rows, first, *refs):
    block_refs, kv_refs = refs[:n_blocks], refs[n_blocks : n_blocks + n_kvs]
    kvown_ref, q_ref, wq_ref, grad_ref, mixed_ref, lse_ref, bias_ref, idc_ref, idr_ref = refs[
        n_blocks + n_kvs : n_blocks + n_kvs + 9
    ]
    dq_ref, qall_ref = refs[-2:]
    pair = first + pl.program_id(0)
    own_rows = idc_ref.shape[0]
    flat = [(ref, i) for ref in block_refs for i in range(ref.shape[0])]
    base = 0
    wq, shift = wq_ref[...], pair_lanes(bias_ref, pair)
    for ref, index in flat:
        rows = (dot(ref[index, 0:SHARED, :], wq) + shift).astype(BF16)
        qall_ref[0, base : base + SHARED, :] = rows * BF16(SCALE)
        base += SHARED
    idc = idc_ref[...]
    allowed = twice((idc == idr_ref[...]) & (idc != 0))
    shared_row = idc == 0
    q = q_ref[0]
    grad = pair_lanes(grad_ref, pair)
    product = stack_heads(grad.astype(F32) * pair_lanes(mixed_ref, pair))
    delta = jnp.sum(product, axis=1, keepdims=True)
    lse = pair_lanes(lse_ref, pair)
    lse = jnp.concatenate([lse[:, 0:1], lse[:, HEAD_DIM : HEAD_DIM + 1]], axis=0)
    qm, gm = stack_heads(q), stack_heads(grad)
    part_rows = lambda x: jnp.concatenate([x[0:SHARED], x[own_rows : own_rows + SHARED]], axis=0)
    qs, gs, delta_s, lse_s = part_rows(qm), part_rows(gm), part_rows(delta), part_rows(lse)
    total, used = None, 0
    for kv_ref in kv_refs:
        count = kv_ref.shape[1] // key_rows
        for start in range(0, count, 8):
            size = min(8, count - start)
            bias = key_bias(flat[used : used + size], key_rows)
            used += size
            span = slice(start * key_rows, (start + size) * key_rows)
            keys = kv_ref[0, span, 0:PAIR]
            values = kv_ref[0, span, PAIR:]
            probs = jnp.exp(dot_nt(qs, keys) + bias - lse_s)
            ds = (probs * (dot_nt(gs, values) - delta_s)).astype(BF16)
            part = dot(ds, keys)
            total = part if total is None else total + part
    keys, values = kvown_ref[0, 0:own_rows, 0:PAIR], kvown_ref[0, 0:own_rows, PAIR:]
    probs = jnp.exp(jnp.where(allowed, dot_nt(qm, keys) - lse, NEG))
    ds = (probs * (dot_nt(gm, values) - delta)).astype(BF16)
    local = unstack_heads(dot(ds, keys)) * SCALE
    shared = jnp.where(shared_row[0:SHARED], unstack_heads(total) * SCALE, local[0:SHARED])
    here = pl.ds(pl.multiple_of(pl.program_id(0) * PAIR, PAIR), PAIR)
    dq_ref[0:SHARED, here] = shared.astype(BF16)
    dq_ref[SHARED:, here] = local[SHARED:].astype(BF16)


def query_back(groups, kvs, kvown, q, mixed_grad, mixed, lse, wq, project_bias, idc, idr, key_rows, first, pairs, after):
    own_rows = idc.shape[0]
    blocks = [b for group in groups for b in group]
    count = sum(b.shape[0] for b in blocks)
    ins = [fixed(b) for b in blocks] + [lead(kv, first) for kv in kvs] + [lead(x, first) for x in (kvown, q)] + [lanes(wq, first)]
    ins += [fixed(x) for x in (mixed_grad, mixed, lse, project_bias, idc, idr)]
    outs = [
        (sds((own_rows, pairs * PAIR), BF16), pl.BlockSpec((own_rows, pairs * PAIR), lambda h: (0, 0))),
        (sds((pairs, count * SHARED, PAIR), BF16), pl.BlockSpec((1, count * SHARED, PAIR), lambda h: (h, 0, 0))),
    ]
    kernel = functools.partial(query_kernel, len(blocks), len(kvs), key_rows, first)
    return call(kernel, ins, outs, "query_back", grid=(pairs,), cost=4.2 * pairs, after=after)


def key_kernel(n_blocks, first, *refs):
    grad_refs = refs[:n_blocks]
    kvown_ref, qall_ref, q_ref, grad_ref, own_stat_ref, idc_ref, idr_ref, live_ref = refs[n_blocks : n_blocks + 8]
    dk_ref, dv_ref, grads_ref, stats_ref = refs[n_blocks + 8 :]
    pair = first + pl.program_id(0)
    own_rows = idc_ref.shape[0]
    rim = kvown_ref.shape[1] - own_rows
    flat = [(ref, i) for ref in grad_refs for i in range(ref.shape[0])]

    @pl.when(pl.program_id(0) == 0)
    def _():
        base = 0
        for begin in range(0, len(flat), 2):
            sums = []
            for ref, i in flat[begin : begin + 2]:
                stat = ref[i, SHARED:, :].astype(F32)
                sums.append(
                    (
                        stat[:, 0:SHARED] + stat[:, SHARED : 2 * SHARED],
                        stat[:, 2 * SHARED : 3 * SHARED] + stat[:, 3 * SHARED :],
                    )
                )
            for kind in range(2):
                stats_ref[kind, :, base : base + 2 * SHARED] = jnp.concatenate([s[kind] for s in sums], axis=1)
            base += 2 * SHARED

    base = 0
    there = pl.ds(pl.multiple_of(pair * PAIR, PAIR), PAIR)
    for ref, i in flat:
        grads_ref[base : base + SHARED, :] = ref[i, 0:SHARED, there]
        base += SHARED
    idc = idc_ref[...]
    allowed = twice((idc == idr_ref[...]) & (idc != 0))
    shared_row = idc == 0
    live = live_ref[0:1, 0:1] > 0.5
    kv = kvown_ref[0]
    k_all, v_all = kv[:, 0:PAIR], kv[:, PAIR:]
    in_shared = lambda x: jnp.concatenate([x[0:SHARED], x[own_rows:]], axis=0)
    q, grad = q_ref[0], pair_lanes(grad_ref, pair)
    n_shared = SHARED + rim
    k_sh, v_sh = stack_heads(in_shared(k_all)), stack_heads(in_shared(v_all))

    def both_rows(ref, kind, rows, columns):
        picked = [ref[kind, pl.ds(2 * pair + head, 1), columns] for head in range(2)]
        return jnp.concatenate([jnp.broadcast_to(p, (rows, p.shape[1])) for p in picked], axis=0)

    dk = dv = None
    chunk = min(base, 1536)
    for start in range(0, base, chunk):
        span = slice(start, start + chunk)
        q_all, g_all = qall_ref[0, span, :], grads_ref[span, :]
        probs = jnp.exp(dot_nt(k_sh, q_all) - both_rows(stats_ref, 0, n_shared, span))
        part_v = dot(probs.astype(BF16), g_all)
        ds = (probs * (dot_nt(v_sh, g_all) - both_rows(stats_ref, 1, n_shared, span))).astype(BF16)
        part_k = dot(ds, q_all)
        dk = part_k if dk is None else dk + part_k
        dv = part_v if dv is None else dv + part_v
    every = slice(None)
    scores = dot_nt(stack_heads(k_all[0:own_rows]), q) - both_rows(own_stat_ref, 0, own_rows, every)
    probs = jnp.exp(jnp.where(allowed, scores, NEG))
    local_v = dot(probs.astype(BF16), grad)
    ds = dot_nt(stack_heads(v_all[0:own_rows]), grad) - both_rows(own_stat_ref, 1, own_rows, every)
    local_k = dot((probs * ds).astype(BF16), q)
    here = pl.ds(pl.multiple_of(pl.program_id(0) * PAIR, PAIR), PAIR)
    for out, shared, local in ((dk_ref, dk, local_k), (dv_ref, dv, local_v)):
        shared, local = unstack_heads(shared), unstack_heads(local)
        out[0:SHARED, here] = jnp.where(shared_row[0:SHARED], shared[0:SHARED], local[0:SHARED]).astype(BF16)
        out[SHARED:own_rows, here] = local[SHARED:].astype(BF16)
        out[own_rows:, here] = jnp.where(live, shared[SHARED:], 0.0).astype(BF16)


def key_back(groups, kvown, qall, q, mixed_grad, own_stats, idc, idr, live, first, pairs, after):
    joined_rows = kvown.shape[1]
    grads = [g for group in groups for g in group]
    ins = [fixed(g) for g in grads] + [lead(kvown, first), lead(qall), lead(q, first)]
    ins += [fixed(x) for x in (mixed_grad, own_stats, idc, idr, live)]
    out = (sds((joined_rows, pairs * PAIR), BF16), pl.BlockSpec((joined_rows, pairs * PAIR), lambda h: (0, 0)))
    scratch = [pltpu.VMEM((qall.shape[1], PAIR), BF16), pltpu.VMEM((2, MARKS, qall.shape[1]), F32)]
    kernel = functools.partial(key_kernel, len(grads), first)
    return call(kernel, ins, [out, out], "key_back", grid=(pairs,), scratch=scratch, cost=3.7 * pairs, after=after)


def input_kernel(dq, dk, dv, weight, stream, arrived, gain, attn_grad, rim_ref, rows_ref, joint_ref, vec_ref):
    own, width = dq.shape
    dq, dk, dv = dq[...], dk[...], dv[...]
    wq, wk, wv = weight[:, 0:width], weight[:, width : 2 * width], weight[:, 2 * width :]
    rim_grad = dot_nt(dk[own:], wk) + dot_nt(dv[own:], wv)
    rim_rows, rim_scale = normalise(arrived[...].astype(F32))
    rim_back, rim_gain, rim_bias = norm_back(rim_grad, rim_rows, rim_scale, gain[...])
    rim_ref[...] = rim_back.astype(BF16)
    own_grad = dot_nt(dq, wq) + dot_nt(dk[:own], wk) + dot_nt(dv[:own], wv)
    own_rows, own_scale = normalise(stream[...])
    own_back, own_gain, own_bias = norm_back(own_grad, own_rows, own_scale, gain[...])
    rows_ref[...] = own_back + attn_grad[...]
    joint_ref[0:own, 0:width] = dq
    joint_ref[own:, 0:width] = jnp.zeros((dk.shape[0] - own, width), BF16)
    joint_ref[:, width : 2 * width] = dk
    joint_ref[:, 2 * width :] = dv
    vec_ref[0:1, :] = own_gain + rim_gain
    vec_ref[1:2, :] = own_bias + rim_bias
    vec_ref[2:3, :] = jnp.sum(dq.astype(F32), axis=0, keepdims=True)
    vec_ref[3:4, :] = jnp.sum(dv.astype(F32), axis=0, keepdims=True)


def pixel_kernel(rows, returned, halo, weight, low_ref, grad_ref):
    place = lax.broadcasted_iota(jnp.int32, (rows.shape[0], halo.shape[1]), 0)
    spread = jnp.where(place == halo[...], 1.0, 0.0).astype(BF16)
    low = (rows[...] + dot(spread, returned[...])).astype(BF16)
    low_ref[...] = low
    grad_ref[...] = dot_nt(low, weight[...]).astype(BF16)


ORDERS = {
    "x": [("gx", 2, None), ("gy", 1, 2), ("gy", 2, 1), ("gy", 4, 0)],
    "y": [("gy", 1, None), ("gy", 2, 1), ("gy", 4, 0)],
    "z": [("gy", 2, None), ("gy", 4, 0), ("gy", 1, 0)],
    "s": [("gy", 1, None)],
    "yx": [("gy", 1, None), ("gx", 2, 2), ("gy", 2, 1), ("gy", 4, 0)],
}


def product_blocks(left, right, core_half, n):
    half = right.shape[1] // 2
    x = left[...]
    for j in range(half // LANES):
        columns = pl.ds(pl.multiple_of(core_half * half + j * LANES, 128), LANES)
        out = dot_tn(x, right[:, columns])
        yield out.reshape(n, out.shape[0] // n, LANES)


def away_kernel(n, n_pairs, *refs):
    pairs, outs = refs[: 2 * n_pairs], refs[2 * n_pairs :]
    other = 1 - lax.axis_index("gx") % 2
    (out,) = outs
    row = 0
    for p in range(n_pairs):
        for block in product_blocks(pairs[2 * p], pairs[2 * p + 1], other, n):
            out[:, row : row + block.shape[1], :] = block.astype(BF16)
            row += block.shape[1]


def home_kernel(n, n_pairs, order, n_small, row, *refs):
    pairs = refs[: 2 * n_pairs]
    arrived = refs[2 * n_pairs]
    small = refs[2 * n_pairs + 1 : 2 * n_pairs + 1 + n_small]
    send, keep = refs[2 * n_pairs + 1 + n_small :][-2:] if order != "s" else (None, refs[-1])
    core = lax.axis_index("gx") % 2
    axis, bit = ORDERS[order][0][:2]
    low = lax.axis_index(axis) // bit % 2 == 0
    half_row = 0

    def put(first, second, start, rows):
        if order == "s":
            for half, value in ((0, first), (1, second)):
                keep[:, half, start : start + rows, :] = value
            return
        if order == "x":
            span = slice(start, start + rows)
            send[:, span, :] = jnp.where(low, second, first)
            keep[:, span, :] = jnp.where(low, first, second)
            return
        for half, value in ((0, first), (1, second)):
            span = slice(start, start + rows)
            value = value.reshape(n // 2 // bit, 2, bit, rows, LANES)
            for out, one, other in ((send, value[:, 1], value[:, 0]), (keep, value[:, 0], value[:, 1])):
                out[:, half, span, :] = jnp.where(low, one, other).reshape(n // 2, rows, LANES)

    for p in range(n_pairs):
        for block in product_blocks(pairs[2 * p], pairs[2 * p + 1], core, n):
            r = block.shape[1]
            block = (block + arrived[:, row : row + r, :].astype(F32)).astype(BF16)
            put(block[:, : r // 2], block[:, r // 2 :], half_row, r // 2)
            row += r
            half_row += r // 2
    if n_small:
        value = small[0][...] + small[1][...]
        put(value, jnp.zeros(value.shape, BF16), half_row, value.shape[1])


def away(pairs, n, name, after=()):
    arrays = [x for pair in pairs for x in pair]
    rows = sum(b.shape[1] // 2 // LANES * a.shape[1] // n for a, b in pairs)
    outs = [(sds((n, rows, LANES), BF16), VMEM)]
    return call(functools.partial(away_kernel, n, len(pairs)), plain(*arrays), outs, name, cost=rows / 135.0, after=after)[0]


def home(pairs, n, arrived, order, name, small=(), first_row=0, after=()):
    arrays = [x for pair in pairs for x in pair] + [arrived] + list(small)
    rows = sum(b.shape[1] // 2 // LANES * a.shape[1] // n // 2 for a, b in pairs)
    rows += small[0].shape[1] if small else 0
    shape = (n, rows, LANES) if order == "x" else (n // 2, 2, rows, LANES)
    kernel = functools.partial(home_kernel, n, len(pairs), order, len(small), first_row)
    if order == "s":
        outs = [(sds((n, 2, rows, LANES), BF16), VMEM)]
        whole = call(kernel, plain(*arrays), outs, name, after=after)[0]
        return whole, lax.psum_scatter(whole, "gy", scatter_dimension=0, tiled=False)
    outs = [(sds(shape, BF16), VMEM)] * 2
    send, keep = call(kernel, plain(*arrays), outs, name, after=after)
    got = swap(send, *ORDERS[order][0][:2])
    shape = ((2, 2, 2) if order == "x" else (2, 2)) + keep.shape[1:]
    return send, (keep.reshape(shape), got.reshape(shape))


def next_step(group, axis, bit, dim):
    keep, got = group
    mine = bit_of(axis, bit)
    pick = lambda x, i: lax.dynamic_index_in_dim(x, i, dim, keepdims=False)
    send = pick(keep, 1 - mine) + pick(got, 1 - mine)
    return send, (pick(keep, mine) + pick(got, mine), swap(send, axis, bit))


def held_step(group, axis, bit, dim, after):
    keep, got = group
    shape = keep.shape[:dim] + keep.shape[dim + 1 :]

    def kernel(keep, got, send, left):
        mine = lax.axis_index(axis) // bit % 2
        for out, side in ((send, 1 - mine), (left, mine)):
            index = (slice(None),) * dim + (side,)
            out[...] = keep[index] + got[index]

    send, left = call(kernel, plain(keep, got), [(sds(shape, BF16), VMEM)] * 2, "step", after=after)
    return send, (left, swap(send, axis, bit))


def all_of(group):
    part = group[0] + group[1] if isinstance(group, tuple) else group
    x_low, core_low = bit_of("gx", 2) == 0, bit_of("gx", 1) == 0
    over = swap(part, "gx", 2)
    if part.ndim == 3:
        both = part + over
    else:
        both = jnp.stack([jnp.where(x_low, part, over), jnp.where(x_low, over, part)])
    across = swap(both, "gx", 1)
    return [jnp.where(core_low, both, across), jnp.where(core_low, across, both)]


def cut(sides, pairs, n):
    outs, start = [], 0
    for a, b in pairs:
        r, blocks = a.shape[1] // n, b.shape[1] // 2 // LANES
        halves = []
        for side in sides:
            piece = side[:, start : start + blocks * r // 2].reshape(2, blocks, r // 2, LANES)
            halves.append(piece.transpose(0, 2, 1, 3).reshape(r, blocks * LANES))
        start += blocks * r // 2
        outs.append(jnp.concatenate(halves, axis=1).astype(F32))
    return outs, [side[0, start:].astype(F32) for side in sides]


def shards(
    pixels,
    frame_index,
    patch_cell,
    tile_id,
    halo_index,
    w_patch,
    first_gain,
    first_bias,
    w_project,
    project_bias,
    w_output,
    merge_bias,
    second_gain,
    second_bias,
    w_up,
    up_bias,
    w_down,
    down_bias,
    w_head,
    cotangent,
):
    n_gx, n_gy = lax.axis_size("gx"), lax.axis_size("gy")
    own, rim = pixels.shape[0], halo_index.shape[0]
    width, hidden, depth = w_output.shape[0], w_up.shape[1], pixels.shape[1]
    key_rows = SHARED + rim
    idc, idr = tile_id.reshape(own, 1), tile_id.reshape(1, own)
    live = jnp.broadcast_to(jnp.where(lax.axis_index("gx") > 0, 1.0, 0.0).astype(F32), (8, 128))
    halo = halo_index.reshape(1, rim)
    row = lambda v: v.reshape(1, -1)
    mat = lambda rows, columns, dtype: (sds((rows, columns), dtype), VMEM)

    high, low = position_table(width)
    stream, outgoing, own_low = call(
        embed_kernel,
        plain(
            pixels, w_patch, row(frame_index), patch_cell, halo, high, low, row(first_gain), row(first_bias)
        ),
        [mat(own, width, F32), mat(rim, width, BF16), mat(own, width, BF16)],
        "embed",
    )
    arrived = shifted(outgoing, "gx", 1)
    unit, first_low = call(
        unit_kernel,
        plain(own_low, arrived, row(first_gain), row(first_bias), idr, live),
        [mat(key_rows + MARKS, width, BF16), mat(own + rim, width, BF16)],
        "unit",
        cost=2.4,
    )
    column = ColumnGather(unit)
    shift = row(project_bias)
    attention = Attention(first_low, w_project, shift, idc, idr, key_rows)
    if column.direct:
        column.second()
        if CFG["early"]:
            after = attention.piece([unit[None], column.near[None]], False)
            column.third(after)
            column.fourth((column.far,))
            attention.piece(column.groups[1], False)
            attention.piece(column.groups[2], True)
        else:
            after = attention.piece([unit[None], column.near[None], column.y0[None]], False)
            column.third(after)
            after = attention.piece([column.y1[None], column.far[None]], False)
            column.fourth(after)
            attention.piece([column.last[None], column.y2[None], column.y3[None]], True)
    else:
        attention.piece(column.groups[0], True)
    groups, kvs, kvown, q = column.groups, attention.kvs, attention.kvown, attention.q
    mixed, lse = attention.state

    mlp_grad = dot_nt(cotangent, w_head)
    down_bias_grad = jnp.sum(mlp_grad, axis=0)
    mlp_low = mlp_grad.astype(BF16)
    act_grad = dot_nt(mlp_low, w_down)
    (
        predicted, act_low, pre_grad, second_low, mixed_low, attn_low, final_low, attn_grad, mixed_grad, grad_unit,
        own_stats, up_sum, second_gain_sum, second_bias_sum, merge_sum,
    ) = call(
        middle_kernel,
        plain(
            mixed, lse, stream, mlp_grad, act_grad, idc, w_output, row(merge_bias), row(second_gain),
            row(second_bias), w_up, row(up_bias), w_down, row(down_bias), w_head,
        ),
        [mat(own, depth, BF16), mat(own, hidden, BF16), mat(own, hidden, BF16)]
        + [mat(own, width, BF16)] * 4
        + [mat(own, width, F32), mat(own, width, BF16), mat(SHARED + MARKS, width, BF16)]
        + [(sds((2, MARKS, own), F32), VMEM), mat(1, hidden, F32)]
        + [mat(1, width, F32)] * 3,
        "middle",
        cost=18.0,
    )
    special = n_gx == 4 and n_gy == 8
    head_pair, down_pair = (final_low, cotangent), (act_low, mlp_low)
    up_pair, output_pair = (second_low, pre_grad), (mixed_low, attn_low)
    gather = (DirectGather if CFG["direct"] else FreeGather)(grad_unit)
    early_a, early_b = [head_pair, down_pair], [up_pair, output_pair]
    q_parts, k_parts = [], []

    def query_piece(first, pairs, after):
        part = query_back(
            groups, kvs, kvown, q, mixed_grad, mixed, lse, w_project, shift, idc, idr, key_rows, first, pairs, after
        )
        q_parts.append(part)
        return (part[0],)

    def key_piece(place, first, pairs, after):
        qall = jnp.concatenate([p[1] for p in q_parts], axis=0) if CFG["qp"] != CFG["kp"] else q_parts[place][1]
        part = key_back(gather.groups, kvown, qall, q, mixed_grad, own_stats, idc, idr, live, first, pairs, after)
        k_parts.append(part)
        return (part[0],)

    after = ()
    if special:
        if CFG["merged"]:
            share_a = share_b = away(early_a + early_b, n_gy, "away")
            gone_a = gone_b = swap(share_a, "gx", 1)
        else:
            share_a, share_b = away(early_a, n_gy, "away"), away(early_b, n_gy, "away")
            gone_a, gone_b = swap(share_a, "gx", 1), swap(share_b, "gx", 1)
        after = (share_a, share_b) if CFG["away_first"] else ()

    def homes(after):
        gate = CFG["gate"]
        if gate >= 1:
            after += (gather.near, gather.mid, gather.y0)
        if gate >= 3:
            after += (gather.far_end, gather.far_mid, gather.y1)
        if CFG["sc"]:
            send, group = home(early_a + early_b, n_gy, gone_a, "s", "home", after=after)
            return (send,), group, None
        send_a, group_a = home(early_a, n_gy, gone_a, "x", "home", after=after)
        after += (send_a,)
        if gate >= 2:
            after += (gather.far_end, gather.far_mid, gather.y1)
        if gate >= 3:
            after += (gather.last_end, gather.y2)
        first_row = 2 * group_a[0].shape[-2] if CFG["merged"] else 0
        send_b, group_b = home(early_b, n_gy, gone_b, CFG["b"], "home", first_row=first_row, after=after)
        return (send_a, send_b), group_a, group_b

    def second_steps(group_a, group_b, after):
        send_a, group_a = held_step(group_a, *ORDERS["x"][1], after)
        send_b, group_b = held_step(group_b, *ORDERS[CFG["b"]][1], after + (send_a,))
        return (send_a, send_b), group_a, group_b

    done_a = done_b = 1
    first = 0
    for i, size in enumerate(CFG["qp"]):
        after = query_piece(first, size, after)
        first += size
        if special and CFG["home"] == i:
            more, group_a, group_b = homes(after)
            after += more
    first = 0
    for i, size in enumerate(CFG["kp"]):
        part = key_piece(i, first, size, after)
        after = part
        first += size
        if special and CFG["ab2"] == i:
            more, group_a, group_b = second_steps(group_a, group_b, after)
            after += more
            done_a = done_b = 2
    dq = jnp.concatenate([p[0] for p in q_parts], axis=1)
    dk = jnp.concatenate([p[0] for p in k_parts], axis=1)
    dv = jnp.concatenate([p[1] for p in k_parts], axis=1)
    rim_grad, partial, joint_grad, first_sums = call(
        input_kernel,
        plain(dq, dk, dv, w_project, stream, arrived, row(first_gain), attn_grad),
        [mat(rim, width, BF16), mat(own, width, F32), mat(own + rim, 3 * width, BF16), mat(8, width, F32)],
        "input",
        cost=6.0,
        after=after,
    )
    returned = shifted(rim_grad, "gx", -1)
    project_pair = (first_low, joint_grad)
    after = ()
    if special:
        share_c = away([project_pair], n_gy, "away")
        gone_c = swap(share_c, "gx", 1)
        after = ()
        if CFG["ab2"] == "c":
            after, group_a, group_b = second_steps(group_a, group_b, (share_c,))
            done_a = done_b = 2
    embed_low, pixel_grad = call(
        pixel_kernel,
        plain(partial, returned, halo, w_patch),
        [mat(own, width, BF16), mat(own, depth, BF16)],
        "pixel",
        cost=3.0,
        after=after if special else (),
    )
    patch_pair = (pixels, embed_low)

    vectors = [
        first_sums[0],
        first_sums[1],
        first_sums[2:4].reshape(-1),
        merge_sum[0],
        second_gain_sum[0],
        second_bias_sum[0],
        up_sum[0],
        down_bias_grad,
    ]
    sizes = [v.shape[0] // n_gy for v in vectors]
    if special:
        core = bit_of("gx", 1)
        small = jnp.stack([jnp.pad(v.reshape(n_gy, z), ((0, 0), (0, LANES - z))) for v, z in zip(vectors, sizes)], axis=1)
        small = jnp.pad(small.astype(BF16).reshape(n_gy, 2, 4, LANES), ((0, 0), (0, 0), (0, MARKS - 4), (0, 0)))
        small_mine = lax.dynamic_index_in_dim(small, core, 1, keepdims=False)
        small_gone = swap(lax.dynamic_index_in_dim(small, 1 - core, 1, keepdims=False), "gx", 1)
        share_d = away([patch_pair], n_gy, "away")
        gone_d = swap(share_d, "gx", 1)
        send_c, group_c = home([project_pair], n_gy, gone_c, CFG["c"], "home", after=(share_d,) if CFG["chain"] else ())
        send_d, group_d = home(
            [patch_pair], n_gy, gone_d, CFG["d"], "home", small=[small_mine, small_gone], after=(send_c,) if CFG["chain"] else ()
        )
        if CFG["ab3"] and done_a == 2:
            send_a, group_a = held_step(group_a, *ORDERS["x"][2], (send_d,))
            send_b, group_b = held_step(group_b, *ORDERS[CFG["b"]][2], (send_d,))
            done_a = done_b = 3
        if CFG["join"]:

            def joined(groups, orders):
                groups = [next_step(group, *ORDERS[order][1])[1] for group, order in zip(groups, orders)]
                for axis, bit, dim in ORDERS["x"][2:]:
                    mine = bit_of(axis, bit)
                    pick = lambda x, i: lax.dynamic_index_in_dim(x, i, dim, keepdims=False)
                    put = lambda i: jnp.concatenate([pick(k, i) + pick(g, i) for k, g in groups], axis=-2)
                    groups = [(put(mine), swap(put(1 - mine), axis, bit))]
                return all_of(groups[0])

            sides = joined([group_a, group_b], ["x", CFG["b"]])
            (head_grad, down_grad, up_grad, output_grad), _ = cut(sides, early_a + early_b, n_gy)
            sides = joined([group_c, group_d], [CFG["c"], CFG["d"]])
            (project_grad, patch_grad), marks = cut(sides, [project_pair, patch_pair], n_gy)
            groups = None
        else:
            groups = []
            for group, hops in (
                *(((group_a, ()),) if CFG["sc"] else ((group_a, ORDERS["x"][done_a:]), (group_b, ORDERS[CFG["b"]][done_b:]))),
                (group_c, ORDERS[CFG["c"]][1:]),
                (group_d, ORDERS[CFG["d"]][1:]),
            ):
                for hop in hops:
                    _, group = next_step(group, *hop)
                groups.append(all_of(group))
        if groups is None:
            pass
        elif CFG["sc"]:
            groups.insert(0, None)
            (head_grad, down_grad, up_grad, output_grad), _ = cut(groups[1], early_a + early_b, n_gy)
        else:
            (head_grad, down_grad), _ = cut(groups[0], early_a, n_gy)
            (up_grad, output_grad), _ = cut(groups[1], early_b, n_gy)
        if groups is not None:
            (project_grad,), _ = cut(groups[2], [project_pair], n_gy)
            (patch_grad,), marks = cut(groups[3], [patch_pair], n_gy)
        small_outs = [marks[i // 4][i % 4, :size] for i, size in enumerate(sizes)]
    else:

        def total(x):
            part = lax.psum_scatter(x.astype(BF16), "gy", scatter_dimension=0, tiled=True)
            return lax.psum(part, "gx").astype(F32)

        pairs = [head_pair, down_pair, up_pair, output_pair, project_pair, patch_pair]
        head_grad, down_grad, up_grad, output_grad, project_grad, patch_grad = [total(dot_tn(a, b)) for a, b in pairs]
        tail = total(jnp.concatenate([v.reshape(n_gy, -1) for v in vectors], axis=1)).reshape(-1)
        starts = [sum(sizes[:i]) for i in range(len(sizes))]
        small_outs = [tail[s : s + z] for s, z in zip(starts, sizes)]
    return (
        predicted,
        pixel_grad,
        patch_grad,
        small_outs[0],
        small_outs[1],
        project_grad,
        small_outs[2],
        output_grad,
        small_outs[3],
        small_outs[4],
        small_outs[5],
        up_grad,
        small_outs[6],
        down_grad,
        small_outs[7],
        head_grad,
    )


def solution(mesh):
    tokens = P(("gx", "gy"))
    rows = P(("gx", "gy"), None)
    in_specs = (rows, tokens, P(None, ("gx", "gy")), tokens, tokens) + (P(),) * 14 + (rows,)
    matrix, vector = P("gy", None), P("gy")
    out_specs = (
        rows,
        rows,
        matrix,
        vector,
        vector,
        matrix,
        vector,
        matrix,
        vector,
        vector,
        vector,
        matrix,
        vector,
        matrix,
        vector,
        matrix,
    )
    return jax.shard_map(shards, mesh=mesh, in_specs=in_specs, out_specs=out_specs, check_vma=False)
```

time: 381 us -> 366 us (0.961)
  waiting for transfers between devices: 93.2 us -> 83.8 us
  Pallas kernels: 168 us -> 162 us
  starting transfers between devices: 60.9 us -> 65.2 us
    ppermute x10, waiting for transfers between devices: 36.8 us -> 16.4 us  [along(): lax.ppermute(x, 'gy', [(2 * a + y, 2 * b + y) for a, b in hops for y in (...]
    ppermute x37 -> x36, waiting for transfers between devices: 55.2 us -> 66.1 us  [swap(): return lax.ppermute(x, axis, [(i, i ^ bit) for i in range(length)])]
    pallas_call x22, Pallas kernels: 168 us -> 162 us  [call(): pl.pallas_call(body, grid=grid or (), in_specs=specs, out_specs=tuple((sp...]
    ppermute x10, starting transfers between devices: 12.1 us -> 18 us  [along(): lax.ppermute(x, 'gy', [(2 * a + y, 2 * b + y) for a, b in hops for y in (...]
    unnamed x102 -> x81, local copies, waits for them, and re-layouts: 7.65 us -> 3.93 us
    ppermute x37 -> x36, starting transfers between devices: 45.2 us -> 43.6 us  [swap(): return lax.ppermute(x, axis, [(i, i ^ bit) for i in range(length)])]
    add x18 -> x17, other arithmetic: 13.4 us -> 13 us  [the longest x7 11.7 us: next_step(): return (send, (pick(keep, mine) + pick(got, mine), swap(send, axis, bit)))]
  transfers between devices with their start and end apart: 49 -> 48, of which waited for: 22 -> 18; matrix products, arithmetic and copies ran while one was open for 9% -> 10% of each run, Pallas kernels for 26% -> 25%
where the time goes in v3:
time: 366 us; the launch traced here: 358 us
  Pallas kernels  162 us (44%)
  waiting for transfers between devices  83.8 us (23%)
  starting transfers between devices  65.2 us (18%)
  other arithmetic  25.6 us (7%)
  local copies, waits for them, and re-layouts  15.3 us (4%)
  matrix products  4.76 us (1%)
    pallas_call x22, Pallas kernels, call(): pl.pallas_call(body, grid=grid or (), in_specs=specs, out_specs=tuple((sp...  162 us
    ppermute x36, waiting for transfers between devices, swap(): return lax.ppermute(x, axis, [(i, i ^ bit) for i in range(length)])  66.1 us
    ppermute x36, starting transfers between devices, swap(): return lax.ppermute(x, axis, [(i, i ^ bit) for i in range(length)])  43.6 us
    ppermute x10, starting transfers between devices, along(): lax.ppermute(x, 'gy', [(2 * a + y, 2 * b + y) for a, b in hops for y in (...  18 us
    ppermute x10, waiting for transfers between devices, along(): lax.ppermute(x, 'gy', [(2 * a + y, 2 * b + y) for a, b in hops for y in (...  16.4 us
    add x7, other arithmetic, next_step(): return (send, (pick(keep, mine) + pick(got, mine), swap(send, axis, bit)))  11.7 us
  transfers between devices with their start and end apart: 48, of which 18 were waited for; matrix products, arithmetic and copies ran while one was open for 10% of the time, Pallas kernels for 25%

profile of v3, /device:TPU:0, one launch (start us, length us, event | category | flops | bytes accessed | tf_op | source)
XLA Modules:
  0.0 358.4 jit_solution(14283802344863523543)
XLA Ops:
  3.2 4.1 %embed.1 = (f32[256,768]{1,0:T(8,128)}, bf16[128,768]{1,0:T(8,128)(2,1)}, bf16[256,768]{1,0:T(8,128)(2,1)}) custom-call(bf16[256,1536]{1,0:T(8,128)(2,1)} %refs_0_.5, bf16[1536,768]{1,0:T(8,128)(2,1)} %refs_3_.11, s32[1,256]{1,0:T(1,128)} %bitcast.267, s32[2,256]{1,0:T(2,128)} %refs_3_.6, s32[1,128]{1,0:T(1,128)} %bitcast.265, ...), custom_call_target="tpu_custom_call" | custom-call | flops 400000000 | bytes 1200000 | tf_op jit(solution)/shard_map/embed/pallas_call | solution.py:156
  7.3 2.4 collective-permute-start
  11.6 2.4 unit.1
  14.0 2.4 collective-permute-start.1
  17.1 9.2 %collective-permute-done.1 = bf16[336,768]{1,0:T(8,128)(2,1)S(1)} collective-permute-done((bf16[336,768]{1,0:T(8,128)(2,1)}, bf16[336,768]{1,0:T(8,128)(2,1)S(1)}, u32[]{:S(2)}, u32[]{:S(2)}) %collective-permute-start.1) | collective-permute-done | bytes 516128 | tf_op jit(solution)/shard_map/ppermute | solution.py:74
  26.3 1.5 collective-permute-start.2
  27.8 2.3 collective-permute-start.7
  34.2 7.0 %collective-permute-done.7 = bf16[336,768]{1,0:T(8,128)(2,1)S(1)} collective-permute-done((bf16[336,768]{1,0:T(8,128)(2,1)}, bf16[336,768]{1,0:T(8,128)(2,1)S(1)}, u32[]{:S(2)}, u32[]{:S(2)}) %collective-permute-start.7) | collective-permute-done | bytes 516128 | tf_op jit(solution)/shard_map/ppermute | solution.py:53
  42.1 15.1 %attend.3 = (bf16[6,960,256]{2,1,0:T(8,128)(2,1)}, bf16[6,256,128]{2,1,0:T(8,128)(2,1)}, bf16[6,384,256]{2,1,0:T(8,128)(2,1)}, f32[256,768]{1,0:T(8,128)}, f32[2...) custom-call(bf16[1,336,768]{2,1,0:T(8,128)(2,1)} %bitcast.215, bf16[1,336,768]{2,1,0:T(8,128)(2,1)} %bitcast.218, ...), custom_call_target="tpu_custom_call" | custom-call | flops 1366666624 | bytes 4100000 | tf_op jit(solution)/shard_map/attend/pallas_call | solution.py:156
  58.0 2.2 choose.2
  60.2 2.3 collective-permute-start.8
  63.3 9.3 %attend.4 = (bf16[6,640,256]{2,1,0:T(8,128)(2,1)}, f32[6,128,384]{2,1,0:T(8,128)}, f32[6,16,384]{2,1,0:T(8,128)}) custom-call(bf16[1,336,768]{2,1,0:T(8,128)(2,1)} %bitcast.212, bf16[1,336,768]{2,1,0:T(8,128)(2,1)} %bitcast.206, bf16[768,2304]{1,0:T(8,128)(2,1)} %refs_3_.10, bf16[768,2304]{1,0:T(8,128)(2,1)} %refs_3_.10, ...), custom_call_target="tpu_custom_call" | custom-call | flops 1011111104 | bytes 3033333 | tf_op jit(solution)/shard_map/attend/pallas_call | solution.py:156
  72.7 2.2 choose.3
  75.0 1.7 fusion.10
  79.1 3.1 fusion.11.refs_4_
  82.2 5.9 %collective-permute-done.9 = bf16[336,768]{1,0:T(8,128)(2,1)} collective-permute-done((bf16[336,768]{1,0:T(8,128)(2,1)}, bf16[336,768]{1,0:T(8,128)(2,1)}, u32[]{:S(2)}, u32[]{:S(2)}) %collective-permute-start.9) | collective-permute-done | bytes 516128 | tf_op jit(solution)/shard_map/ppermute | solution.py:53
  88.1 13.4 %attend.5 = (bf16[6,960,256]{2,1,0:T(8,128)(2,1)}, f32[256,768]{1,0:T(8,128)}, f32[256,768]{1,0:T(8,128)}) custom-call(bf16[1,336,768]{2,1,0:T(8,128)(2,1)} %bitcast.209, bf16[1,336,768]{2,1,0:T(8,128)(2,1)} %bitcast.10.refs_1_.refs_6_, bf16[1,336,768]{2,1,0:T(8,128)(2,1)} %bitcast.11.refs_2_.refs_7_, bf16[768,2304]{1,0:T(8,128)(2,1)} %refs_3_.10, ...), custom_call_target="tpu_custom_call" | custom-call | flops 1366666624 | bytes 4100000 | tf_op jit(solution)/shard_map/attend/pallas_call | solution.py:156
  101.5 18.0 %middle.1 = (bf16[256,1536]{1,0:T(8,128)(2,1)}, bf16[256,3072]{1,0:T(8,128)(2,1)}, bf16[256,3072]{1,0:T(8,128)(2,1)}, bf16[256,768]{1,0:T(8,128)(2,1)}, bf16[256...) custom-call(f32[256,768]{1,0:T(8,128)} %get-tuple-element.82.refs_0_, ...), custom_call_target="tpu_custom_call" | custom-call | flops 1800000000 | bytes 5400000 | tf_op jit(solution)/shard_map/middle/pallas_call | solution.py:156
  119.5 5.0 %away.4.refs_20_ = bf16[8,576,384]{2,1,0:T(8,128)(2,1)} custom-call(bf16[256,768]{1,0:T(8,128)(2,1)} %get-tuple-element.91.refs_0_, bf16[256,1536]{1,0:T(8,128)(2,1)} %refs_1_.5, bf16[256,3072]{1,0:T(8,128)(2,1)} %get-tuple-element.92.refs_2_, bf16[256,768]{1,0:T(8,128)(2,1)} %copy-done.3), custom_call_target="tpu_custom_call" | custom-call | flops 426666656 | bytes 1280000 | tf_op jit(solution)/shard_map/away/pallas_call | solution.py:156
  124.6 1.7 collective-permute-start.19
  126.2 5.0 %away.5.refs_21_ = bf16[8,480,384]{2,1,0:T(8,128)(2,1)} custom-call(bf16[256,768]{1,0:T(8,128)(2,1)} %get-tuple-element.93.refs_0_, bf16[256,3072]{1,0:T(8,128)(2,1)} %get-tuple-element.94.refs_1_, bf16[256,768]{1,0:T(8,128)(2,1)} %get-tuple-element.95.refs_2_, bf16[256,768]{1,0:T(8,128)(2,1)} %get-tuple-element.96.refs_3_), custom_call_target="tpu_custom_call" | custom-call | flops 355555552 | bytes 1066666 | tf_op jit(solution)/shard_map/away/pallas_call | solution.py:156
  131.3 5.5 %collective-permute-start.10 = (bf16[208,768]{1,0:T(8,128)(2,1)S(1)}, bf16[208,768]{1,0:T(8,128)(2,1)}, u32[]{:S(2)}, u32[]{:S(2)}) collective-permute-start(bf16[208,768]{1,0:T(8,128)(2,1)S(1)} %copy-done.9), channel_id=1, source_target_pairs={{0,2},{1,3},{2,0},{3,1},{4,6},{5,7},{6,4},{7,5},{8,10},{9,11},{10,... | collective-permute-start | bytes 958472 | tf_op jit(solution)/shard_map/ppermute | solution.py:74
  136.8 1.4 collective-permute-start.13
  138.2 6.6 %collective-permute-done.10 = bf16[208,768]{1,0:T(8,128)(2,1)} collective-permute-done((bf16[208,768]{1,0:T(8,128)(2,1)S(1)}, bf16[208,768]{1,0:T(8,128)(2,1)}, u32[]{:S(2)}, u32[]{:S(2)}) %collective-permute-start.10) | collective-permute-done | bytes 319520 | tf_op jit(solution)/shard_map/ppermute | solution.py:74
  144.8 1.4 collective-permute-start.15
  149.4 12.8 %query_back.2 = (bf16[256,384]{1,0:T(8,128)(2,1)}, bf16[3,1536,128]{2,1,0:T(8,128)(2,1)}) custom-call(bf16[1,336,768]{2,1,0:T(8,128)(2,1)} %bitcast.216, bf16[1,336,768]{2,1,0:T(8,128)(2,1)} %bitcast.219, bf16[1,336,768]{2,1,0:T(8,128)(2,1)} %bitcast.222, bf16[1,336,768]{2,1,0:T(8,128)(2,1)} %bitcast.213, bf16[1,336,768]{2,1,0:T(8,128)(2,1)} %bitcast.207, ...), custom_call_target="tpu_custom_call" | custom-call | flops 1260000000 | bytes 3780000 | tf_op jit(solution)/shard_map/query_back/pallas_call | solution.py:156
  162.2 1.6 collective-permute-start.12
  163.7 1.7 broadcast_select_fusion.5
  167.3 1.5 collective-permute-start.18
  168.9 12.8 %query_back.3 = (bf16[256,384]{1,0:T(8,128)(2,1)}, bf16[3,1536,128]{2,1,0:T(8,128)(2,1)}) custom-call(bf16[1,336,768]{2,1,0:T(8,128)(2,1)} %bitcast.217, bf16[1,336,768]{2,1,0:T(8,128)(2,1)} %bitcast.220, bf16[1,336,768]{2,1,0:T(8,128)(2,1)} %bitcast.223, bf16[1,336,768]{2,1,0:T(8,128)(2,1)} %bitcast.214, bf16[1,336,768]{2,1,0:T(8,128)(2,1)} %bitcast.208, ...), custom_call_target="tpu_custom_call" | custom-call | flops 1260000000 | bytes 3780000 | tf_op jit(solution)/shard_map/query_back/pallas_call | solution.py:156
  181.7 1.7 pad_maximum_fusion.3.refs_0_
  183.4 6.2 %home.4 = (bf16[8,288,384]{2,1,0:T(8,128)(2,1)}, bf16[8,288,384]{2,1,0:T(8,128)(2,1)}) custom-call(bf16[256,768]{1,0:T(8,128)(2,1)} %get-tuple-element.91.refs_0_, bf16[256,1536]{1,0:T(8,128)(2,1)} %refs_1_.5, bf16[256,3072]{1,0:T(8,128)(2,1)} %get-tuple-element.92.refs_2_, bf16[256,768]{1,0:T(8,128)(2,1)} %copy-done.3, bf16[8,576,384]{2,1,0:T(8,128)(2,1)} %copy-done.7, ...), custom_call_target="tpu_custom_call" | custom-call | flops 400000000 | bytes 1200000 | tf_op jit(solution)/shard_map/home/pallas_call | solution.py:156
  189.7 5.5 %home.5 = (bf16[4,2,240,384]{3,2,1,0:T(8,128)(2,1)}, bf16[4,2,240,384]{3,2,1,0:T(8,128)(2,1)}) custom-call(bf16[256,768]{1,0:T(8,128)(2,1)} %get-tuple-element.93.refs_0_, bf16[256,3072]{1,0:T(8,128)(2,1)} %get-tuple-element.94.refs_1_, bf16[256,768]{1,0:T(8,128)(2,1)} %get-tuple-element.95.refs_2_, bf16[256,768]{1,0:T(8,128)(2,1)} %get-tuple-element.96.refs_3_, ...), custom_call_target="tpu_custom_call" | custom-call | flops 400000000 | bytes 1200000 | tf_op jit(solution)/shard_map/home/pallas_call | solution.py:156
  195.2 11.0 %key_back.2 = (bf16[384,384]{1,0:T(8,128)(2,1)}, bf16[384,384]{1,0:T(8,128)(2,1)}) custom-call(bf16[1,208,768]{2,1,0:T(8,128)(2,1)} %bitcast.226, bf16[1,208,768]{2,1,0:T(8,128)(2,1)} %bitcast.14.refs_1_, bf16[1,208,768]{2,1,0:T(8,128)(2,1)} %bitcast.15.refs_2_, bf16[1,208,768]{2,1,0:T(8,128)(2,1)} %bitcast.16.refs_3_, ...), custom_call_target="tpu_custom_call" | custom-call | flops 1110000000 | bytes 3330000 | tf_op jit(solution)/shard_map/key_back/pallas_call | solution.py:156
  206.3 11.2 %key_back.3 = (bf16[384,384]{1,0:T(8,128)(2,1)}, bf16[384,384]{1,0:T(8,128)(2,1)}) custom-call(bf16[1,208,768]{2,1,0:T(8,128)(2,1)} %bitcast.227, bf16[1,208,768]{2,1,0:T(8,128)(2,1)} %bitcast.14.refs_1_, bf16[1,208,768]{2,1,0:T(8,128)(2,1)} %bitcast.15.refs_2_, bf16[1,208,768]{2,1,0:T(8,128)(2,1)} %bitcast.16.refs_3_, ...), custom_call_target="tpu_custom_call" | custom-call | flops 1110000000 | bytes 3330000 | tf_op jit(solution)/shard_map/key_back/pallas_call | solution.py:156
  217.5 2.2 pad_maximum_fusion
  219.6 6.7 %input.1 = (bf16[128,768]{1,0:T(8,128)(2,1)}, f32[256,768]{1,0:T(8,128)}, bf16[384,2304]{1,0:T(8,128)(2,1)}, f32[8,768]{1,0:T(8,128)}) custom-call(bf16[256,768]{1,0:T(8,128)(2,1)} %pad_maximum_fusion.3.refs_0_, bf16[384,768]{1,0:T(8,128)(2,1)} %get-tuple-element.172.refs_1_, bf16[384,768]{1,0:T(8,128)(2,1)} %get-tuple-element.173.refs_2_, ...), custom_call_target="tpu_custom_call" | custom-call | flops 600000000 | bytes 1800000 | tf_op jit(solution)/shard_map/input/pallas_call | solution.py:156
  228.2 1.4 collective-permute-start.36
  229.7 4.2 %away.7 = bf16[8,288,384]{2,1,0:T(8,128)(2,1)} custom-call(bf16[384,768]{1,0:T(8,128)(2,1)} %get-tuple-element.74.refs_6_.refs_0_, bf16[384,2304]{1,0:T(8,128)(2,1)} %get-tuple-element.121.refs_1_), custom_call_target="tpu_custom_call" | custom-call | flops 213333328 | bytes 640000 | tf_op jit(solution)/shard_map/away/pallas_call | solution.py:156
  235.0 3.8 %pixel.1 = (bf16[256,768]{1,0:T(8,128)(2,1)}, bf16[256,1536]{1,0:T(8,128)(2,1)}) custom-call(f32[256,768]{1,0:T(8,128)} %get-tuple-element.110.refs_0_, bf16[128,768]{1,0:T(8,128)(2,1)} %copy-done.18, s32[1,128]{1,0:T(1,128)} %bitcast.266, bf16[1536,768]{1,0:T(8,128)(2,1)} %refs_3_.11), custom_call_target="tpu_custom_call" | custom-call | flops 300000000 | bytes 900000 | tf_op jit(solution)/shard_map/pixel/pallas_call | solution.py:156
  238.8 2.8 away.6
  243.3 1.3 collective-permute-done.23.refs_4_
  245.3 3.4 home.6
  248.6 10.0 %collective-permute-start.24 = (bf16[4,2,112,384]{3,2,1,0:T(8,128)(2,1)}, bf16[4,2,112,384]{3,2,1,0:T(8,128)(2,1)}, u32[]{:S(2)}, u32[]{:S(2)}) collective-permute-start(bf16[4,2,112,384]{3,2,1,0:T(8,128)(2,1)} %get-tuple-element.120), channel_id=1, source_target_pairs={{0,2},{1,3},{2,0},{3,1},{4,6},{5,7},{6,4},{7,5},{8,10},{9,11},{10,... | collective-permute-start | bytes 2064392 | tf_op jit(solution)/shard_map/ppermute | solution.py:53
  258.6 4.9 %collective-permute-done.36 = bf16[4,2,240,384]{3,2,1,0:T(8,128)(2,1)} collective-permute-done((bf16[4,2,240,384]{3,2,1,0:T(8,128)(2,1)S(1)}, bf16[4,2,240,384]{3,2,1,0:T(8,128)(2,1)}, u32[]{:S(2)}, u32[]{:S(2)}) %collective-permute-start.36) | collective-permute-done | bytes 1474592 | tf_op jit(solution)/shard_map/ppermute | solution.py:53
  263.5 2.9 dynamic-slice_add_fusion.1
  266.4 1.7 collective-permute-start.37
  268.1 6.6 %collective-permute-done.24 = bf16[4,2,112,384]{3,2,1,0:T(8,128)(2,1)} collective-permute-done((bf16[4,2,112,384]{3,2,1,0:T(8,128)(2,1)}, bf16[4,2,112,384]{3,2,1,0:T(8,128)(2,1)}, u32[]{:S(2)}, u32[]{:S(2)}) %collective-permute-start.24) | collective-permute-done | bytes 688160 | tf_op jit(solution)/shard_map/ppermute | solution.py:53
  274.7 1.9 dynamic-slice_add_fusion.3
  276.6 4.7 %collective-permute-start.25 = (bf16[2,2,112,384]{3,2,1,0:T(8,128)(2,1)}, bf16[2,2,112,384]{3,2,1,0:T(8,128)(2,1)S(1)}, u32[]{:S(2)}, u32[]{:S(2)}) collective-permute-start(bf16[2,2,112,384]{3,2,1,0:T(8,128)(2,1)} %get-tuple-element.137), channel_id=1, source_target_pairs={{0,4},{1,5},{2,6},{3,7},{4,0},{5,1},{6,2},{7,3},{8,12},{9,13},{10,... | collective-permute-start | bytes 1032200 | tf_op jit(solution)/shard_map/ppermute | solution.py:53
  281.3 3.1 dynamic-slice_add_fusion
  285.3 4.7 %home.7 = (bf16[8,144,384]{2,1,0:T(8,128)(2,1)}, bf16[8,144,384]{2,1,0:T(8,128)(2,1)}) custom-call(bf16[384,768]{1,0:T(8,128)(2,1)} %get-tuple-element.74.refs_6_.refs_0_, bf16[384,2304]{1,0:T(8,128)(2,1)} %get-tuple-element.121.refs_1_, bf16[8,288,384]{2,1,0:T(8,128)(2,1)} %collective-permute-done.29.refs_2_), custom_call_target="tpu_custom_call" | custom-call | flops 400000000 | bytes 1200000 | tf_op jit(solution)/shard_map/home/pallas_call | solution.py:156
  290.1 6.8 %collective-permute-done.25 = bf16[2,2,112,384]{3,2,1,0:T(8,128)(2,1)S(1)} collective-permute-done((bf16[2,2,112,384]{3,2,1,0:T(8,128)(2,1)}, bf16[2,2,112,384]{3,2,1,0:T(8,128)(2,1)S(1)}, u32[]{:S(2)}, u32[]{:S(2)}) %collective-permute-start.25) | collective-permute-done | bytes 344096 | tf_op jit(solution)/shard_map/ppermute | solution.py:53
  299.2 10.1 %collective-permute-done.26 = bf16[2,112,384]{2,1,0:T(8,128)(2,1)S(1)} collective-permute-done((bf16[2,112,384]{2,1,0:T(8,128)(2,1)S(1)}, bf16[2,112,384]{2,1,0:T(8,128)(2,1)S(1)}, u32[]{:S(2)}, u32[]{:S(2)}) %collective-permute-start.26) | collective-permute-done | bytes 172064 | tf_op jit(solution)/shard_map/ppermute | solution.py:53
  312.3 1.7 collective-permute-start.44
  316.4 3.3 collective-permute-done.39
  319.7 1.8 collective-permute-start.40
  322.6 3.5 collective-permute-done.40
  329.0 2.2 collective-permute-start.32
  331.7 10.0 %collective-permute-done.32 = bf16[2,144,384]{2,1,0:T(8,128)(2,1)S(1)} collective-permute-done((bf16[2,144,384]{2,1,0:T(8,128)(2,1)S(1)}, bf16[2,144,384]{2,1,0:T(8,128)(2,1)S(1)}, u32[]{:S(2)}, u32[]{:S(2)}) %collective-permute-start.32) | collective-permute-done | bytes 221216 | tf_op jit(solution)/shard_map/ppermute | solution.py:53
  343.2 1.5 collective-permute-start.46
  344.7 3.2 collective-permute-done.33
  347.9 1.6 collective-permute-start.34
  350.3 2.4 collective-permute-done.34
  (224 shorter events, 45.1 us)
Async XLA Ops:
  3.2 29.6 %copy-start.21 = (s32[256]{0:T(256)S(1)}, s32[256]{0:T(256)}, u32[]{:S(2)}) copy-start(s32[256]{0:T(256)} %param.25) | copy-start | bytes 3076
  3.2 30.4 %copy-start.24 = (f32[1536]{0:T(1024)S(1)}, f32[1536]{0:T(1024)}, u32[]{:S(2)}) copy-start(f32[1536]{0:T(1024)} %param.31) | copy-start | bytes 18436
  7.3 3.6 %collective-permute-start = (bf16[128,768]{1,0:T(8,128)(2,1)}, bf16[128,768]{1,0:T(8,128)(2,1)S(1)}, u32[]{:S(2)}, u32[]{:S(2)}) collective-permute-start(bf16[128,768]{1,0:T(8,128)(2,1)} %get-tuple-element.72), channel_id=1, source_target_pairs={{0,8},{8,16},{16,24},{1,9},{9,17},{17,25},{2,10},{10,18},{18,26},{... | collective-permute-start | bytes 589832 | tf_op jit(solution)/shard_map/ppermute | solution.py:48
  14.0 12.3 %collective-permute-start.1 = (bf16[336,768]{1,0:T(8,128)(2,1)}, bf16[336,768]{1,0:T(8,128)(2,1)S(1)}, u32[]{:S(2)}, u32[]{:S(2)}) collective-permute-start(bf16[336,768]{1,0:T(8,128)(2,1)} %get-tuple-element.73), channel_id=1, source_target_pairs={{0,2},{1,3},{2,0},{3,1},{4,6},{5,7},{6,4},{7,5},{8,10},{9,11},{10,... | collective-permute-start | bytes 1548296 | tf_op jit(solution)/shard_map/ppermute | solution.py:74
  16.4 13.8 %collective-permute-start.4 = (bf16[336,768]{1,0:T(8,128)(2,1)}, bf16[336,768]{1,0:T(8,128)(2,1)S(1)}, u32[]{:S(2)}, u32[]{:S(2)}) collective-permute-start(bf16[336,768]{1,0:T(8,128)(2,1)} %get-tuple-element.73), channel_id=1, source_target_pairs={{2,4},{3,5},{4,2},{5,3},{10,12},{11,13},{12,10},{13,11},{18,20},{1... | collective-permute-start | bytes 1548296 | tf_op jit(solution)/shard_map/ppermute | solution.py:74
  26.3 14.9 %copy-start.5 = (bf16[336,768]{1,0:T(8,128)(2,1)}, bf16[336,768]{1,0:T(8,128)(2,1)S(1)}, u32[]{:S(2)}) copy-start(bf16[336,768]{1,0:T(8,128)(2,1)S(1)} %collective-permute-done.1) | copy-start | bytes 1548292
  26.3 5.2 %collective-permute-start.2 = (bf16[336,768]{1,0:T(8,128)(2,1)S(1)}, bf16[336,768]{1,0:T(8,128)(2,1)}, u32[]{:S(2)}, u32[]{:S(2)}) collective-permute-start(bf16[336,768]{1,0:T(8,128)(2,1)S(1)} %collective-permute-done.1), channel_id=1, source_target_pairs={{2,4},{3,5},{4,2},{5,3},{10,12},{11,13},{12,10},{13,11},{18,20},{1... | collective-permute-start | bytes 1548296 | tf_op jit(solution)/shard_map/ppermute | solution.py:74
  27.8 13.4 %collective-permute-start.7 = (bf16[336,768]{1,0:T(8,128)(2,1)}, bf16[336,768]{1,0:T(8,128)(2,1)S(1)}, u32[]{:S(2)}, u32[]{:S(2)}) collective-permute-start(bf16[336,768]{1,0:T(8,128)(2,1)} %get-tuple-element.73), channel_id=1, source_target_pairs={{0,1},{1,0},{2,3},{3,2},{4,5},{5,4},{6,7},{7,6},{8,9},{9,8},{10,11... | collective-permute-start | bytes 1548296 | tf_op jit(solution)/shard_map/ppermute | solution.py:53
  30.1 27.0 %copy-start.14 = (bf16[336,768]{1,0:T(8,128)(2,1)}, bf16[336,768]{1,0:T(8,128)(2,1)S(1)}, u32[]{:S(2)}) copy-start(bf16[336,768]{1,0:T(8,128)(2,1)S(1)} %collective-permute-done.4.refs_1_) | copy-start | bytes 1548292
  30.1 27.1 %collective-permute-start.6 = (bf16[336,768]{1,0:T(8,128)(2,1)S(1)}, bf16[336,768]{1,0:T(8,128)(2,1)S(1)}, u32[]{:S(2)}, u32[]{:S(2)}) collective-permute-start(bf16[336,768]{1,0:T(8,128)(2,1)S(1)} %collective-permute-done.4.refs_1_), channel_id=1, source_target_pairs={{2,0},{3,1},{4,6},{5,7},{10,8},{11,9},{12,14},{13,15},{18,16},{19,... | collective-permute-start | bytes 1548296 | tf_op jit(solution)/shard_map/ppermute | solution.py:74
  31.4 31.1 %collective-permute-start.5 = (bf16[336,768]{1,0:T(8,128)(2,1)S(1)}, bf16[336,768]{1,0:T(8,128)(2,1)S(1)}, u32[]{:S(2)}, u32[]{:S(2)}) collective-permute-start(bf16[336,768]{1,0:T(8,128)(2,1)S(1)} %collective-permute-done.1), channel_id=1, source_target_pairs={{0,1},{1,0},{2,3},{3,2},{4,5},{5,4},{6,7},{7,6},{8,9},{9,8},{10,11... | collective-permute-start | bytes 1548296 | tf_op jit(solution)/shard_map/ppermute | solution.py:53
  31.5 41.2 %collective-permute-start.3 = (bf16[336,768]{1,0:T(8,128)(2,1)}, bf16[336,768]{1,0:T(8,128)(2,1)}, u32[]{:S(2)}, u32[]{:S(2)}) collective-permute-start(bf16[336,768]{1,0:T(8,128)(2,1)} %collective-permute-done.2.refs_1_), channel_id=1, source_target_pairs={{2,0},{3,1},{4,6},{5,7},{10,8},{11,9},{12,14},{13,15},{18,16},{19,... | collective-permute-start | bytes 1548296 | tf_op jit(solution)/shard_map/ppermute | solution.py:74
  58.0 21.1 %slice-start = ((s8[4718592]{0:T(1024)(128)(4,1)}), s8[4194304]{0:T(1024)(128)(4,1)S(1)}, s32[]{:S(2)}) async-start(s8[4718592]{0:T(1024)(128)(4,1)} %bitcast.204), calls=%async_computation | async-start | bytes 8388608
  60.2 22.0 %collective-permute-start.8 = (bf16[336,768]{1,0:T(8,128)(2,1)}, bf16[336,768]{1,0:T(8,128)(2,1)}, u32[]{:S(2)}, u32[]{:S(2)}) collective-permute-start(bf16[336,768]{1,0:T(8,128)(2,1)} %choose.2), channel_id=1, source_target_pairs={{0,1},{1,0},{2,3},{3,2},{4,5},{5,4},{6,7},{7,6},{8,9},{9,8},{10,11... | collective-permute-start | bytes 1548296 | tf_op jit(solution)/shard_map/ppermute | solution.py:53
  63.3 11.7 %copy-start.1 = (bf16[256,1536]{1,0:T(8,128)(2,1)S(1)}, bf16[256,1536]{1,0:T(8,128)(2,1)}, u32[]{:S(2)}) copy-start(bf16[256,1536]{1,0:T(8,128)(2,1)} %refs_1_.5) | copy-start | bytes 2359300
  63.3 15.8 %slice-start.1 = ((s8[4718592]{0:T(1024)(128)(4,1)}), s8[524288]{0:T(1024)(128)(4,1)S(1)}, s32[]{:S(2)}) async-start(s8[4718592]{0:T(1024)(128)(4,1)} %bitcast.204), calls=%async_computation.1 | async-start | bytes 1048576
  74.9 13.2 %collective-permute-start.9 = (bf16[336,768]{1,0:T(8,128)(2,1)}, bf16[336,768]{1,0:T(8,128)(2,1)}, u32[]{:S(2)}, u32[]{:S(2)}) collective-permute-start(bf16[336,768]{1,0:T(8,128)(2,1)} %choose.3), channel_id=1, source_target_pairs={{0,1},{1,0},{2,3},{3,2},{4,5},{5,4},{6,7},{7,6},{8,9},{9,8},{10,11... | collective-permute-start | bytes 1548296 | tf_op jit(solution)/shard_map/ppermute | solution.py:53
  124.6 42.7 %collective-permute-start.19 = (bf16[8,576,384]{2,1,0:T(8,128)(2,1)}, bf16[8,576,384]{2,1,0:T(8,128)(2,1)S(1)}, u32[]{:S(2)}, u32[]{:S(2)}) collective-permute-start(bf16[8,576,384]{2,1,0:T(8,128)(2,1)} %away.4.refs_20_), channel_id=1, source_target_pairs={{0,8},{8,0},{16,24},{24,16},{1,9},{9,1},{17,25},{25,17},{2,10},{10... | collective-permute-start | bytes 10616840 | tf_op jit(solution)/shard_map/ppermute | solution.py:53
  131.3 58.4 %collective-permute-start.20 = (bf16[8,480,384]{2,1,0:T(8,128)(2,1)}, bf16[8,480,384]{2,1,0:T(8,128)(2,1)}, u32[]{:S(2)}, u32[]{:S(2)}) collective-permute-start(bf16[8,480,384]{2,1,0:T(8,128)(2,1)} %away.5.refs_21_), channel_id=1, source_target_pairs={{0,8},{8,0},{16,24},{24,16},{1,9},{9,1},{17,25},{25,17},{2,10},{10... | collective-permute-start | bytes 8847368 | tf_op jit(solution)/shard_map/ppermute | solution.py:53
  131.3 13.5 %collective-permute-start.10 = (bf16[208,768]{1,0:T(8,128)(2,1)S(1)}, bf16[208,768]{1,0:T(8,128)(2,1)}, u32[]{:S(2)}, u32[]{:S(2)}) collective-permute-start(bf16[208,768]{1,0:T(8,128)(2,1)S(1)} %copy-done.9), channel_id=1, source_target_pairs={{0,2},{1,3},{2,0},{3,1},{4,6},{5,7},{6,4},{7,5},{8,10},{9,11},{10,... | collective-permute-start | bytes 958472 | tf_op jit(solution)/shard_map/ppermute | solution.py:74
  136.8 9.3 %collective-permute-start.13 = (bf16[208,768]{1,0:T(8,128)(2,1)S(1)}, bf16[208,768]{1,0:T(8,128)(2,1)}, u32[]{:S(2)}, u32[]{:S(2)}) collective-permute-start(bf16[208,768]{1,0:T(8,128)(2,1)S(1)} %copy-done.9), channel_id=1, source_target_pairs={{2,4},{3,5},{4,2},{5,3},{10,12},{11,13},{12,10},{13,11},{18,20},{1... | collective-permute-start | bytes 958472 | tf_op jit(solution)/shard_map/ppermute | solution.py:74
  144.8 3.3 collective-permute-start.15
  146.1 16.0 %collective-permute-start.14 = (bf16[208,768]{1,0:T(8,128)(2,1)}, bf16[208,768]{1,0:T(8,128)(2,1)}, u32[]{:S(2)}, u32[]{:S(2)}) collective-permute-start(bf16[208,768]{1,0:T(8,128)(2,1)} %collective-permute-done.13), channel_id=1, source_target_pairs={{2,0},{3,1},{4,6},{5,7},{10,8},{11,9},{12,14},{13,15},{18,16},{19,... | collective-permute-start | bytes 958472 | tf_op jit(solution)/shard_map/ppermute | solution.py:74
  147.6 47.7 %collective-permute-start.11 = (bf16[208,768]{1,0:T(8,128)(2,1)}, bf16[208,768]{1,0:T(8,128)(2,1)}, u32[]{:S(2)}, u32[]{:S(2)}) collective-permute-start(bf16[208,768]{1,0:T(8,128)(2,1)} %get-tuple-element.99), channel_id=1, source_target_pairs={{0,1},{1,0},{2,3},{3,2},{4,5},{5,4},{6,7},{7,6},{8,9},{9,8},{10,11... | collective-permute-start | bytes 958472 | tf_op jit(solution)/shard_map/ppermute | solution.py:53
  148.1 17.9 %collective-permute-start.16 = (bf16[208,768]{1,0:T(8,128)(2,1)}, bf16[208,768]{1,0:T(8,128)(2,1)S(1)}, u32[]{:S(2)}, u32[]{:S(2)}) collective-permute-start(bf16[208,768]{1,0:T(8,128)(2,1)} %collective-permute-done.15), channel_id=1, source_target_pairs={{2,0},{3,1},{4,6},{5,7},{10,8},{11,9},{12,14},{13,15},{18,16},{19,... | collective-permute-start | bytes 958472 | tf_op jit(solution)/shard_map/ppermute | solution.py:74
  162.2 33.0 %collective-permute-start.12 = (bf16[208,768]{1,0:T(8,128)(2,1)}, bf16[208,768]{1,0:T(8,128)(2,1)}, u32[]{:S(2)}, u32[]{:S(2)}) collective-permute-start(bf16[208,768]{1,0:T(8,128)(2,1)} %collective-permute-done.10), channel_id=1, source_target_pairs={{0,1},{1,0},{2,3},{3,2},{4,5},{5,4},{6,7},{7,6},{8,9},{9,8},{10,11... | collective-permute-start | bytes 958472 | tf_op jit(solution)/shard_map/ppermute | solution.py:53
  166.0 29.2 %collective-permute-start.17 = (bf16[208,768]{1,0:T(8,128)(2,1)}, bf16[208,768]{1,0:T(8,128)(2,1)}, u32[]{:S(2)}, u32[]{:S(2)}) collective-permute-start(bf16[208,768]{1,0:T(8,128)(2,1)} %broadcast_select_fusion.5), channel_id=1, source_target_pairs={{0,1},{1,0},{2,3},{3,2},{4,5},{5,4},{6,7},{7,6},{8,9},{9,8},{10,11... | collective-permute-start | bytes 958472 | tf_op jit(solution)/shard_map/ppermute | solution.py:53
  167.3 14.4 %copy-start.7 = (bf16[8,576,384]{2,1,0:T(8,128)(2,1)}, bf16[8,576,384]{2,1,0:T(8,128)(2,1)S(1)}, u32[]{:S(2)}) copy-start(bf16[8,576,384]{2,1,0:T(8,128)(2,1)S(1)} %collective-permute-done.19.refs_4_) | copy-start | bytes 10616836
  167.3 27.9 %collective-permute-start.18 = (bf16[208,768]{1,0:T(8,128)(2,1)}, bf16[208,768]{1,0:T(8,128)(2,1)}, u32[]{:S(2)}, u32[]{:S(2)}) collective-permute-start(bf16[208,768]{1,0:T(8,128)(2,1)} %broadcast_select_fusion.4), channel_id=1, source_target_pairs={{0,1},{1,0},{2,3},{3,2},{4,5},{5,4},{6,7},{7,6},{8,9},{9,8},{10,11... | collective-permute-start | bytes 958472 | tf_op jit(solution)/shard_map/ppermute | solution.py:53
  168.9 12.8 %copy-start.12 = (bf16[256,384]{1,0:T(8,128)(2,1)S(1)}, bf16[256,384]{1,0:T(8,128)(2,1)}, u32[]{:S(2)}) copy-start(bf16[256,384]{1,0:T(8,128)(2,1)} %get-tuple-element.97.refs_20_) | copy-start | bytes 589828
  206.2 11.2 %copy-start.10 = (bf16[384,384]{1,0:T(8,128)(2,1)S(1)}, bf16[384,384]{1,0:T(8,128)(2,1)}, u32[]{:S(2)}) copy-start(bf16[384,384]{1,0:T(8,128)(2,1)} %get-tuple-element.104.refs_16_) | copy-start | bytes 884740
  206.3 11.2 %copy-start.17 = (bf16[384,384]{1,0:T(8,128)(2,1)S(1)}, bf16[384,384]{1,0:T(8,128)(2,1)}, u32[]{:S(2)}) copy-start(bf16[384,384]{1,0:T(8,128)(2,1)} %get-tuple-element.107) | copy-start | bytes 884740
  219.6 8.0 %copy-start.31 = (f32[1,768]{1,0:T(1,128)S(1)}, f32[1,768]{1,0:T(1,128)}, u32[]{:S(2)}) copy-start(f32[1,768]{1,0:T(1,128)} %get-tuple-element.117) | copy-start | bytes 9220
  219.6 8.2 %copy-start.23 = (f32[1,3072]{1,0:T(1,128)S(1)}, f32[1,3072]{1,0:T(1,128)}, u32[]{:S(2)}) copy-start(f32[1,3072]{1,0:T(1,128)} %get-tuple-element.118) | copy-start | bytes 36868
  219.6 8.3 %copy-start.2 = (bf16[8,288,384]{2,1,0:T(8,128)(2,1)S(1)}, bf16[8,288,384]{2,1,0:T(8,128)(2,1)}, u32[]{:S(2)}) copy-start(bf16[8,288,384]{2,1,0:T(8,128)(2,1)} %get-tuple-element.102.refs_6_.refs_17_) | copy-start | bytes 5308420
  219.6 8.6 %copy-start.8 = (bf16[4,2,240,384]{3,2,1,0:T(8,128)(2,1)S(1)}, bf16[4,2,240,384]{3,2,1,0:T(8,128)(2,1)}, u32[]{:S(2)}) copy-start(bf16[4,2,240,384]{3,2,1,0:T(8,128)(2,1)} %get-tuple-element.103.refs_18_) | copy-start | bytes 4423684
  226.3 8.0 %collective-permute-start.21 = (bf16[128,768]{1,0:T(8,128)(2,1)}, bf16[128,768]{1,0:T(8,128)(2,1)S(1)}, u32[]{:S(2)}, u32[]{:S(2)}) collective-permute-start(bf16[128,768]{1,0:T(8,128)(2,1)} %get-tuple-element.111), channel_id=1, source_target_pairs={{8,0},{16,8},{24,16},{9,1},{17,9},{25,17},{10,2},{18,10},{26,18},{... | collective-permute-start | bytes 589832 | tf_op jit(solution)/shard_map/ppermute | solution.py:48
  227.9 53.4 %collective-permute-start.42 = (bf16[8,288,384]{2,1,0:T(8,128)(2,1)S(1)}, bf16[8,288,384]{2,1,0:T(8,128)(2,1)}, u32[]{:S(2)}, u32[]{:S(2)}) collective-permute-start(bf16[8,288,384]{2,1,0:T(8,128)(2,1)S(1)} %copy-done.2), channel_id=1, source_target_pairs={{0,16},{8,24},{16,0},{24,8},{1,17},{9,25},{17,1},{25,9},{2,18},{10... | collective-permute-start | bytes 5308424 | tf_op jit(solution)/shard_map/ppermute | solution.py:53
  228.2 35.3 %collective-permute-start.36 = (bf16[4,2,240,384]{3,2,1,0:T(8,128)(2,1)S(1)}, bf16[4,2,240,384]{3,2,1,0:T(8,128)(2,1)}, u32[]{:S(2)}, u32[]{:S(2)}) collective-permute-start(bf16[4,2,240,384]{3,2,1,0:T(8,128)(2,1)S(1)} %copy-done.8), channel_id=1, source_target_pairs={{0,1},{1,0},{2,3},{3,2},{4,5},{5,4},{6,7},{7,6},{8,9},{9,8},{10,11... | collective-permute-start | bytes 4423688 | tf_op jit(solution)/shard_map/ppermute | solution.py:53
  233.9 51.4 %collective-permute-start.29 = (bf16[8,288,384]{2,1,0:T(8,128)(2,1)}, bf16[8,288,384]{2,1,0:T(8,128)(2,1)}, u32[]{:S(2)}, u32[]{:S(2)}) collective-permute-start(bf16[8,288,384]{2,1,0:T(8,128)(2,1)} %away.7), channel_id=1, source_target_pairs={{0,8},{8,0},{16,24},{24,16},{1,9},{9,1},{17,25},{25,17},{2,10},{10... | collective-permute-start | bytes 5308424 | tf_op jit(solution)/shard_map/ppermute | solution.py:53
  241.6 3.2 collective-permute-start.22
  242.2 2.4 collective-permute-start.23
  248.6 26.1 %collective-permute-start.24 = (bf16[4,2,112,384]{3,2,1,0:T(8,128)(2,1)}, bf16[4,2,112,384]{3,2,1,0:T(8,128)(2,1)}, u32[]{:S(2)}, u32[]{:S(2)}) collective-permute-start(bf16[4,2,112,384]{3,2,1,0:T(8,128)(2,1)} %get-tuple-element.120), channel_id=1, source_target_pairs={{0,2},{1,3},{2,0},{3,1},{4,6},{5,7},{6,4},{7,5},{8,10},{9,11},{10,... | collective-permute-start | bytes 2064392 | tf_op jit(solution)/shard_map/ppermute | solution.py:53
  263.5 11.2 %copy-start.13 = (bf16[4,2,112,384]{3,2,1,0:T(8,128)(2,1)S(1)}, bf16[4,2,112,384]{3,2,1,0:T(8,128)(2,1)}, u32[]{:S(2)}) copy-start(bf16[4,2,112,384]{3,2,1,0:T(8,128)(2,1)} %get-tuple-element.119) | copy-start | bytes 2064388
  266.4 31.5 %collective-permute-start.37 = (bf16[2,2,240,384]{3,2,1,0:T(8,128)(2,1)}, bf16[2,2,240,384]{3,2,1,0:T(8,128)(2,1)}, u32[]{:S(2)}, u32[]{:S(2)}) collective-permute-start(bf16[2,2,240,384]{3,2,1,0:T(8,128)(2,1)} %get-tuple-element.131), channel_id=1, source_target_pairs={{0,16},{8,24},{16,0},{24,8},{1,17},{9,25},{17,1},{25,9},{2,18},{10... | collective-permute-start | bytes 2211848 | tf_op jit(solution)/shard_map/ppermute | solution.py:53
  276.6 20.3 %collective-permute-start.25 = (bf16[2,2,112,384]{3,2,1,0:T(8,128)(2,1)}, bf16[2,2,112,384]{3,2,1,0:T(8,128)(2,1)S(1)}, u32[]{:S(2)}, u32[]{:S(2)}) collective-permute-start(bf16[2,2,112,384]{3,2,1,0:T(8,128)(2,1)} %get-tuple-element.137), channel_id=1, source_target_pairs={{0,4},{1,5},{2,6},{3,7},{4,0},{5,1},{6,2},{7,3},{8,12},{9,13},{10,... | collective-permute-start | bytes 1032200 | tf_op jit(solution)/shard_map/ppermute | solution.py:53
  284.4 26.6 %collective-permute-start.43 = (bf16[2,2,288,384]{3,2,1,0:T(8,128)(2,1)}, bf16[2,2,288,384]{3,2,1,0:T(8,128)(2,1)}, u32[]{:S(2)}, u32[]{:S(2)}) collective-permute-start(bf16[2,2,288,384]{3,2,1,0:T(8,128)(2,1)} %get-tuple-element.129), channel_id=1, source_target_pairs={{0,1},{1,0},{2,3},{3,2},{4,5},{5,4},{6,7},{7,6},{8,9},{9,8},{10,11... | collective-permute-start | bytes 2654216 | tf_op jit(solution)/shard_map/ppermute | solution.py:53
  290.0 23.9 %collective-permute-start.30 = (bf16[8,144,384]{2,1,0:T(8,128)(2,1)}, bf16[8,144,384]{2,1,0:T(8,128)(2,1)}, u32[]{:S(2)}, u32[]{:S(2)}) collective-permute-start(bf16[8,144,384]{2,1,0:T(8,128)(2,1)} %get-tuple-element.123), channel_id=1, source_target_pairs={{0,16},{8,24},{16,0},{24,8},{1,17},{9,25},{17,1},{25,9},{2,18},{10... | collective-permute-start | bytes 2654216 | tf_op jit(solution)/shard_map/ppermute | solution.py:53
  296.9 12.4 %collective-permute-start.26 = (bf16[2,112,384]{2,1,0:T(8,128)(2,1)S(1)}, bf16[2,112,384]{2,1,0:T(8,128)(2,1)S(1)}, u32[]{:S(2)}, u32[]{:S(2)}) collective-permute-start(bf16[2,112,384]{2,1,0:T(8,128)(2,1)S(1)} %fusion.6), channel_id=1, source_target_pairs={{0,1},{1,0},{2,3},{3,2},{4,5},{5,4},{6,7},{7,6},{8,9},{9,8},{10,11... | collective-permute-start | bytes 516104 | tf_op jit(solution)/shard_map/ppermute | solution.py:53
  299.1 11.6 %collective-permute-start.38 = (bf16[2,240,384]{2,1,0:T(8,128)(2,1)S(1)}, bf16[2,240,384]{2,1,0:T(8,128)(2,1)S(1)}, u32[]{:S(2)}, u32[]{:S(2)}) collective-permute-start(bf16[2,240,384]{2,1,0:T(8,128)(2,1)S(1)} %get-tuple-element.135), channel_id=1, source_target_pairs={{0,2},{1,3},{2,0},{3,1},{4,6},{5,7},{6,4},{7,5},{8,10},{9,11},{10,... | collective-permute-start | bytes 1105928 | tf_op jit(solution)/shard_map/ppermute | solution.py:53
  310.3 6.0 %collective-permute-start.27 = (bf16[2,112,384]{2,1,0:T(8,128)(2,1)S(1)}, bf16[2,112,384]{2,1,0:T(8,128)(2,1)S(1)}, u32[]{:S(2)}, u32[]{:S(2)}) collective-permute-start(bf16[2,112,384]{2,1,0:T(8,128)(2,1)S(1)} %bitcast_add_fusion.13), channel_id=1, source_target_pairs={{0,16},{8,24},{16,0},{24,8},{1,17},{9,25},{17,1},{25,9},{2,18},{10... | collective-permute-start | bytes 516104 | tf_op jit(solution)/shard_map/ppermute | solution.py:53
  310.7 9.0 %collective-permute-start.39 = (bf16[240,384]{1,0:T(8,128)(2,1)S(1)}, bf16[240,384]{1,0:T(8,128)(2,1)S(1)}, u32[]{:S(2)}, u32[]{:S(2)}) collective-permute-start(bf16[240,384]{1,0:T(8,128)(2,1)S(1)} %fusion.5), channel_id=1, source_target_pairs={{0,4},{1,5},{2,6},{3,7},{4,0},{5,1},{6,2},{7,3},{8,12},{9,13},{10,... | collective-permute-start | bytes 552968 | tf_op jit(solution)/shard_map/ppermute | solution.py:53
  312.3 16.0 %collective-permute-start.44 = (bf16[2,288,384]{2,1,0:T(8,128)(2,1)S(1)}, bf16[2,288,384]{2,1,0:T(8,128)(2,1)S(1)}, u32[]{:S(2)}, u32[]{:S(2)}) collective-permute-start(bf16[2,288,384]{2,1,0:T(8,128)(2,1)S(1)} %get-tuple-element.133), channel_id=1, source_target_pairs={{0,2},{1,3},{2,0},{3,1},{4,6},{5,7},{6,4},{7,5},{8,10},{9,11},{10,... | collective-permute-start | bytes 1327112 | tf_op jit(solution)/shard_map/ppermute | solution.py:53
  315.4 13.5 %collective-permute-start.31 = (bf16[2,2,144,384]{3,2,0,1:T(8,128)(2,1)S(1)}, bf16[2,2,144,384]{3,2,0,1:T(8,128)(2,1)S(1)}, u32[]{:S(2)}, u32[]{:S(2)}) collective-permute-start(bf16[2,2,144,384]{3,2,0,1:T(8,128)(2,1)S(1)} %fusion), channel_id=1, source_target_pairs={{0,1},{1,0},{2,3},{3,2},{4,5},{5,4},{6,7},{7,6},{8,9},{9,8},{10,11... | collective-permute-start | bytes 1327112 | tf_op jit(solution)/shard_map/ppermute | solution.py:53
  316.3 5.2 %collective-permute-start.28 = (bf16[2,112,384]{2,1,0:T(8,128)(2,1)S(1)}, bf16[2,112,384]{2,1,0:T(8,128)(2,1)S(1)}, u32[]{:S(2)}, u32[]{:S(2)}) collective-permute-start(bf16[2,112,384]{2,1,0:T(8,128)(2,1)S(1)} %add.284), channel_id=1, source_target_pairs={{0,8},{8,0},{16,24},{24,16},{1,9},{9,1},{17,25},{25,17},{2,10},{10... | collective-permute-start | bytes 516104 | tf_op jit(solution)/shard_map/ppermute | solution.py:53
  319.7 6.4 %collective-permute-start.40 = (bf16[240,384]{1,0:T(8,128)(2,1)S(1)}, bf16[240,384]{1,0:T(8,128)(2,1)S(1)}, u32[]{:S(2)}, u32[]{:S(2)}) collective-permute-start(bf16[240,384]{1,0:T(8,128)(2,1)S(1)} %bitcast_add_fusion.10), channel_id=1, source_target_pairs={{0,16},{8,24},{16,0},{24,8},{1,17},{9,25},{17,1},{25,9},{2,18},{10... | collective-permute-start | bytes 552968 | tf_op jit(solution)/shard_map/ppermute | solution.py:53
  326.2 5.0 %collective-permute-start.41 = (bf16[2,240,384]{2,1,0:T(8,128)(2,1)S(1)}, bf16[2,240,384]{2,1,0:T(8,128)(2,1)S(1)}, u32[]{:S(2)}, u32[]{:S(2)}) collective-permute-start(bf16[2,240,384]{2,1,0:T(8,128)(2,1)S(1)} %pad_maximum_fusion.4), channel_id=1, source_target_pairs={{0,8},{8,0},{16,24},{24,16},{1,9},{9,1},{17,25},{25,17},{2,10},{10... | collective-permute-start | bytes 1105928 | tf_op jit(solution)/shard_map/ppermute | solution.py:53
  328.4 14.8 %collective-permute-start.45 = (bf16[288,384]{1,0:T(8,128)(2,1)S(1)}, bf16[288,384]{1,0:T(8,128)(2,1)S(1)}, u32[]{:S(2)}, u32[]{:S(2)}) collective-permute-start(bf16[288,384]{1,0:T(8,128)(2,1)S(1)} %fusion.3), channel_id=1, source_target_pairs={{0,4},{1,5},{2,6},{3,7},{4,0},{5,1},{6,2},{7,3},{8,12},{9,13},{10,... | collective-permute-start | bytes 663560 | tf_op jit(solution)/shard_map/ppermute | solution.py:53
  329.0 12.8 %collective-permute-start.32 = (bf16[2,144,384]{2,1,0:T(8,128)(2,1)S(1)}, bf16[2,144,384]{2,1,0:T(8,128)(2,1)S(1)}, u32[]{:S(2)}, u32[]{:S(2)}) collective-permute-start(bf16[2,144,384]{2,1,0:T(8,128)(2,1)S(1)} %get-tuple-element.141), channel_id=1, source_target_pairs={{0,2},{1,3},{2,0},{3,1},{4,6},{5,7},{6,4},{7,5},{8,10},{9,11},{10,... | collective-permute-start | bytes 663560 | tf_op jit(solution)/shard_map/ppermute | solution.py:53
  341.8 6.1 %collective-permute-start.33 = (bf16[144,384]{1,0:T(8,128)(2,1)S(1)}, bf16[144,384]{1,0:T(8,128)(2,1)S(1)}, u32[]{:S(2)}, u32[]{:S(2)}) collective-permute-start(bf16[144,384]{1,0:T(8,128)(2,1)S(1)} %fusion.7), channel_id=1, source_target_pairs={{0,4},{1,5},{2,6},{3,7},{4,0},{5,1},{6,2},{7,3},{8,12},{9,13},{10,... | collective-permute-start | bytes 331784 | tf_op jit(solution)/shard_map/ppermute | solution.py:53
  343.2 9.7 %collective-permute-start.46 = (bf16[288,384]{1,0:T(8,128)(2,1)S(1)}, bf16[288,384]{1,0:T(8,128)(2,1)S(1)}, u32[]{:S(2)}, u32[]{:S(2)}) collective-permute-start(bf16[288,384]{1,0:T(8,128)(2,1)S(1)} %bitcast_add_fusion.5), channel_id=1, source_target_pairs={{0,16},{8,24},{16,0},{24,8},{1,17},{9,25},{17,1},{25,9},{2,18},{10... | collective-permute-start | bytes 663560 | tf_op jit(solution)/shard_map/ppermute | solution.py:53
  347.9 4.8 %collective-permute-start.34 = (bf16[144,384]{1,0:T(8,128)(2,1)S(1)}, bf16[144,384]{1,0:T(8,128)(2,1)S(1)}, u32[]{:S(2)}, u32[]{:S(2)}) collective-permute-start(bf16[144,384]{1,0:T(8,128)(2,1)S(1)} %bitcast_add_fusion.16), channel_id=1, source_target_pairs={{0,16},{8,24},{16,0},{24,8},{1,17},{9,25},{17,1},{25,9},{2,18},{10... | collective-permute-start | bytes 331784 | tf_op jit(solution)/shard_map/ppermute | solution.py:53
  352.8 1.5 collective-permute-start.35
  353.0 2.7 collective-permute-start.47
  (18 other events, 51.8 us)
